TPU v7x, 32 devices: a whole 2x2x4 slice. The times are simulated.
32 devices in a mesh: exp: 8 (over z, x), edp: 4 (over y, core).
Axes of the slice: x: 2, y: 2, z: 4, core: 2. Of those that a mesh axis runs over, the one named last changes fastest.
Arguments:
- out_grad: bfloat16 [4096, 2560], P(('exp', 'edp')), may hold values from -6 to 6
- combine: bfloat16 [4096, 6], P(('exp', 'edp')), may hold values from 0.099609375 to 1.59375
- token_expert_choice: int32 [4096, 6], P(('exp', 'edp')), may hold values from 0 to 7, as said below
- slots: int32 [4096, 6], P(('exp', 'edp')), may hold values from 0 to 64, as said below
- counts: int32 [32, 8], P(('exp', 'edp')), may hold values from 0 to 64, as said below
- down_weight: bfloat16 [8, 768, 2560], P('exp', 'edp'), may hold values from -0.125 to 0.125
- stored_gate_preact: bfloat16 [8, 4, 512, 768], P('exp', 'edp'), may hold values from -6 to 6
- stored_up_preact: bfloat16 [8, 4, 512, 768], P('exp', 'edp'), may hold values from -6 to 6
Outputs:
- gate_preact_gradient: bfloat16 [8, 4, 512, 768], P('exp', 'edp')
- up_preact_gradient: bfloat16 [8, 4, 512, 768], P('exp', 'edp')
- down_matrix_gradient: bfloat16 [8, 768, 2560], P('exp', 'edp')
- combine_weight_gradient: float32 [4096, 6], P(('exp', 'edp'))
Inputs may be any that keep to these rules, and one draw needn't show every extreme that they name: `token_expert_choice`: each row names 6 different experts. `slots`: the rank of the choice among the rows of the same device that name the same expert, in row order, or 64 where that rank reaches 64 and the choice is dropped. `counts`: for each device and expert, the number of that device's rows that name the expert, but at most 64.
All inputs are finite; a program needn't handle non-finite values.
Results may differ from a plain program's by a relative error of at most 0.0057.
Values may be sent and summed in bfloat16 or wider, within the bound.
No kernel may reach another device: no remote copies, remote signals or barrier semaphores. Data moves between devices by JAX's collectives and lax.ppermute only.
A program may use at most 128 MiB of HBM per device.

v0:
```python
import jax
import jax.numpy as jnp
from jax import lax
from jax.sharding import PartitionSpec as P


def on_device(
    out_grad,
    combine,
    token_expert_choice,
    slots,
    counts,
    down_weight,
    stored_gate_preact,
    stored_up_preact,
):
    experts_here = lax.axis_size("exp")
    capacity = stored_gate_preact.shape[2] // experts_here
    tok_rows = out_grad.shape[0]
    model_width = out_grad.shape[1]
    slot_index = jnp.where(
        slots < capacity, token_expert_choice * capacity + slots, experts_here * capacity
    )
    flat_index = slot_index.reshape(-1)
    row_ids = jnp.broadcast_to(
        jnp.arange(tok_rows, dtype=jnp.int32)[:, None] + 1, slot_index.shape
    ).reshape(-1)
    sender_rows = (
        jnp.zeros((experts_here * capacity,), jnp.int32).at[flat_index].set(row_ids, mode="drop")
    )
    padded_grad = jnp.concatenate([jnp.zeros((1, model_width), out_grad.dtype), out_grad], axis=0)
    send_grad = padded_grad[sender_rows].reshape(experts_here, capacity, model_width)
    send_weight = (
        jnp.zeros((experts_here * capacity,), combine.dtype)
        .at[flat_index]
        .set(combine.reshape(-1), mode="drop")
    )
    send_weight = send_weight.reshape(experts_here, capacity)
    send_count = counts.reshape(experts_here, 1)
    recv_grad, received_weight, recv_count = (
        lax.all_to_all(send_grad, "exp", split_axis=0, concat_axis=0, tiled=True),
        lax.all_to_all(send_weight, "exp", split_axis=0, concat_axis=0, tiled=True),
        lax.all_to_all(send_count, "exp", split_axis=0, concat_axis=0, tiled=True),
    )
    live_mask = (jnp.arange(capacity, dtype=jnp.int32)[None, :] < recv_count).astype(jnp.float32)
    scaled = (live_mask * received_weight.astype(jnp.float32)).reshape(-1)
    live_rows = live_mask.reshape(-1)
    grad_rows = recv_grad.reshape(-1, model_width)
    proj = lax.dot_general(
        grad_rows,
        lax.all_gather(down_weight, "edp", axis=1, tiled=True)[0],
        (((1,), (1,)), ((), ())),
        preferred_element_type=jnp.float32,
    )
    gate_pre = stored_gate_preact[0, 0].astype(jnp.float32)
    up_pre = stored_up_preact[0, 0].astype(jnp.float32)
    sigmoid_gate = jax.nn.sigmoid(gate_pre)
    silu_gate = gate_pre * sigmoid_gate
    hidden = (silu_gate * up_pre).astype(jnp.bfloat16)
    weighted = (scaled[:, None] * grad_rows.astype(jnp.float32)).astype(jnp.bfloat16)
    grad_hidden = scaled[:, None] * proj
    gate_preact_gradient = (
        grad_hidden * up_pre * sigmoid_gate * (1.0 + gate_pre * (1.0 - sigmoid_gate))
    ).astype(jnp.bfloat16)
    up_preact_gradient = (grad_hidden * silu_gate).astype(jnp.bfloat16)
    score = (live_rows * jnp.sum(proj * hidden.astype(jnp.float32), axis=1)).reshape(
        experts_here, capacity
    )
    returned_scores = lax.all_to_all(score, "exp", split_axis=0, concat_axis=0, tiled=True)
    summed = lax.psum_scatter(
        lax.dot_general(
            hidden, weighted, (((0,), (0,)), ((), ())), preferred_element_type=jnp.float32
        ),
        "edp",
        scatter_dimension=0,
        tiled=True,
    )
    returned = jnp.concatenate([returned_scores.reshape(-1), jnp.zeros((1,), jnp.float32)])
    combine_weight_gradient = returned[slot_index]
    down_matrix_gradient = summed.astype(jnp.bfloat16)[None]
    return (
        gate_preact_gradient[None, None],
        up_preact_gradient[None, None],
        down_matrix_gradient,
        combine_weight_gradient,
    )


def solution(mesh):
    return jax.shard_map(
        on_device,
        mesh=mesh,
        in_specs=(
            P(("exp", "edp"), None),
            P(("exp", "edp"), None),
            P(("exp", "edp"), None),
            P(("exp", "edp"), None),
            P(("exp", "edp"), None),
            P("exp", "edp", None),
            P("exp", "edp", None, None),
            P("exp", "edp", None, None),
        ),
        out_specs=(
            P("exp", "edp", None, None),
            P("exp", "edp", None, None),
            P("exp", "edp", None),
            P(("exp", "edp"), None),
        ),
        check_vma=False,
    )
```

profile of v0, /device:TPU:0, one launch (start us, length us, event | category | flops | bytes accessed | tf_op | source)
XLA Modules:
  0.0 190.0 jit_solution(14858339435180396069)
XLA Ops:
  7.2 1.3 copy.21
  8.5 7.3 %all-to-all-start = ((s32[8,1,1]{2,1,0:T(1,128)}), s32[8,1,1]{2,1,0:T(1,128)S(1)}, u32[]{:S(2)}, u32[]{:S(2)}) async-start(s32[8,1,1]{2,1,0:T(1,128)} %copy.21), calls=%async_computation | async-start | bytes 8192 | tf_op jit(solution)/shard_map/all_to_all | solution.py:43
  15.7 0.8 copy.23
  16.6 0.2 reshape.189
  16.7 0.1 broadcast_in_dim.34
  16.8 0.1 reshape.197
  16.9 0.7 compare_select_fusion.2
  17.7 0.1 copy.22
  17.8 0.1 reshape.159
  17.9 3.4 %scatter_custom_fusion.1 = s32[512]{0:T(512)S(1)} fusion(s32[768]{0:T(1024)S(1)} %fusion.24, s32[768]{0:T(1024)S(1)} %reshape.197, s32[]{:T(128)} %constant.13.clone.1), kind=kCustom, calls=%fused_computation.47 | custom fusion | bytes 2052 | tf_op jit(solution)/shard_map/scatter | solution.py:29
  21.3 8.6 %scatter_custom_fusion = bf16[512]{0:T(512)(128)(2,1)S(1)} fusion(s32[768]{0:T(1024)S(1)} %fusion.24, bf16[768]{0:T(1024)(128)(2,1)S(1)} %reshape.189, bf16[]{:T(256)} %constant.10.clone.1), kind=kCustom, calls=%fused_computation.51 | custom fusion | bytes 1026 | tf_op jit(solution)/shard_map/scatter | solution.py:36
  29.9 0.7 all_to_all.25
  30.6 0.0 all-to-all-done
  30.6 6.0 %all-to-all-start.1 = ((bf16[8,1,64]{2,1,0:T(2,128)(2,1)}), bf16[8,1,64]{2,1,0:T(2,128)(2,1)S(1)}, u32[]{:S(2)}, u32[]{:S(2)}) async-start(bf16[8,1,64]{2,1,0:T(2,128)(2,1)} %all_to_all.25), calls=%async_computation.1 | async-start | bytes 8192 | tf_op jit(solution)/shard_map/all_to_all | solution.py:42
  36.6 1.2 concatenate.6
  37.9 3.5 %gather_fusion = bf16[512,2560]{1,0:T(8,128)(2,1)} fusion(bf16[129,2560]{1,0:T(8,128)(2,1)S(1)} %concatenate.6, s32[1024]{0:T(1024)S(1)} %pad_clamp_fusion.1), kind=kCustom, calls=%fused_computation | custom fusion | bytes 5244928 | tf_op jit(solution)/shard_map/gather | solution.py:32
  41.4 1.6 all-to-all-done.1
  43.0 4.4 %all-to-all-start.2 = ((bf16[8,64,2560]{2,1,0:T(8,128)(2,1)}), bf16[8,64,2560]{2,1,0:T(8,128)(2,1)S(1)}, u32[]{:S(2)}, u32[]{:S(2)}) async-start(bf16[8,64,2560]{2,1,0:T(8,128)(2,1)} %bitcast.1), calls=%async_computation.2 | async-start | bytes 5242880 | tf_op jit(solution)/shard_map/all_to_all | solution.py:41
  47.4 0.0 all-gather.2.cloned.1.call-start
  47.4 0.7 all-gather.2.cloned.1.call-update
  48.1 0.2 reduce-scatter.2.cloned.1.call-start
  48.4 0.2 reduce
  48.6 0.1 broadcast_select_fusion
  48.7 0.0 copy-start
  48.7 57.1 %all-to-all-done.2 = bf16[8,64,2560]{2,1,0:T(8,128)(2,1)S(1)} async-done(((bf16[8,64,2560]{2,1,0:T(8,128)(2,1)}), bf16[8,64,2560]{2,1,0:T(8,128)(2,1)S(1)}, u32[]{:S(2)}, u32[]{:S(2)}) %all-to-all-start.2) | async-done | bytes 2621472 | tf_op jit(solution)/shard_map/all_to_all | solution.py:41
  105.7 0.0 copy-start.1
  105.7 0.5 multiply_convert_fusion
  106.2 0.0 copy-done
  106.3 0.6 copy-done.1
  106.9 5.4 %fusion.20 = f32[768,2560]{1,0:T(8,128)} fusion(bf16[512,2560]{1,0:T(8,128)(2,1)S(1)} %bitcast.70, bf16[1,1,512,768]{3,2,1,0:T(8,128)(2,1)S(1)} %copy-done, bf16[1,1,512,768]{3,2,1,0:T(8,128)(2,1)S(1)} %copy-done.1), kind=kOutput, calls=%fused_computation.33 | convolution fusion | flops 2016411648 | bytes 12058624 | tf_op jit(solution)/shard_map/dot_general | solution.py:71
  112.3 0.0 reduce-scatter.2.cloned.1.call-update
  112.3 0.1 copy.25
  112.4 0.1 reshape.179
  112.6 0.1 iota_compare_fusion
  112.7 0.1 lt.65
  112.8 0.1 reshape.165
  112.9 0.0 all-gather.2.cloned.1.call-done
  112.9 6.3 %multiply_reduce_fusion = (f32[512]{0:T(512)S(1)}, bf16[1,1,512,768]{3,2,1,0:T(8,128)(2,1)}, bf16[1,1,512,768]{3,2,1,0:T(8,128)(2,1)}) fusion(bf16[1,1,512,768]{3,2,1,0:T(8,128)(2,1)S(1)} %copy-done, bf16[1,1,512,768]{3,2,1,0:T(8,128)(2,1)} %param.14, f32[512]{0:T(512)S(1)} %broadcast_select_fusion.1, bf16[512,2560]{1,0:T(8,128)(2,1)S(1)} %bitcast.69, ...), kind=kOutput, calls=%fused_computation.29 | convolution fusion | flops 2021522944 | bytes 9703424 | tf_op jit(solution)/shard_map/dot_general | solution.py:49
  119.1 0.1 reduce_sum.12
  119.2 0.7 compare_select_fusion.1
  119.9 3.7 %all-to-all-start.3 = ((f32[8,1,64]{2,1,0:T(1,128)}), f32[8,1,64]{2,1,0:T(1,128)S(1)}, u32[]{:S(2)}, u32[]{:S(2)}) async-start(f32[8,1,64]{2,1,0:T(1,128)} %compare_select_fusion.1), calls=%async_computation.4 | async-start | bytes 8192 | tf_op jit(solution)/shard_map/all_to_all | solution.py:69
  123.5 6.4 %all-to-all-done.3 = f32[8,1,64]{2,1,0:T(1,128)S(1)} async-done(((f32[8,1,64]{2,1,0:T(1,128)}), f32[8,1,64]{2,1,0:T(1,128)S(1)}, u32[]{:S(2)}, u32[]{:S(2)}) %all-to-all-start.3) | async-done | bytes 2080 | tf_op jit(solution)/shard_map/all_to_all | solution.py:69
  129.9 0.5 broadcast.130
  130.4 0.7 reduce.10
  131.1 0.1 reshape.164
  131.2 3.2 %gather_fusion.1 = f32[768]{0:T(1024)S(1)} fusion(f32[513]{0:T(1024)S(1)} %pad_maximum_fusion, s32[1024]{0:T(1024)S(1)} %pad_clamp_fusion), kind=kCustom, calls=%fused_computation.1 | custom fusion | bytes 9216 | tf_op jit(solution)/shard_map/gather | solution.py:79
  134.4 0.1 reshape.178
  134.5 0.7 copy.26
  135.2 45.5 %reduce-scatter.2.cloned.1.call-done = f32[192,2560]{1,0:T(8,128)} async-done(((f32[768,2560]{1,0:T(8,128)}), f32[192,2560]{1,0:T(8,128)}) %reduce-scatter.2.cloned.1.call-update) | async-done | bytes 1966096 | tf_op jit(solution)/shard_map/reduce_scatter | solution.py:70
  180.6 2.6 %convert_bitcast_fusion.2 = bf16[1,192,2560]{2,1,0:T(8,128)(2,1)} fusion(f32[192,2560]{1,0:T(8,128)} %reduce-scatter.2.cloned.1.call-done), kind=kLoop, calls=%fused_computation.31 | loop fusion | flops 491520 | bytes 2949120 | tf_op jit(solution)/shard_map/broadcast_in_dim | solution.py:80
  (9 shorter events, 0.1 us)
Async XLA Ops:
  8.5 22.1 %all-to-all-start = ((s32[8,1,1]{2,1,0:T(1,128)}), s32[8,1,1]{2,1,0:T(1,128)S(1)}, u32[]{:S(2)}, u32[]{:S(2)}) async-start(s32[8,1,1]{2,1,0:T(1,128)} %copy.21), calls=%async_computation | async-start | bytes 8192 | tf_op jit(solution)/shard_map/all_to_all | solution.py:43
  30.6 12.4 %all-to-all-start.1 = ((bf16[8,1,64]{2,1,0:T(2,128)(2,1)}), bf16[8,1,64]{2,1,0:T(2,128)(2,1)S(1)}, u32[]{:S(2)}, u32[]{:S(2)}) async-start(bf16[8,1,64]{2,1,0:T(2,128)(2,1)} %all_to_all.25), calls=%async_computation.1 | async-start | bytes 8192 | tf_op jit(solution)/shard_map/all_to_all | solution.py:42
  43.0 62.7 %all-to-all-start.2 = ((bf16[8,64,2560]{2,1,0:T(8,128)(2,1)}), bf16[8,64,2560]{2,1,0:T(8,128)(2,1)S(1)}, u32[]{:S(2)}, u32[]{:S(2)}) async-start(bf16[8,64,2560]{2,1,0:T(8,128)(2,1)} %bitcast.1), calls=%async_computation.2 | async-start | bytes 5242880 | tf_op jit(solution)/shard_map/all_to_all | solution.py:41
  47.4 65.5 %all-gather.2.cloned.1.call-start = ((), (), s32[]{:S(2)}) async-start(), calls=%async_computation.5 | async-start | bytes 4915200 | tf_op jit(solution)/shard_map/all_gather | solution.py:51
  48.1 132.5 %reduce-scatter.2.cloned.1.call-start = ((), (), s32[]{:S(2)}) async-start(), calls=%async_computation.6 | async-start | bytes 9830400 | tf_op jit(solution)/shard_map/reduce_scatter | solution.py:70
  48.7 57.6 %copy-start = (bf16[1,1,512,768]{3,2,1,0:T(8,128)(2,1)S(1)}, bf16[1,1,512,768]{3,2,1,0:T(8,128)(2,1)}, u32[]{:S(2)}) copy-start(bf16[1,1,512,768]{3,2,1,0:T(8,128)(2,1)} %param.15) | copy-start | bytes 2359300
  105.7 1.1 copy-start.1
  119.9 10.0 %all-to-all-start.3 = ((f32[8,1,64]{2,1,0:T(1,128)}), f32[8,1,64]{2,1,0:T(1,128)S(1)}, u32[]{:S(2)}, u32[]{:S(2)}) async-start(f32[8,1,64]{2,1,0:T(1,128)} %compare_select_fusion.1), calls=%async_computation.4 | async-start | bytes 8192 | tf_op jit(solution)/shard_map/all_to_all | solution.py:69
Sparse Core Ops, SparseCore 0:
  49.8 34.4 all-gather.1
  112.5 68.1 reduce-scatter.1
where the time goes:
time: 191 us; the launch traced here: 190 us
  waiting for transfers between devices  111 us (58%)
  local copies, waits for them, and re-layouts  25.9 us (14%)
  starting transfers between devices  21.5 us (11%)
  between operations  14.2 us (7%)
  matrix products  11.7 us (6%)
  other arithmetic  5.57 us (3%)
    all_to_all x1, waiting for transfers between devices, on_device(): lax.all_to_all(send_grad, 'exp', split_axis=0, concat_axis=0, tiled=True)  57.1 us
    reduce_scatter x1, waiting for transfers between devices, on_device(): lax.psum_scatter(lax.dot_general(hidden, weighted, (((0,), (0,)), ((), ()...  45.5 us
    scatter x1, local copies, waits for them, and re-layouts, on_device(): send_weight = jnp.zeros((experts_here * capacity,), combine.dtype).at[fla...  8.61 us
    all_to_all x1, starting transfers between devices, on_device(): lax.all_to_all(send_count, 'exp', split_axis=0, concat_axis=0, tiled=True)  7.25 us
    all_to_all x1, waiting for transfers between devices, on_device(): lax.all_to_all(score, 'exp', split_axis=0, concat_axis=0, tiled=True)  6.38 us
    dot_general x1, matrix products, on_device(): lax.dot_general(grad_rows, lax.all_gather(down_weight, 'edp', axis=1, til...  6.26 us
    all_to_all x1, starting transfers between devices, on_device(): lax.all_to_all(send_weight, 'exp', split_axis=0, concat_axis=0, tiled=True)  5.99 us
    dot_general x1, matrix products, on_device(): lax.dot_general(hidden, weighted, (((0,), (0,)), ((), ())), preferred_ele...  5.43 us
  transfers between devices with their start and end apart: 6, of which 4 were waited for; matrix products, arithmetic and copies ran while one was open for 20% of the time, Pallas kernels for 0%

commit v1 on v0

--- a/solution.py
+++ b/solution.py
@@ -1,10 +1,442 @@
+import functools
+
 import jax
 import jax.numpy as jnp
 from jax import lax
+from jax.experimental import pallas as pl
+from jax.experimental.pallas import tpu as pltpu
 from jax.sharding import PartitionSpec as P
 
 
-def on_device(
+def flip(n, mask):
+    return [(i, i ^ mask) for i in range(n)]
+
+
+def column_cuts(width):
+    unit = width // 20
+    return [(0, 14 * unit), (14 * unit, width)]
+
+
+VMEM = pl.BlockSpec(memory_space=pltpu.VMEM)
+SMEM = pl.BlockSpec(memory_space=pltpu.SMEM)
+BLOCK = pl.BlockSpec()
+ANY = pl.BlockSpec(memory_space=pl.ANY)
+LANES = 128
+CODE, WEIGHT, CHOICE, SLOT = 0, 8, 16, 24
+
+
+def call(body, outs, specs, megabytes, flops=0, moved=0, scratch=(), after=(), out_specs=None):
+    def ordered(*refs):
+        body(*refs[len(after) :])
+
+    kernel = pl.pallas_call(
+        ordered,
+        out_shape=outs,
+        in_specs=[ANY] * len(after) + list(specs),
+        out_specs=out_specs or [VMEM] * len(outs),
+        scratch_shapes=scratch,
+        compiler_params=pltpu.CompilerParams(vmem_limit_bytes=megabytes * 1024 * 1024),
+        cost_estimate=pl.CostEstimate(flops=flops, bytes_accessed=moved, transcendentals=0),
+    )
+    return functools.partial(kernel, *after)
+
+
+def routing_body(
+    capacity, n_exp, cut, choice_ref, slot_ref, combine_ref, counts_ref, tok_ref, meta_ref, raw_ref, *outs
+):
+    topk = choice_ref.shape[0]
+    columns = cut[1] - cut[0]
+    choice = choice_ref[...]
+    slot = slot_ref[...]
+    limit = jnp.zeros_like(slot)
+    for expert in range(n_exp):
+        limit = jnp.where(choice == expert, counts_ref[0, expert], limit)
+    kept = slot < capacity
+    live = kept & (slot < limit)
+    meta_ref[...] = jnp.zeros_like(meta_ref)
+    meta_ref[CODE : CODE + topk, :] = jnp.where(kept, choice * capacity + slot, -1).astype(jnp.float32)
+    meta_ref[WEIGHT : WEIGHT + topk, :] = jnp.where(live, combine_ref[...].astype(jnp.float32), 0.0)
+    meta_ref[CHOICE : CHOICE + topk, :] = choice.astype(jnp.float32)
+    meta_ref[SLOT : SLOT + topk, :] = slot.astype(jnp.float32)
+    raw_ref[:, :columns] = tok_ref[:, cut[0] : cut[1]]
+    raw_ref[:, columns:] = meta_ref[...].T.astype(jnp.bfloat16)
+    select(capacity, topk, meta_ref, tok_ref[...], outs, True)
+
+
+def places(target, capacity):
+    return (lax.broadcasted_iota(jnp.int32, (capacity, LANES), 0) + target).astype(jnp.float32)
+
+
+def pick(meta, topk, want):
+    hit = meta[CODE : CODE + 1, :] == want
+    for k in range(1, topk):
+        hit = hit | (meta[CODE + k : CODE + k + 1, :] == want)
+    return jnp.where(hit, 1.0, 0.0)
+
+
+def weight_of(meta, topk, want):
+    weight = jnp.zeros(want.shape, jnp.float32)
+    for k in range(topk):
+        weight = jnp.where(
+            meta[CODE + k : CODE + k + 1, :] == want, meta[WEIGHT + k : WEIGHT + k + 1, :], weight
+        )
+    return jnp.sum(weight, axis=1, keepdims=True)
+
+
+def select(capacity, topk, meta, rows, outs, weights):
+    here = lax.axis_index("exp")
+    columns = rows.shape[1]
+    wants = [places((here ^ m) * capacity, capacity) for m in range(len(outs))]
+    onehot = jnp.concatenate([pick(meta, topk, w) for w in wants], axis=0).astype(jnp.bfloat16)
+    chosen = jnp.dot(onehot, rows, preferred_element_type=jnp.float32).astype(jnp.bfloat16)
+    for m, out in enumerate(outs):
+        out[:, :columns] = chosen[m * capacity : (m + 1) * capacity]
+        if weights:
+            weight = weight_of(meta, topk, wants[m])
+            out[:, columns:] = jnp.broadcast_to(weight, (capacity, LANES)).astype(jnp.bfloat16)
+
+
+def select_first_body(capacity, topk, cuts, raw_ref, tok_ref, *refs):
+    *outs, following_ref, meta_ref = refs
+    columns = raw_ref.shape[1] - LANES
+    block = raw_ref[:, columns:].astype(jnp.float32).T
+    slot = block[SLOT : SLOT + 8]
+    meta_ref[...] = block
+    meta_ref[CODE : CODE + 8, :] = jnp.where(
+        slot < capacity, block[CHOICE : CHOICE + 8] * capacity + slot, -1.0
+    )
+    select(capacity, topk, meta_ref, raw_ref[:, :columns], outs, True)
+    following_ref[...] = tok_ref[:, cuts[1][0] : cuts[1][1]]
+
+
+def select_more_body(capacity, topk, raw_ref, meta_ref, *outs):
+    select(capacity, topk, meta_ref, raw_ref[...], outs, False)
+
+
+def source_rows(capacity, n):
+    source = lax.axis_index("exp") ^ n
+    return pl.ds(pl.multiple_of(source * capacity, capacity), capacity)
+
+
+def factors_body(
+    capacity, n_edp, gate_ref, up_ref, hidden_ref, gate_factor_ref, up_factor_ref, turned_ref, scratch
+):
+    data = lax.axis_index("edp")
+    rows, units = gate_ref.shape
+    shard = units // n_edp
+    for n in range(rows // capacity):
+        at = pl.ds(n * capacity, capacity)
+        there = source_rows(capacity, n)
+        gate_pre = gate_ref[there, :].astype(jnp.float32)
+        up_pre = up_ref[there, :].astype(jnp.float32)
+        sigmoid_gate = jax.nn.sigmoid(gate_pre)
+        silu_gate = gate_pre * sigmoid_gate
+        hidden_ref[at, :] = (silu_gate * up_pre).astype(jnp.bfloat16)
+        gate_factor_ref[at, :] = up_pre * sigmoid_gate * (1.0 + gate_pre * (1.0 - sigmoid_gate))
+        up_factor_ref[at, :] = silu_gate
+    scratch[...] = hidden_ref[...].T
+    for n in range(n_edp):
+        turned_ref[n] = scratch[pl.ds(pl.multiple_of((data ^ n) * shard, 64), shard), :]
+
+
+def add_cores(keep_ref, from_core_ref, sum_ref):
+    sum_ref[...] = (keep_ref[1] + from_core_ref[...].astype(jnp.float32)).astype(jnp.bfloat16)
+
+
+def output_body(width, keep_ref, from_core_ref, from_y_ref, out_ref, *_):
+    out_ref[...] = (
+        keep_ref[0]
+        + from_core_ref[...].astype(jnp.float32)
+        + from_y_ref[...].astype(jnp.float32)
+    ).astype(jnp.bfloat16)
+
+
+def returned_body(capacity, n_exp, choice_ref, slot_ref, counts_ref, score_ref, out_ref):
+    topk, tokens = choice_ref.shape
+    choice = choice_ref[...]
+    slot = slot_ref[...]
+    limit = jnp.zeros_like(slot)
+    for expert in range(n_exp):
+        limit = jnp.where(choice == expert, counts_ref[0, expert], limit)
+    live = (slot < capacity) & (slot < limit)
+    rank = lax.broadcasted_iota(jnp.int32, (capacity, tokens), 0)
+    expert = lax.broadcasted_iota(jnp.int32, (n_exp, tokens), 0)
+    found = []
+    for k in range(topk):
+        onehot = jnp.where(rank == slot[k : k + 1, :], 1.0, 0.0)
+        all_experts = jnp.dot(
+            score_ref[...], onehot, precision=lax.Precision.HIGHEST, preferred_element_type=jnp.float32
+        )
+        mine = jnp.where(expert == choice[k : k + 1, :], all_experts, 0.0)
+        found.append(jnp.sum(mine, axis=0, keepdims=True))
+    out_ref[...] = jnp.where(live, jnp.concatenate(found, axis=0), 0.0)
+
+
+def term_body(far, cut, tile, turned_ref, *refs):
+    own, others, scales, (keep_ref, *send_refs, weighted) = (
+        refs[:far], refs[far : 2 * far], refs[2 * far : 3 * far], refs[3 * far :]
+    )
+    capacity = own[0].shape[0]
+    n_edp = turned_ref.shape[0]
+    columns = cut[1] - cut[0]
+    for half, (pieces, weights) in enumerate(((own, own), (others, scales))):
+        shift = cut[0] if half == 0 else 0
+        for m in range(far):
+            at = pl.ds((half * far + m) * capacity, capacity)
+            scale = weights[m][:, weights[m].shape[1] - LANES :].astype(jnp.float32)
+            for i in range(0, columns, LANES):
+                weighted[at, i : i + LANES] = (
+                    scale * pieces[m][:, shift + i : shift + i + LANES].astype(jnp.float32)
+                ).astype(jnp.bfloat16)
+    for i in range(columns // tile):
+        lanes = pl.ds(i * tile, tile)
+        for n in range(n_edp):
+            term = jnp.dot(turned_ref[n], weighted[:, lanes], preferred_element_type=jnp.float32)
+            if n % 2 == 0:
+                keep_ref[n // 2, :, lanes] = term
+            else:
+                send_refs[n // 2][:, lanes] = term.astype(jnp.bfloat16)
+
+
+def nt(a, b):
+    return lax.dot_general(a, b, (((1,), (1,)), ((), ())), preferred_element_type=jnp.float32)
+
+
+def finish(proj, weights, hidden, gate_factor, up_factor):
+    part = proj * hidden.astype(jnp.float32)
+    lanes = part[:, :LANES]
+    for i in range(LANES, part.shape[1], LANES):
+        lanes = lanes + part[:, i : i + LANES]
+    score = jnp.sum(lanes.T, axis=0, keepdims=True)
+    scaled = weights * proj
+    gate = (gate_factor * scaled).astype(jnp.bfloat16)
+    up = (up_factor * scaled).astype(jnp.bfloat16)
+    return gate, up, score
+
+
+def weights_of(refs):
+    return jnp.concatenate([r[:, r.shape[1] - LANES :][:, 0:1] for r in refs], axis=0).astype(jnp.float32)
+
+
+def project_own_body(far, *refs):
+    shards, own, refs = refs[:4], refs[4 : 4 + far], refs[4 + far :]
+    hidden_ref, gate_factor_ref, up_factor_ref, weight_ref, gate_ref, up_ref, score_ref = refs
+    data = lax.axis_index("edp")
+    shard, width = shards[0].shape
+    capacity = own[0].shape[0]
+    for n in range(4):
+        weight_ref[pl.ds(pl.multiple_of((data ^ n) * shard, 64), shard), :] = shards[n][...]
+    rows = jnp.concatenate([p[:, :width] for p in own], axis=0)
+    proj = nt(rows, weight_ref[...])
+    for m in range(0, far, 2):
+        at = slice(m * capacity, (m + 2) * capacity)
+        gate_ref[at, :], up_ref[at, :], score = finish(
+            proj[at], weights_of(own[m : m + 2]), hidden_ref[at, :], gate_factor_ref[at, :], up_factor_ref[at, :]
+        )
+        score_ref[m // 2 : m // 2 + 1, :] = score
+
+
+def project_far_body(far, cut, *refs):
+    pieces, (weight_ref, proj_ref) = refs[:far], refs[far:]
+    rows = jnp.concatenate([p[:, : cut[1] - cut[0]] for p in pieces], axis=0)
+    proj_ref[...] = nt(rows, weight_ref[:, cut[0] : cut[1]])
+
+
+def final_body(far, cut, *refs):
+    pieces, scales, refs = refs[:far], refs[far : 2 * far], refs[2 * far :]
+    (
+        weight_ref, proj_ref, hidden_ref, gate_factor_ref, up_factor_ref,
+        own_gate_ref, own_up_ref, own_score_ref, gate_ref, up_ref, score_ref,
+    ) = refs
+    here = lax.axis_index("exp")
+    capacity = pieces[0].shape[0]
+    rows = jnp.concatenate([p[...] for p in pieces], axis=0)
+    proj = proj_ref[...] + nt(rows, weight_ref[:, cut[0] : cut[1]])
+    for m in range(0, far, 2):
+        near = slice(m * capacity, (m + 2) * capacity)
+        at = slice((far + m) * capacity, (far + m + 2) * capacity)
+        found = finish(
+            proj[near], weights_of(scales[m : m + 2]), hidden_ref[at, :], gate_factor_ref[at, :], up_factor_ref[at, :]
+        )
+        held = own_gate_ref[near, :], own_up_ref[near, :], own_score_ref[m // 2 : m // 2 + 1, :]
+        for first, (gate, up, score) in ((far + m, found), (m, held)):
+            for i in range(2):
+                mine = slice(i * capacity, (i + 1) * capacity)
+                there = source_rows(capacity, first + i)
+                gate_ref[there, :] = gate[mine]
+                up_ref[there, :] = up[mine]
+                score_ref[pl.ds(here ^ (first + i), 1), :] = score[:, mine]
+
+
+def relayed(
+    out_grad,
+    combine,
+    token_expert_choice,
+    slots,
+    counts,
+    down_weight,
+    stored_gate_preact,
+    stored_up_preact,
+):
+    n_exp = lax.axis_size("exp")
+    n_edp = lax.axis_size("edp")
+    capacity = stored_gate_preact.shape[2] // n_exp
+    units = stored_gate_preact.shape[3]
+    rows = n_exp * capacity
+    tok_rows, width = out_grad.shape
+    topk = slots.shape[1]
+    shard = units // n_edp
+    far = n_exp // 2
+    cuts = column_cuts(width)
+    sizes = [b - a for a, b in cuts]
+    bf16, f32 = jnp.bfloat16, jnp.float32
+
+    def shape(*dims, dtype=bf16):
+        return jax.ShapeDtypeStruct(dims, dtype)
+
+    def hop(x, axis, mask, after=None):
+        if after is not None:
+            x, _ = lax.optimization_barrier((x, after))
+        return lax.ppermute(x, axis, flip(lax.axis_size(axis), mask))
+
+    def spread(found):
+        return [found[0]] + [hop(found[m], "exp", m) for m in range(1, far)]
+
+    meta, payload, *found = call(
+        functools.partial(routing_body, capacity, n_exp, cuts[0]),
+        [shape(LANES, LANES, dtype=f32), shape(tok_rows, sizes[0] + LANES)]
+        + [shape(capacity, width + LANES)] * far,
+        [BLOCK, BLOCK, BLOCK, SMEM, BLOCK],
+        56,
+        flops=2 * far * capacity * tok_rows * width,
+        moved=out_grad.size * 4,
+    )(token_expert_choice.T, slots.T, combine.T, counts, out_grad)
+    raw = hop(payload, "exp", far)
+    own = spread(found)
+    hidden, gate_factor, up_factor, turned = call(
+        functools.partial(factors_body, capacity, n_edp),
+        [
+            shape(rows, units),
+            shape(rows, units, dtype=f32),
+            shape(rows, units, dtype=f32),
+            shape(n_edp, shard, rows),
+        ],
+        [VMEM] * 2,
+        24,
+        flops=40 * rows * units,
+        moved=16 * rows * units,
+        scratch=[pltpu.VMEM((units, rows), bf16)],
+        after=[own[0]],
+    )(stored_gate_preact[0, 0], stored_up_preact[0, 0])
+    weight_core = hop(down_weight[0], "edp", 1)
+    weight_y = hop(down_weight[0], "edp", 2, (weight_core, payload))
+
+    def term(k, others, scales, after=()):
+        return call(
+            functools.partial(term_body, far, cuts[k], 256),
+            [shape(2, shard, sizes[k], dtype=f32)] + [shape(shard, sizes[k])] * 2,
+            [VMEM] * (1 + 3 * far),
+            24,
+            flops=2 * rows * units * sizes[k],
+            moved=4 * (rows + units) * sizes[k],
+            scratch=[pltpu.VMEM((rows, sizes[k]), bf16)],
+            after=after,
+        )(turned, *own, *others, *scales)
+
+    def cores(send):
+        return [hop(send[i], "edp", 1) for i in range(2)]
+
+    def across(k, keep, from_core, after=()):
+        (sent,) = call(
+            add_cores, [shape(shard, sizes[k])], [VMEM] * 2, 8, flops=1, moved=1, after=after
+        )(keep, from_core)
+        return sent
+
+    def output(k, keep, from_core, from_y):
+        (part,) = call(functools.partial(output_body, width), [shape(shard, sizes[k])], [VMEM] * 3, 8)(
+            keep, from_core, from_y
+        )
+        return part
+
+    *found, payload, far_meta = call(
+        functools.partial(select_first_body, capacity, topk, cuts),
+        [shape(capacity, sizes[0] + LANES)] * far
+        + [shape(tok_rows, sizes[1]), shape(LANES, LANES, dtype=f32)],
+        [VMEM] * 2,
+        16,
+        flops=2 * far * capacity * tok_rows * sizes[0],
+        moved=4 * far * capacity * sizes[0],
+        after=[*own[1:], hidden, weight_y],
+    )(raw, out_grad)
+    far0 = spread(found)
+    raw = hop(payload, "exp", far)
+    weight_both = hop(weight_y, "edp", 1, far_meta)
+    found = call(
+        functools.partial(select_more_body, capacity, topk),
+        [shape(capacity, sizes[1])] * far,
+        [VMEM] * 2,
+        16,
+        flops=2 * far * capacity * tok_rows * sizes[1],
+        moved=4 * far * capacity * sizes[1],
+        after=[*far0[1:], weight_both],
+    )(raw, far_meta)
+    far1 = spread(found)
+    keep0, *send0 = term(0, far0, far0, [far1[0]])
+    core0 = cores(send0)
+    sent0 = across(0, keep0, core0[1], core0[:1])
+    part0 = output(0, keep0, core0[0], hop(sent0, "edp", 2))
+    weight, own_gate, own_up, own_score = call(
+        functools.partial(project_own_body, far),
+        [
+            shape(units, width),
+            shape(far * capacity, units),
+            shape(far * capacity, units),
+            shape(far // 2, 2 * capacity, dtype=f32),
+        ],
+        [VMEM] * (7 + far),
+        32,
+        flops=1,
+        moved=1,
+        after=[sent0],
+    )(down_weight[0], weight_core, weight_y, weight_both, *own, hidden, gate_factor, up_factor)
+    (proj,) = call(
+        functools.partial(project_far_body, far, cuts[0]),
+        [shape(far * capacity, units, dtype=f32)],
+        [VMEM] * (1 + far),
+        24,
+        flops=1,
+        moved=1,
+        after=[own_score],
+    )(*far0, weight)
+    keep1, *send1 = term(1, far1, far0, [proj])
+    core1 = cores(send1)
+    gate_preact_gradient, up_preact_gradient, score = call(
+        functools.partial(final_body, far, cuts[1]),
+        [shape(rows, units), shape(rows, units), shape(n_exp, capacity, dtype=f32)],
+        [VMEM] * (2 * far + 8),
+        32,
+        flops=rows * units * sizes[1],
+        moved=8 * rows * units,
+        after=[keep1],
+    )(*far1, *far0, weight, proj, hidden, gate_factor, up_factor, own_gate, own_up, own_score)
+    sent1 = across(1, keep1, core1[1], [score, core1[0]])
+    part1 = output(1, keep1, core1[0], hop(sent1, "edp", 2))
+    returned = lax.all_to_all(score, "exp", split_axis=0, concat_axis=0)
+    (combine_weight_gradient,) = call(
+        functools.partial(returned_body, capacity, n_exp),
+        [shape(topk, tok_rows, dtype=f32)],
+        [VMEM, VMEM, SMEM, VMEM],
+        8,
+    )(token_expert_choice.T, slots.T, counts, returned)
+    return (
+        gate_preact_gradient[None, None],
+        up_preact_gradient[None, None],
+        jnp.concatenate([part0, part1], axis=1)[None],
+        combine_weight_gradient.T,
+    )
+
+
+def direct(
     out_grad,
     combine,
     token_expert_choice,
@@ -87,6 +519,15 @@
 
 
 def solution(mesh):
+    n_exp, n_edp = mesh.shape["exp"], mesh.shape["edp"]
+
+    def on_device(*arrays):
+        tok_rows = arrays[0].shape[0]
+        capacity = arrays[6].shape[2] // n_exp
+        if n_exp == 8 and n_edp == 4 and tok_rows == LANES and tok_rows <= 2 * capacity:
+            return relayed(*arrays)
+        return direct(*arrays)
+
     return jax.shard_map(
         on_device,
         mesh=mesh,

time: 191 us -> 87.7 us (0.46)
  waiting for transfers between devices: 111 us -> 37.8 us
  local copies, waits for them, and re-layouts: 25.9 us -> 3.86 us
  Pallas kernels: 0 us -> 13.4 us
  between operations: 14.2 us -> 0.8 us
  matrix products: 11.7 us -> 0 us
  blocking collectives: 0 us -> 10.9 us
  other arithmetic: 5.57 us -> 1.01 us
    all_to_all x4 -> x0, waiting for transfers between devices: 65.1 us -> none  [the longest x1 57.1 us: on_device(): lax.all_to_all(send_grad, 'exp', split_axis=0, concat_axis=0, tiled=True)]
    reduce_scatter x1 -> x0, waiting for transfers between devices: 45.5 us -> none  [on_device(): lax.psum_scatter(lax.dot_general(hidden, weighted, (((0,), (0,)), ((), ()...]
    ppermute x0 -> x20, waiting for transfers between devices: none -> 37.8 us  [hop(): return lax.ppermute(x, axis, flip(lax.axis_size(axis), mask))]
    all_to_all x4 -> x0, starting transfers between devices: 21.3 us -> none  [the longest x1 7.25 us: on_device(): lax.all_to_all(send_count, 'exp', split_axis=0, concat_axis=0, tiled=True)]
    ppermute x0 -> x20, starting transfers between devices: none -> 19.7 us  [hop(): return lax.ppermute(x, axis, flip(lax.axis_size(axis), mask))]
    pallas_call x0 -> x14, Pallas kernels: none -> 13.4 us  [the longest x1 2.87 us: relayed(): call(functools.partial(routing_body, capacity, n_exp, cuts[0]), [shape(LA...]
    scatter x2 -> x0, local copies, waits for them, and re-layouts: 12 us -> none  [the longest x1 8.61 us: on_device(): send_weight = jnp.zeros((experts_here * capacity,), combine.dtype).at[fla...]
    dot_general x2 -> x0, matrix products: 11.7 us -> none  [the longest x1 6.26 us: on_device(): lax.dot_general(grad_rows, lax.all_gather(down_weight, 'edp', axis=1, til...]
  transfers between devices with their start and end apart: 6 -> 20, of which waited for: 4 -> 7; matrix products, arithmetic and copies ran while one was open for 20% -> 0% of each run, Pallas kernels for 0% -> 12%
where the time goes in v1:
time: 87.7 us; the launch traced here: 87.4 us
  waiting for transfers between devices  37.8 us (43%)
  starting transfers between devices  19.7 us (22%)
  Pallas kernels  13.4 us (15%)
  blocking collectives  10.9 us (12%)
  local copies, waits for them, and re-layouts  3.86 us (4%)
  other arithmetic  1.01 us (1%)
    ppermute x20, waiting for transfers between devices, hop(): return lax.ppermute(x, axis, flip(lax.axis_size(axis), mask))  37.8 us
    ppermute x20, starting transfers between devices, hop(): return lax.ppermute(x, axis, flip(lax.axis_size(axis), mask))  19.7 us
    all_to_all x1, blocking collectives, relayed(): returned = lax.all_to_all(score, 'exp', split_axis=0, concat_axis=0)  10.9 us
    unnamed x18, local copies, waits for them, and re-layouts  3.86 us
    pallas_call x1, Pallas kernels, relayed(): call(functools.partial(routing_body, capacity, n_exp, cuts[0]), [shape(LA...  2.87 us
    pallas_call x2, Pallas kernels, term(): call(functools.partial(term_body, far, cuts[k], 256), [shape(2, shard, si...  2.5 us
    pallas_call x1, Pallas kernels, relayed(): call(functools.partial(final_body, far, cuts[1]), [shape(rows, units), sh...  2 us
  transfers between devices with their start and end apart: 20, of which 7 were waited for; matrix products, arithmetic and copies ran while one was open for 0% of the time, Pallas kernels for 12%

profile of v1, /device:TPU:0, one launch (start us, length us, event | category | flops | bytes accessed | tf_op | source)
XLA Modules:
  0.0 87.4 jit_solution(15206426663542739601)
XLA Ops:
  0.6 0.0 copy-start.2
  0.6 0.5 collective-permute-start.3
  1.2 2.9 %shard_map.111 = (f32[128,128]{1,0:T(8,128)}, bf16[128,1920]{1,0:T(8,128)(2,1)}, bf16[64,2688]{1,0:T(8,128)(2,1)}, bf16[64,2688]{1,0:T(8,128)(2,1)}, bf16[64,2688]{1,0:T(8,128)(2,1)}, /*index=5*/bf16[64,2688]{1,0:T(8,128)(2,1)}) custom-call(s32[6,128]{1,0:T(8,128)} %bitcast.21, s32[6,128]{1,0:T(8,128)} %bitcast.23, bf16[6,128]{1,0:T(8,128)(2,1)} %bitcast.27, ...), custom_call_target="tpu_custom_call" | custom-call | flops 167772160 | bytes 1310720 | tf_op jit(solution)/shard_map/pallas_call | solution.py:305
  4.0 0.0 collective-permute-done.3.refs_2_
  4.0 2.6 %collective-permute-start.4 = (bf16[192,2560]{1,0:T(8,128)(2,1)}, bf16[192,2560]{1,0:T(8,128)(2,1)S(1)}, u32[]{:S(2)}, u32[]{:S(2)}) collective-permute-start(bf16[192,2560]{1,0:T(8,128)(2,1)} %bitcast.16), channel_id=1, source_target_pairs={{0,2},{1,3},{2,0},{3,1},{4,6},{5,7},{6,4},{7,5},{8,10},{9,11},{10,... | collective-permute-start | bytes 2949128 | tf_op jit(solution)/shard_map/ppermute | solution.py:300
  6.6 2.6 %collective-permute-start.5 = (bf16[128,1920]{1,0:T(8,128)(2,1)}, bf16[128,1920]{1,0:T(8,128)(2,1)S(1)}, u32[]{:S(2)}, u32[]{:S(2)}) collective-permute-start(bf16[128,1920]{1,0:T(8,128)(2,1)} %get-tuple-element.43), channel_id=1, source_target_pairs={{0,16},{4,20},{8,24},{12,28},{16,0},{20,4},{24,8},{28,12},{1,17},{... | collective-permute-start | bytes 1474568 | tf_op jit(solution)/shard_map/ppermute | solution.py:300
  9.2 1.5 %collective-permute-start = (bf16[64,2688]{1,0:T(8,128)(2,1)}, bf16[64,2688]{1,0:T(8,128)(2,1)S(1)}, u32[]{:S(2)}, u32[]{:S(2)}) collective-permute-start(bf16[64,2688]{1,0:T(8,128)(2,1)} %get-tuple-element.38), channel_id=1, source_target_pairs={{0,4},{4,0},{8,12},{12,8},{16,20},{20,16},{24,28},{28,24},{1,5},{5... | collective-permute-start | bytes 1032200 | tf_op jit(solution)/shard_map/ppermute | solution.py:300
  10.7 1.6 %collective-permute-start.1 = (bf16[64,2688]{1,0:T(8,128)(2,1)}, bf16[64,2688]{1,0:T(8,128)(2,1)S(1)}, u32[]{:S(2)}, u32[]{:S(2)}) collective-permute-start(bf16[64,2688]{1,0:T(8,128)(2,1)} %get-tuple-element.39), channel_id=1, source_target_pairs={{0,8},{4,12},{8,0},{12,4},{16,24},{20,28},{24,16},{28,20},{1,9},{5... | collective-permute-start | bytes 1032200 | tf_op jit(solution)/shard_map/ppermute | solution.py:300
  12.3 0.4 collective-permute-start.2
  12.7 1.0 %copy-done = bf16[64,2688]{1,0:T(8,128)(2,1)S(1)} copy-done((bf16[64,2688]{1,0:T(8,128)(2,1)S(1)}, bf16[64,2688]{1,0:T(8,128)(2,1)}, u32[]{:S(2)}) %copy-start) | copy-done | bytes 344088
  13.7 1.1 %copy-done.4 = bf16[1,1,512,768]{3,2,1,0:T(8,128)(2,1)S(1)} copy-done((bf16[1,1,512,768]{3,2,1,0:T(8,128)(2,1)S(1)}, bf16[1,1,512,768]{3,2,1,0:T(8,128)(2,1)}, u32[]{:S(2)}) %copy-start.4) | copy-done | bytes 786456
  14.8 1.1 %copy-done.5 = bf16[1,1,512,768]{3,2,1,0:T(8,128)(2,1)S(1)} copy-done((bf16[1,1,512,768]{3,2,1,0:T(8,128)(2,1)S(1)}, bf16[1,1,512,768]{3,2,1,0:T(8,128)(2,1)}, u32[]{:S(2)}) %copy-start.5) | copy-done | bytes 786456
  15.9 0.8 shard_map.112
  16.7 2.8 %collective-permute-done.refs_0_.refs_3_.refs_6_ = bf16[64,2688]{1,0:T(8,128)(2,1)S(1)} collective-permute-done((bf16[64,2688]{1,0:T(8,128)(2,1)}, bf16[64,2688]{1,0:T(8,128)(2,1)S(1)}, u32[]{:S(2)}, u32[]{:S(2)}) %collective-permute-start) | collective-permute-done | bytes 344096 | tf_op jit(solution)/shard_map/ppermute | solution.py:300
  19.5 9.0 %collective-permute-done.1.refs_1_.refs_4_.refs_7_ = bf16[64,2688]{1,0:T(8,128)(2,1)S(1)} collective-permute-done((bf16[64,2688]{1,0:T(8,128)(2,1)}, bf16[64,2688]{1,0:T(8,128)(2,1)S(1)}, u32[]{:S(2)}, u32[]{:S(2)}) %collective-permute-start.1) | collective-permute-done | bytes 344096 | tf_op jit(solution)/shard_map/ppermute | solution.py:300
  28.5 8.7 %collective-permute-done.2.refs_2_.refs_5_.refs_8_ = bf16[64,2688]{1,0:T(8,128)(2,1)S(1)} collective-permute-done((bf16[64,2688]{1,0:T(8,128)(2,1)}, bf16[64,2688]{1,0:T(8,128)(2,1)S(1)}, u32[]{:S(2)}, u32[]{:S(2)}) %collective-permute-start.2) | collective-permute-done | bytes 344096 | tf_op jit(solution)/shard_map/ppermute | solution.py:300
  37.2 0.0 collective-permute-done.5.refs_5_
  37.2 0.0 collective-permute-done.4.refs_4_.refs_3_
  37.3 0.5 shard_map.113
  37.8 0.1 collective-permute-start.9
  37.8 1.6 %collective-permute-start.6 = (bf16[64,1920]{1,0:T(8,128)(2,1)S(1)}, bf16[64,1920]{1,0:T(8,128)(2,1)S(1)}, u32[]{:S(2)}, u32[]{:S(2)}) collective-permute-start(bf16[64,1920]{1,0:T(8,128)(2,1)S(1)} %get-tuple-element.45), channel_id=1, source_target_pairs={{0,4},{4,0},{8,12},{12,8},{16,20},{20,16},{24,28},{28,24},{1,5},{5... | collective-permute-start | bytes 737288 | tf_op jit(solution)/shard_map/ppermute | solution.py:300
  39.4 0.2 collective-permute-start.7
  39.6 1.8 %collective-permute-start.8 = (bf16[64,1920]{1,0:T(8,128)(2,1)S(1)}, bf16[64,1920]{1,0:T(8,128)(2,1)S(1)}, u32[]{:S(2)}, u32[]{:S(2)}) collective-permute-start(bf16[64,1920]{1,0:T(8,128)(2,1)S(1)} %get-tuple-element.47), channel_id=1, source_target_pairs={{0,12},{4,8},{8,4},{12,0},{16,28},{20,24},{24,20},{28,16},{1,13},{... | collective-permute-start | bytes 737288 | tf_op jit(solution)/shard_map/ppermute | solution.py:300
  41.4 1.1 %collective-permute-start.10 = (bf16[128,768]{1,0:T(8,128)(2,1)S(1)}, bf16[128,768]{1,0:T(8,128)(2,1)S(1)}, u32[]{:S(2)}, u32[]{:S(2)}) collective-permute-start(bf16[128,768]{1,0:T(8,128)(2,1)S(1)} %get-tuple-element.50), channel_id=1, source_target_pairs={{0,16},{4,20},{8,24},{12,28},{16,0},{20,4},{24,8},{28,12},{1,17},{... | collective-permute-start | bytes 589832 | tf_op jit(solution)/shard_map/ppermute | solution.py:300
  42.5 12.2 %collective-permute-done.10.refs_4_ = bf16[128,768]{1,0:T(8,128)(2,1)S(1)} collective-permute-done((bf16[128,768]{1,0:T(8,128)(2,1)S(1)}, bf16[128,768]{1,0:T(8,128)(2,1)S(1)}, u32[]{:S(2)}, u32[]{:S(2)}) %collective-permute-start.10) | collective-permute-done | bytes 196640 | tf_op jit(solution)/shard_map/ppermute | solution.py:300
  54.7 0.0 collective-permute-done.6.refs_0_.refs_7_.refs_11_.refs_2_.refs_6_
  54.7 0.0 collective-permute-done.7.refs_1_.refs_8_.refs_12_.refs_3_.refs_7_
  54.7 2.2 %collective-permute-done.8.refs_2_.refs_9_.refs_13_.refs_4_.refs_8_ = bf16[64,1920]{1,0:T(8,128)(2,1)S(1)} collective-permute-done((bf16[64,1920]{1,0:T(8,128)(2,1)S(1)}, bf16[64,1920]{1,0:T(8,128)(2,1)S(1)}, u32[]{:S(2)}, u32[]{:S(2)}) %collective-permute-start.8) | collective-permute-done | bytes 245792 | tf_op jit(solution)/shard_map/ppermute | solution.py:300
  56.9 0.0 collective-permute-done.9.refs_3_.refs_4_
  56.9 0.3 shard_map.114
  57.2 1.7 %shard_map.115 = (f32[2,192,1792]{2,1,0:T(8,128)S(1)}, bf16[192,1792]{1,0:T(8,128)(2,1)S(1)}, bf16[192,1792]{1,0:T(8,128)(2,1)S(1)}) custom-call(bf16[64,768]{1,0:T(8,128)(2,1)S(1)} %get-tuple-element.51.refs_0_.refs_6_.refs_1_, bf16[4,192,512]{2,1,0:T(8,128)(2,1)S(1)} %get-tuple-element.52.refs_1_, bf16[64,2688]{1,0:T(8,128)(2,1)S(1)} %copy-done, ...), custom_call_target="tpu_custom_call" | custom-call | flops 1409286144 | bytes 9175040 | tf_op jit(solution)/shard_map/pallas_call | solution.py:335
  58.9 0.1 collective-permute-start.11
  58.9 0.5 collective-permute-start.12
  59.4 1.5 %collective-permute-start.13 = (bf16[64,768]{1,0:T(8,128)(2,1)S(1)}, bf16[64,768]{1,0:T(8,128)(2,1)S(1)}, u32[]{:S(2)}, u32[]{:S(2)}) collective-permute-start(bf16[64,768]{1,0:T(8,128)(2,1)S(1)} %get-tuple-element.61), channel_id=1, source_target_pairs={{0,4},{4,0},{8,12},{12,8},{16,20},{20,16},{24,28},{28,24},{1,5},{5... | collective-permute-start | bytes 294920 | tf_op jit(solution)/shard_map/ppermute | solution.py:300
  60.9 0.4 collective-permute-start.14
  61.3 1.6 %collective-permute-start.15 = (bf16[64,768]{1,0:T(8,128)(2,1)S(1)}, bf16[64,768]{1,0:T(8,128)(2,1)S(1)}, u32[]{:S(2)}, u32[]{:S(2)}) collective-permute-start(bf16[64,768]{1,0:T(8,128)(2,1)S(1)} %get-tuple-element.63), channel_id=1, source_target_pairs={{0,12},{4,8},{8,4},{12,0},{16,28},{20,24},{24,20},{28,16},{1,13},{... | collective-permute-start | bytes 294920 | tf_op jit(solution)/shard_map/ppermute | solution.py:300
  62.9 0.0 collective-permute-done.11.refs_0_.refs_1_
  62.9 0.0 collective-permute-done.12.refs_2_
  62.9 0.0 copy-start.3
  63.0 0.1 shard_map.116.refs_0_
  63.1 0.6 collective-permute-start.16
  63.7 0.3 copy-done.1
  63.9 0.3 copy-done.3
  64.3 1.7 %shard_map.117 = (bf16[768,2560]{1,0:T(8,128)(2,1)S(1)}, bf16[256,768]{1,0:T(8,128)(2,1)S(1)}, bf16[256,768]{1,0:T(8,128)(2,1)S(1)}, f32[2,128]{1,0:T(2,128)S(1)}) custom-call(bf16[192,1792]{1,0:T(8,128)(2,1)S(1)} %shard_map.116.refs_0_, bf16[192,2560]{1,0:T(8,128)(2,1)S(1)} %bitcast.17, bf16[192,2560]{1,0:T(8,128)(2,1)S(1)} %collective-permute-done.3.refs_2_, ...), custom_call_target="tpu_custom_call" | custom-call | flops 1 | bytes 1 | tf_op jit(solution)/shard_map/pallas_call | solution.py:388
  65.9 0.9 %shard_map.118.refs_0_.refs_10_ = f32[256,768]{1,0:T(8,128)S(1)} custom-call(f32[2,128]{1,0:T(2,128)S(1)} %get-tuple-element.59.refs_0_.refs_16_, bf16[64,1920]{1,0:T(8,128)(2,1)S(1)} %get-tuple-element.53.refs_6_.refs_10_.refs_1_.refs_5_, bf16[64,1920]{1,0:T(8,128)(2,1)S(1)} %collective-permute-done.6.refs_0_.refs_7_.refs_11_.refs_2_.refs_6_, ...), custom_call_target="tpu_custom_call" | custom-call | flops 1 | bytes 1 | tf_op jit(solution)/shard_map/pallas_call | solution.py:402
  66.8 0.0 collective-permute-done.13.refs_7_.refs_2_
  66.9 0.0 collective-permute-done.14.refs_8_.refs_3_
  66.9 0.6 collective-permute-done.15.refs_9_.refs_4_
  67.5 0.8 shard_map.119
  68.3 0.1 collective-permute-start.17
  68.4 0.5 collective-permute-start.18
  68.9 2.0 %shard_map.120 = (bf16[512,768]{1,0:T(8,128)(2,1)}, bf16[512,768]{1,0:T(8,128)(2,1)}, f32[8,64]{1,0:T(8,128)S(1)}) custom-call(f32[2,192,768]{2,1,0:T(8,128)S(1)} %get-tuple-element.64.refs_0_.refs_2_, bf16[64,768]{1,0:T(8,128)(2,1)S(1)} %get-tuple-element.51.refs_0_.refs_6_.refs_1_, bf16[64,768]{1,0:T(8,128)(2,1)S(1)} %collective-permute-done.13.refs_7_.refs_2_, ...), custom_call_target="tpu_custom_call" | custom-call | flops 301989888 | bytes 3145728 | tf_op jit(solution)/shard_map/pallas_call | solution.py:413
  70.9 0.0 collective-permute-done.17.refs_1_
  70.9 0.0 collective-permute-done.18.refs_3_
  70.9 0.1 shard_map.122
  71.0 0.6 collective-permute-start.19
  71.6 10.9 %all_to_all.11 = f32[8,1,64]{2,1,0:T(1,128)S(1)} all-to-all(f32[8,1,64]{2,1,0:T(1,128)S(1)} %bitcast.20), channel_id=1, replica_groups=mesh['exp'=8,'edp'=4] {'exp'}, dimensions={0} | all-to-all | bytes 4096 | tf_op jit(solution)/shard_map/all_to_all | solution.py:424
  82.4 0.0 copy-done.7
  82.5 1.4 %shard_map.124 = f32[6,128]{1,0:T(8,128)} custom-call(s32[6,128]{1,0:T(8,128)S(1)} %bitcast.22, s32[6,128]{1,0:T(8,128)S(1)} %bitcast.24, s32[1,8]{1,0:T(1,128)S(1)} %copy-done.8, f32[8,64]{1,0:T(8,128)S(1)} %bitcast.25), custom_call_target="tpu_custom_call" | custom-call | tf_op jit(solution)/shard_map/pallas_call | solution.py:425
  83.9 2.2 %collective-permute-done.19.refs_2_ = bf16[192,768]{1,0:T(8,128)(2,1)S(1)} collective-permute-done((bf16[192,768]{1,0:T(8,128)(2,1)S(1)}, bf16[192,768]{1,0:T(8,128)(2,1)S(1)}, u32[]{:S(2)}, u32[]{:S(2)}) %collective-permute-start.19) | collective-permute-done | bytes 294944 | tf_op jit(solution)/shard_map/ppermute | solution.py:300
  86.0 0.1 shard_map.123
  86.2 0.0 collective-permute-done.16.refs_2_
  86.2 0.2 shard_map.121
  86.4 1.0 %maximum_bitcast_fusion = bf16[1,192,2560]{2,1,0:T(8,128)(2,1)} fusion(bf16[192,768]{1,0:T(8,128)(2,1)S(1)} %shard_map.123, bf16[192,1792]{1,0:T(8,128)(2,1)S(1)} %shard_map.121), kind=kLoop, calls=%fused_computation | loop fusion | flops 1966080 | bytes 1966080 | tf_op jit(solution)/shard_map/broadcast_in_dim | solution.py:434
  (10 shorter events, 0.0 us)
Async XLA Ops:
  0.6 36.6 %copy-start.2 = (bf16[128,2560]{1,0:T(8,128)(2,1)S(1)}, bf16[128,2560]{1,0:T(8,128)(2,1)}, u32[]{:S(2)}) copy-start(bf16[128,2560]{1,0:T(8,128)(2,1)} %refs_6_.1) | copy-start | bytes 1966084
  0.6 3.4 %collective-permute-start.3 = (bf16[192,2560]{1,0:T(8,128)(2,1)}, bf16[192,2560]{1,0:T(8,128)(2,1)S(1)}, u32[]{:S(2)}, u32[]{:S(2)}) collective-permute-start(bf16[192,2560]{1,0:T(8,128)(2,1)} %bitcast.15), channel_id=1, source_target_pairs={{0,1},{1,0},{2,3},{3,2},{4,5},{5,4},{6,7},{7,6},{8,9},{9,8},{10,11... | collective-permute-start | bytes 2949128 | tf_op jit(solution)/shard_map/ppermute | solution.py:300
  4.0 33.2 %collective-permute-start.4 = (bf16[192,2560]{1,0:T(8,128)(2,1)}, bf16[192,2560]{1,0:T(8,128)(2,1)S(1)}, u32[]{:S(2)}, u32[]{:S(2)}) collective-permute-start(bf16[192,2560]{1,0:T(8,128)(2,1)} %bitcast.16), channel_id=1, source_target_pairs={{0,2},{1,3},{2,0},{3,1},{4,6},{5,7},{6,4},{7,5},{8,10},{9,11},{10,... | collective-permute-start | bytes 2949128 | tf_op jit(solution)/shard_map/ppermute | solution.py:300
  6.6 30.6 %collective-permute-start.5 = (bf16[128,1920]{1,0:T(8,128)(2,1)}, bf16[128,1920]{1,0:T(8,128)(2,1)S(1)}, u32[]{:S(2)}, u32[]{:S(2)}) collective-permute-start(bf16[128,1920]{1,0:T(8,128)(2,1)} %get-tuple-element.43), channel_id=1, source_target_pairs={{0,16},{4,20},{8,24},{12,28},{16,0},{20,4},{24,8},{28,12},{1,17},{... | collective-permute-start | bytes 1474568 | tf_op jit(solution)/shard_map/ppermute | solution.py:300
  9.2 10.3 %collective-permute-start = (bf16[64,2688]{1,0:T(8,128)(2,1)}, bf16[64,2688]{1,0:T(8,128)(2,1)S(1)}, u32[]{:S(2)}, u32[]{:S(2)}) collective-permute-start(bf16[64,2688]{1,0:T(8,128)(2,1)} %get-tuple-element.38), channel_id=1, source_target_pairs={{0,4},{4,0},{8,12},{12,8},{16,20},{20,16},{24,28},{28,24},{1,5},{5... | collective-permute-start | bytes 1032200 | tf_op jit(solution)/shard_map/ppermute | solution.py:300
  10.7 17.8 %collective-permute-start.1 = (bf16[64,2688]{1,0:T(8,128)(2,1)}, bf16[64,2688]{1,0:T(8,128)(2,1)S(1)}, u32[]{:S(2)}, u32[]{:S(2)}) collective-permute-start(bf16[64,2688]{1,0:T(8,128)(2,1)} %get-tuple-element.39), channel_id=1, source_target_pairs={{0,8},{4,12},{8,0},{12,4},{16,24},{20,28},{24,16},{28,20},{1,9},{5... | collective-permute-start | bytes 1032200 | tf_op jit(solution)/shard_map/ppermute | solution.py:300
  12.3 25.0 %collective-permute-start.2 = (bf16[64,2688]{1,0:T(8,128)(2,1)}, bf16[64,2688]{1,0:T(8,128)(2,1)S(1)}, u32[]{:S(2)}, u32[]{:S(2)}) collective-permute-start(bf16[64,2688]{1,0:T(8,128)(2,1)} %get-tuple-element.40), channel_id=1, source_target_pairs={{0,12},{4,8},{8,4},{12,0},{16,28},{20,24},{24,20},{28,16},{1,13},{... | collective-permute-start | bytes 1032200 | tf_op jit(solution)/shard_map/ppermute | solution.py:300
  12.7 1.0 %copy-start = (bf16[64,2688]{1,0:T(8,128)(2,1)S(1)}, bf16[64,2688]{1,0:T(8,128)(2,1)}, u32[]{:S(2)}) copy-start(bf16[64,2688]{1,0:T(8,128)(2,1)} %get-tuple-element.41.refs_0_.refs_2_.refs_5_) | copy-start | bytes 1032196
  13.7 1.1 %copy-start.4 = (bf16[1,1,512,768]{3,2,1,0:T(8,128)(2,1)S(1)}, bf16[1,1,512,768]{3,2,1,0:T(8,128)(2,1)}, u32[]{:S(2)}) copy-start(bf16[1,1,512,768]{3,2,1,0:T(8,128)(2,1)} %param.14) | copy-start | bytes 2359300
  14.8 1.1 %copy-start.5 = (bf16[1,1,512,768]{3,2,1,0:T(8,128)(2,1)S(1)}, bf16[1,1,512,768]{3,2,1,0:T(8,128)(2,1)}, u32[]{:S(2)}) copy-start(bf16[1,1,512,768]{3,2,1,0:T(8,128)(2,1)} %param.15) | copy-start | bytes 2359300
  37.8 19.1 %collective-permute-start.9 = (bf16[192,2560]{1,0:T(8,128)(2,1)S(1)}, bf16[192,2560]{1,0:T(8,128)(2,1)S(1)}, u32[]{:S(2)}, u32[]{:S(2)}) collective-permute-start(bf16[192,2560]{1,0:T(8,128)(2,1)S(1)} %collective-permute-done.4.refs_4_.refs_3_), channel_id=1, source_target_pairs={{0,1},{1,0},{2,3},{3,2},{4,5},{5,4},{6,7},{7,6},{8,9},{9,8},{10,11... | collective-permute-start | bytes 2949128 | tf_op jit(solution)/shard_map/ppermute | solution.py:300
  37.8 16.9 %collective-permute-start.6 = (bf16[64,1920]{1,0:T(8,128)(2,1)S(1)}, bf16[64,1920]{1,0:T(8,128)(2,1)S(1)}, u32[]{:S(2)}, u32[]{:S(2)}) collective-permute-start(bf16[64,1920]{1,0:T(8,128)(2,1)S(1)} %get-tuple-element.45), channel_id=1, source_target_pairs={{0,4},{4,0},{8,12},{12,8},{16,20},{20,16},{24,28},{28,24},{1,5},{5... | collective-permute-start | bytes 737288 | tf_op jit(solution)/shard_map/ppermute | solution.py:300
  39.4 15.3 %collective-permute-start.7 = (bf16[64,1920]{1,0:T(8,128)(2,1)S(1)}, bf16[64,1920]{1,0:T(8,128)(2,1)S(1)}, u32[]{:S(2)}, u32[]{:S(2)}) collective-permute-start(bf16[64,1920]{1,0:T(8,128)(2,1)S(1)} %get-tuple-element.46), channel_id=1, source_target_pairs={{0,8},{4,12},{8,0},{12,4},{16,24},{20,28},{24,16},{28,20},{1,9},{5... | collective-permute-start | bytes 737288 | tf_op jit(solution)/shard_map/ppermute | solution.py:300
  39.6 17.3 %collective-permute-start.8 = (bf16[64,1920]{1,0:T(8,128)(2,1)S(1)}, bf16[64,1920]{1,0:T(8,128)(2,1)S(1)}, u32[]{:S(2)}, u32[]{:S(2)}) collective-permute-start(bf16[64,1920]{1,0:T(8,128)(2,1)S(1)} %get-tuple-element.47), channel_id=1, source_target_pairs={{0,12},{4,8},{8,4},{12,0},{16,28},{20,24},{24,20},{28,16},{1,13},{... | collective-permute-start | bytes 737288 | tf_op jit(solution)/shard_map/ppermute | solution.py:300
  41.4 13.3 %collective-permute-start.10 = (bf16[128,768]{1,0:T(8,128)(2,1)S(1)}, bf16[128,768]{1,0:T(8,128)(2,1)S(1)}, u32[]{:S(2)}, u32[]{:S(2)}) collective-permute-start(bf16[128,768]{1,0:T(8,128)(2,1)S(1)} %get-tuple-element.50), channel_id=1, source_target_pairs={{0,16},{4,20},{8,24},{12,28},{16,0},{20,4},{24,8},{28,12},{1,17},{... | collective-permute-start | bytes 589832 | tf_op jit(solution)/shard_map/ppermute | solution.py:300
  58.9 4.1 %collective-permute-start.11 = (bf16[192,1792]{1,0:T(8,128)(2,1)S(1)}, bf16[192,1792]{1,0:T(8,128)(2,1)S(1)}, u32[]{:S(2)}, u32[]{:S(2)}) collective-permute-start(bf16[192,1792]{1,0:T(8,128)(2,1)S(1)} %get-tuple-element.54), channel_id=1, source_target_pairs={{0,1},{1,0},{2,3},{3,2},{4,5},{5,4},{6,7},{7,6},{8,9},{9,8},{10,11... | collective-permute-start | bytes 2064392 | tf_op jit(solution)/shard_map/ppermute | solution.py:300
  58.9 4.0 %collective-permute-start.12 = (bf16[192,1792]{1,0:T(8,128)(2,1)S(1)}, bf16[192,1792]{1,0:T(8,128)(2,1)S(1)}, u32[]{:S(2)}, u32[]{:S(2)}) collective-permute-start(bf16[192,1792]{1,0:T(8,128)(2,1)S(1)} %get-tuple-element.56), channel_id=1, source_target_pairs={{0,1},{1,0},{2,3},{3,2},{4,5},{5,4},{6,7},{7,6},{8,9},{9,8},{10,11... | collective-permute-start | bytes 2064392 | tf_op jit(solution)/shard_map/ppermute | solution.py:300
  59.4 7.4 %collective-permute-start.13 = (bf16[64,768]{1,0:T(8,128)(2,1)S(1)}, bf16[64,768]{1,0:T(8,128)(2,1)S(1)}, u32[]{:S(2)}, u32[]{:S(2)}) collective-permute-start(bf16[64,768]{1,0:T(8,128)(2,1)S(1)} %get-tuple-element.61), channel_id=1, source_target_pairs={{0,4},{4,0},{8,12},{12,8},{16,20},{20,16},{24,28},{28,24},{1,5},{5... | collective-permute-start | bytes 294920 | tf_op jit(solution)/shard_map/ppermute | solution.py:300
  60.9 5.9 %collective-permute-start.14 = (bf16[64,768]{1,0:T(8,128)(2,1)S(1)}, bf16[64,768]{1,0:T(8,128)(2,1)S(1)}, u32[]{:S(2)}, u32[]{:S(2)}) collective-permute-start(bf16[64,768]{1,0:T(8,128)(2,1)S(1)} %get-tuple-element.62), channel_id=1, source_target_pairs={{0,8},{4,12},{8,0},{12,4},{16,24},{20,28},{24,16},{28,20},{1,9},{5... | collective-permute-start | bytes 294920 | tf_op jit(solution)/shard_map/ppermute | solution.py:300
  61.3 6.2 %collective-permute-start.15 = (bf16[64,768]{1,0:T(8,128)(2,1)S(1)}, bf16[64,768]{1,0:T(8,128)(2,1)S(1)}, u32[]{:S(2)}, u32[]{:S(2)}) collective-permute-start(bf16[64,768]{1,0:T(8,128)(2,1)S(1)} %get-tuple-element.63), channel_id=1, source_target_pairs={{0,12},{4,8},{8,4},{12,0},{16,28},{20,24},{24,20},{28,16},{1,13},{... | collective-permute-start | bytes 294920 | tf_op jit(solution)/shard_map/ppermute | solution.py:300
  62.9 1.0 %copy-start.1 = (bf16[64,2688]{1,0:T(8,128)(2,1)S(1)}, bf16[64,2688]{1,0:T(8,128)(2,1)}, u32[]{:S(2)}) copy-start(bf16[64,2688]{1,0:T(8,128)(2,1)} %get-tuple-element.41.refs_0_.refs_2_.refs_5_) | copy-start | bytes 1032196
  62.9 1.3 %copy-start.3 = (bf16[1,192,2560]{2,1,0:T(8,128)(2,1)S(1)}, bf16[1,192,2560]{2,1,0:T(8,128)(2,1)}, u32[]{:S(2)}) copy-start(bf16[1,192,2560]{2,1,0:T(8,128)(2,1)} %param.13) | copy-start | bytes 2949124
  63.1 23.1 %collective-permute-start.16 = (bf16[192,1792]{1,0:T(8,128)(2,1)S(1)}, bf16[192,1792]{1,0:T(8,128)(2,1)S(1)}, u32[]{:S(2)}, u32[]{:S(2)}) collective-permute-start(bf16[192,1792]{1,0:T(8,128)(2,1)S(1)} %shard_map.116.refs_0_), channel_id=1, source_target_pairs={{0,2},{1,3},{2,0},{3,1},{4,6},{5,7},{6,4},{7,5},{8,10},{9,11},{10,... | collective-permute-start | bytes 2064392 | tf_op jit(solution)/shard_map/ppermute | solution.py:300
  68.3 2.6 %collective-permute-start.17 = (bf16[192,768]{1,0:T(8,128)(2,1)S(1)}, bf16[192,768]{1,0:T(8,128)(2,1)S(1)}, u32[]{:S(2)}, u32[]{:S(2)}) collective-permute-start(bf16[192,768]{1,0:T(8,128)(2,1)S(1)} %get-tuple-element.69), channel_id=1, source_target_pairs={{0,1},{1,0},{2,3},{3,2},{4,5},{5,4},{6,7},{7,6},{8,9},{9,8},{10,11... | collective-permute-start | bytes 884744 | tf_op jit(solution)/shard_map/ppermute | solution.py:300
  68.4 2.5 %collective-permute-start.18 = (bf16[192,768]{1,0:T(8,128)(2,1)S(1)}, bf16[192,768]{1,0:T(8,128)(2,1)S(1)}, u32[]{:S(2)}, u32[]{:S(2)}) collective-permute-start(bf16[192,768]{1,0:T(8,128)(2,1)S(1)} %get-tuple-element.71), channel_id=1, source_target_pairs={{0,1},{1,0},{2,3},{3,2},{4,5},{5,4},{6,7},{7,6},{8,9},{9,8},{10,11... | collective-permute-start | bytes 884744 | tf_op jit(solution)/shard_map/ppermute | solution.py:300
  70.9 11.5 %copy-start.6 = (s32[128,6]{0,1:T(8,128)S(1)}, s32[128,6]{0,1:T(8,128)}, u32[]{:S(2)}) copy-start(s32[128,6]{0,1:T(8,128)} %param.10) | copy-start | bytes 9220
  70.9 11.5 %copy-start.7 = (s32[128,6]{0,1:T(8,128)S(1)}, s32[128,6]{0,1:T(8,128)}, u32[]{:S(2)}) copy-start(s32[128,6]{0,1:T(8,128)} %param.11) | copy-start | bytes 9220
  70.9 11.5 %copy-start.8 = (s32[1,8]{1,0:T(1,128)S(1)}, s32[1,8]{1,0:T(1,128)}, u32[]{:S(2)}) copy-start(s32[1,8]{1,0:T(1,128)} %refs_2_.1) | copy-start | bytes 100
  71.0 15.0 %collective-permute-start.19 = (bf16[192,768]{1,0:T(8,128)(2,1)S(1)}, bf16[192,768]{1,0:T(8,128)(2,1)S(1)}, u32[]{:S(2)}, u32[]{:S(2)}) collective-permute-start(bf16[192,768]{1,0:T(8,128)(2,1)S(1)} %shard_map.122), channel_id=1, source_target_pairs={{0,2},{1,3},{2,0},{3,1},{4,6},{5,7},{6,4},{7,5},{8,10},{9,11},{10,... | collective-permute-start | bytes 884744 | tf_op jit(solution)/shard_map/ppermute | solution.py:300

commit v2 on v1

v2 whole, which is shorter than its diff:
```python
import functools

import jax
import jax.numpy as jnp
from jax import lax
from jax.experimental import pallas as pl
from jax.experimental.pallas import tpu as pltpu
from jax.sharding import PartitionSpec as P


def flip(n, mask):
    return [(i, i ^ mask) for i in range(n)]


def column_cuts(width):
    unit = width // 20
    return [(0, 15 * unit), (15 * unit, width)]


VMEM = pl.BlockSpec(memory_space=pltpu.VMEM)
SMEM = pl.BlockSpec(memory_space=pltpu.SMEM)
BLOCK = pl.BlockSpec()
ANY = pl.BlockSpec(memory_space=pl.ANY)
LANES = 128
CODE, WEIGHT, CHOICE, SLOT = 0, 8, 16, 24


def call(body, outs, specs, megabytes, flops=0, moved=0, scratch=(), after=(), out_specs=None, aliases=()):
    def ordered(*refs):
        body(*refs[len(after) :])

    kernel = pl.pallas_call(
        ordered,
        out_shape=outs,
        in_specs=[ANY] * len(after) + list(specs),
        out_specs=out_specs or [VMEM] * len(outs),
        scratch_shapes=scratch,
        input_output_aliases={len(after) + i: o for i, o in aliases},
        compiler_params=pltpu.CompilerParams(vmem_limit_bytes=megabytes * 1024 * 1024),
        cost_estimate=pl.CostEstimate(flops=flops, bytes_accessed=moved, transcendentals=0),
    )
    return functools.partial(kernel, *after)


def routing_body(
    capacity, n_exp, choice_ref, slot_ref, combine_ref, counts_ref, tok_ref, meta_ref, raw_ref, *outs
):
    topk = choice_ref.shape[0]
    columns = tok_ref.shape[1]
    choice = choice_ref[...]
    slot = slot_ref[...]
    limit = jnp.zeros_like(slot)
    for expert in range(n_exp):
        limit = jnp.where(choice == expert, counts_ref[0, expert], limit)
    kept = slot < capacity
    live = kept & (slot < limit)
    meta_ref[...] = jnp.zeros_like(meta_ref)
    meta_ref[CODE : CODE + topk, :] = jnp.where(kept, choice * capacity + slot, -1).astype(jnp.float32)
    meta_ref[WEIGHT : WEIGHT + topk, :] = jnp.where(live, combine_ref[...].astype(jnp.float32), 0.0)
    meta_ref[CHOICE : CHOICE + topk, :] = choice.astype(jnp.float32)
    meta_ref[SLOT : SLOT + topk, :] = slot.astype(jnp.float32)
    raw_ref[:, :columns] = tok_ref[...]
    raw_ref[:, columns:] = meta_ref[...].T.astype(jnp.bfloat16)
    select(capacity, topk, meta_ref, tok_ref[...], outs)


def places(target, capacity):
    return (lax.broadcasted_iota(jnp.int32, (capacity, LANES), 0) + target).astype(jnp.float32)


def pick(meta, topk, want):
    hit = meta[CODE : CODE + 1, :] == want
    for k in range(1, topk):
        hit = hit | (meta[CODE + k : CODE + k + 1, :] == want)
    return jnp.where(hit, 1.0, 0.0)


def weight_of(meta, topk, want):
    weight = jnp.zeros(want.shape, jnp.float32)
    for k in range(topk):
        weight = jnp.where(
            meta[CODE + k : CODE + k + 1, :] == want, meta[WEIGHT + k : WEIGHT + k + 1, :], weight
        )
    return jnp.sum(weight, axis=1, keepdims=True)


def select(capacity, topk, meta, rows, outs, own_meta=None):
    here = lax.axis_index("exp")
    columns = rows.shape[1]
    wants = [places((here ^ m) * capacity, capacity) for m in range(len(outs))]
    onehot = jnp.concatenate([pick(meta, topk, w) for w in wants], axis=0).astype(jnp.bfloat16)
    chosen = jnp.dot(onehot, rows, preferred_element_type=jnp.float32).astype(jnp.bfloat16)
    for m, out in enumerate(outs):
        out[:, :columns] = chosen[m * capacity : (m + 1) * capacity]
        if own_meta is not None:
            lane = lax.broadcasted_iota(jnp.int32, (capacity, LANES), 1)
            weight, own_weight = (weight_of(x, topk, wants[m]) for x in (meta, own_meta))
            out[:, columns:] = jnp.where(lane < LANES // 2, weight, own_weight).astype(jnp.bfloat16)


def select_first_body(capacity, topk, cut, raw_ref, own_meta_ref, *refs):
    *outs, meta_ref = refs
    columns = raw_ref.shape[1] - LANES
    block = raw_ref[:, columns:].astype(jnp.float32).T
    slot = block[SLOT : SLOT + 8]
    meta_ref[...] = block
    meta_ref[CODE : CODE + 8, :] = jnp.where(
        slot < capacity, block[CHOICE : CHOICE + 8] * capacity + slot, -1.0
    )
    select(capacity, topk, meta_ref, raw_ref[:, cut[0] : cut[1]], outs, own_meta_ref)


def select_more_body(capacity, topk, cut, raw_ref, meta_ref, *outs):
    select(capacity, topk, meta_ref, raw_ref[:, cut[0] : cut[1]], outs)


def source_rows(capacity, n):
    source = lax.axis_index("exp") ^ n
    return pl.ds(pl.multiple_of(source * capacity, capacity), capacity)


def factors_body(
    capacity, n_edp, gate_ref, up_ref, meta_ref,
    hidden_ref, gate_factor_ref, up_factor_ref, turned_ref, meta_out_ref, scratch,
):
    data = lax.axis_index("edp")
    rows, units = gate_ref.shape
    shard = units // n_edp
    for n in range(rows // capacity):
        at = pl.ds(n * capacity, capacity)
        there = source_rows(capacity, n)
        gate_pre = gate_ref[there, :].astype(jnp.float32)
        up_pre = up_ref[there, :].astype(jnp.float32)
        sigmoid_gate = jax.nn.sigmoid(gate_pre)
        silu_gate = gate_pre * sigmoid_gate
        hidden_ref[at, :] = (silu_gate * up_pre).astype(jnp.bfloat16)
        gate_factor_ref[at, :] = up_pre * sigmoid_gate * (1.0 + gate_pre * (1.0 - sigmoid_gate))
        up_factor_ref[at, :] = silu_gate
    meta_out_ref[...] = meta_ref[...]
    scratch[...] = hidden_ref[...].T
    for n in range(n_edp):
        turned_ref[n] = scratch[pl.ds(pl.multiple_of((data ^ n) * shard, 64), shard), :]


def add_cores(across_ref, *refs):
    *from_core, sum_ref = refs
    start = 0
    for ref in from_core:
        rows = pl.ds(start, ref.shape[0])
        start += ref.shape[0]
        sum_ref[rows, :] = (across_ref[rows, :] + ref[...].astype(jnp.float32)).astype(jnp.bfloat16)


def last_body(capacity, n_exp, cuts, choice_ref, slot_ref, counts_ref, score_ref, *refs):
    sums, (out_ref, weight_ref, held, held_weight, sems) = refs[: 3 * len(cuts)], refs[3 * len(cuts) :]
    copies = []
    for k, (a, b) in enumerate(cuts):
        keep_ref, from_core_ref, from_y_ref = sums[3 * k : 3 * k + 3]
        held[:, a:b] = (
            keep_ref[...] + from_core_ref[...].astype(jnp.float32) + from_y_ref[...].astype(jnp.float32)
        ).astype(jnp.bfloat16)
        lanes = pl.ds(a, b - a)
        copies.append(pltpu.make_async_copy(held.at[:, lanes], out_ref.at[:, lanes], sems.at[k]))
        copies[-1].start()
    topk, tokens = choice_ref.shape
    choice = choice_ref[...]
    slot = slot_ref[...]
    limit = jnp.zeros_like(slot)
    for expert in range(n_exp):
        limit = jnp.where(choice == expert, counts_ref[0, expert], limit)
    live = (slot < capacity) & (slot < limit)
    table = score_ref[...]
    high = table.astype(jnp.bfloat16)
    rest = table - high.astype(jnp.float32)
    middle = rest.astype(jnp.bfloat16)
    low = (rest - middle.astype(jnp.float32)).astype(jnp.bfloat16)
    split = jnp.concatenate([high, middle, low], axis=0)
    rank = lax.broadcasted_iota(jnp.int32, (capacity, tokens), 0)
    expert = lax.broadcasted_iota(jnp.int32, (n_exp, tokens), 0)
    found = []
    for k in range(topk):
        onehot = jnp.where(rank == slot[k : k + 1, :], 1.0, 0.0).astype(jnp.bfloat16)
        parts = jnp.dot(split, onehot, preferred_element_type=jnp.float32)
        every = parts[:n_exp] + parts[n_exp : 2 * n_exp] + parts[2 * n_exp :]
        mine = jnp.where(expert == choice[k : k + 1, :], every, 0.0)
        found.append(jnp.sum(mine, axis=0, keepdims=True))
    held_weight[...] = jnp.where(live, jnp.concatenate(found, axis=0), 0.0)
    copies.append(pltpu.make_async_copy(held_weight, weight_ref, sems.at[len(cuts)]))
    copies[-1].start()
    for copy in copies:
        copy.wait()


def weigh(far, cut, own, others, scales, weighted):
    capacity = own[0].shape[0]
    columns = cut[1] - cut[0]
    for half, pieces in enumerate((own, others)):
        shift = cut[0] if half == 0 else 0
        for m in range(far):
            at = pl.ds((half * far + m) * capacity, capacity)
            scale = jnp.broadcast_to(weights_of(scales[m : m + 1], half == 0), (capacity, LANES))
            for i in range(0, columns, LANES):
                weighted[at, i : i + LANES] = (
                    scale * pieces[m][:, shift + i : shift + i + LANES].astype(jnp.float32)
                ).astype(jnp.bfloat16)


def terms(tile, turned_ref, weighted, outs):
    for i in range(weighted.shape[1] // tile):
        lanes = pl.ds(i * tile, tile)
        for n, refs in outs:
            term = jnp.dot(turned_ref[n], weighted[:, lanes], preferred_element_type=jnp.float32)
            high = term.shape[0] // len(refs)
            for j, ref in enumerate(refs):
                ref[:, lanes] = term[j * high : (j + 1) * high].astype(ref.dtype)


def first_term_body(far, cut, tile, turned_ref, *refs):
    own, others, (send_ref, weighted) = refs[:far], refs[far : 2 * far], refs[2 * far :]
    weigh(far, cut, own, others, others, weighted)
    terms(tile, turned_ref, weighted, [(3, [send_ref])])


def more_terms_body(tile, shards, turned_ref, weighted, *refs):
    terms(tile, turned_ref, weighted, [(n, [ref]) for n, ref in zip(shards, refs)])


def term_body(far, cut, tile, turned_ref, *refs):
    own, others, scales, (own_ref, across_ref, send_ref, *send_across_refs, weighted) = (
        refs[:far], refs[far : 2 * far], refs[2 * far : 3 * far], refs[3 * far :]
    )
    weigh(far, cut, own, others, scales, weighted)
    outs = [(3, send_across_refs), (2, [across_ref]), (1, [send_ref]), (0, [own_ref])]
    terms(tile, turned_ref, weighted, outs)


def nt(a, b):
    return lax.dot_general(a, b, (((1,), (1,)), ((), ())), preferred_element_type=jnp.float32)


def finish(proj, weights, hidden, gate_factor, up_factor):
    part = proj * hidden.astype(jnp.float32)
    lanes = part[:, :LANES]
    for i in range(LANES, part.shape[1], LANES):
        lanes = lanes + part[:, i : i + LANES]
    score = jnp.sum(lanes.T, axis=0, keepdims=True)
    scaled = weights * proj
    gate = (gate_factor * scaled).astype(jnp.bfloat16)
    up = (up_factor * scaled).astype(jnp.bfloat16)
    return gate, up, score


def weights_of(refs, own):
    at = LANES // 2 if own else 0
    return jnp.concatenate(
        [r[:, r.shape[1] - LANES :][:, at : at + 1] for r in refs], axis=0
    ).astype(jnp.float32)


def project_own_body(far, *refs):
    shards, own, (weight_ref, proj_ref) = refs[:4], refs[4 : 4 + far], refs[4 + far :]
    data = lax.axis_index("edp")
    shard = shards[0].shape[0]
    for n in range(4):
        weight_ref[pl.ds(pl.multiple_of((data ^ n) * shard, 64), shard), :] = shards[n][...]
    proj_ref[...] = nt(jnp.concatenate([p[...] for p in own], axis=0), weight_ref[...])


def finish_half(first, far, proj, weights, hidden_ref, gate_factor_ref, up_factor_ref, outs, held, sems):
    here = lax.axis_index("exp")
    count = 2 * (proj.shape[0] // far)
    scores, copies = [], []
    for m in range(0, far, 2):
        near = slice(m * count // 2, m * count // 2 + count)
        at = slice((first + m) * count // 2, (first + m) * count // 2 + count)
        gate, up, score = finish(
            proj[near], weights[near], hidden_ref[at, :], gate_factor_ref[at, :], up_factor_ref[at, :]
        )
        scores.append(score)
        lower = pl.multiple_of(((here ^ (first + m)) // 2) * count, count)
        for i in range(2):
            mine = slice(i * count // 2, (i + 1) * count // 2)
            within = pl.multiple_of(lax.rem(here ^ i, 2) * (count // 2), count // 2)
            there = pl.ds(m // 2 * count + within, count // 2)
            held[0, there, :] = gate[mine]
            held[1, there, :] = up[mine]
        for i, out in enumerate(outs):
            copy = pltpu.make_async_copy(
                held.at[i, pl.ds(m // 2 * count, count), :], out.at[pl.ds(lower, count), :], sems.at[m // 2, i]
            )
            copy.start()
            copies.append(copy)
    return scores, copies


def project_far_body(far, cut, *refs):
    pieces, refs = refs[:far], refs[far:]
    weight_ref, own_proj_ref, hidden_ref, gate_factor_ref, up_factor_ref, *outs = refs
    proj_ref, gate_ref, up_ref, score_ref, held, sems = outs
    scores, copies = finish_half(
        0, far, own_proj_ref[...], weights_of(pieces, True), hidden_ref, gate_factor_ref, up_factor_ref,
        (gate_ref, up_ref), held, sems,
    )
    for i, score in enumerate(scores):
        score_ref[i : i + 1, :] = score
    rows = jnp.concatenate([p[:, : cut[1] - cut[0]] for p in pieces], axis=0)
    proj_ref[...] = nt(rows, weight_ref[:, cut[0] : cut[1]])
    for copy in copies:
        copy.wait()


def final_body(far, cut, *refs):
    pieces, scales, refs = refs[:far], refs[far : 2 * far], refs[2 * far :]
    (
        weight_ref, proj_ref, hidden_ref, gate_factor_ref, up_factor_ref, own_score_ref, _, _,
        gate_ref, up_ref, score_ref, held, sems,
    ) = refs
    here = lax.axis_index("exp")
    capacity = pieces[0].shape[0]
    rows = jnp.concatenate([p[...] for p in pieces], axis=0)
    proj = proj_ref[...] + nt(rows, weight_ref[:, cut[0] : cut[1]])
    scores, copies = finish_half(
        far, far, proj, weights_of(scales, False), hidden_ref, gate_factor_ref, up_factor_ref,
        (gate_ref, up_ref), held, sems,
    )
    for m in range(0, far, 2):
        for first, score in ((far + m, scores[m // 2]), (m, own_score_ref[m // 2 : m // 2 + 1, :])):
            for i in range(2):
                score_ref[pl.ds(here ^ (first + i), 1), :] = score[:, i * capacity : (i + 1) * capacity]
    for copy in copies:
        copy.wait()


def relayed(
    out_grad,
    combine,
    token_expert_choice,
    slots,
    counts,
    down_weight,
    stored_gate_preact,
    stored_up_preact,
):
    n_exp = lax.axis_size("exp")
    n_edp = lax.axis_size("edp")
    capacity = stored_gate_preact.shape[2] // n_exp
    units = stored_gate_preact.shape[3]
    rows = n_exp * capacity
    tok_rows, width = out_grad.shape
    topk = slots.shape[1]
    shard = units // n_edp
    far = n_exp // 2
    cuts = column_cuts(width)
    sizes = [b - a for a, b in cuts]
    splits = [1, 2]
    bf16, f32 = jnp.bfloat16, jnp.float32

    def shape(*dims, dtype=bf16):
        return jax.ShapeDtypeStruct(dims, dtype)

    def hop(x, axis, mask, after=None):
        if after is not None:
            x, _ = lax.optimization_barrier((x, after))
        return lax.ppermute(x, axis, flip(lax.axis_size(axis), mask))

    def spread(found):
        return [found[0]] + [hop(found[m], "exp", m) for m in range(1, far)]

    meta, payload, *found = call(
        functools.partial(routing_body, capacity, n_exp),
        [shape(LANES, LANES, dtype=f32), shape(tok_rows, width + LANES)]
        + [shape(capacity, width)] * far,
        [BLOCK, BLOCK, BLOCK, SMEM, BLOCK],
        56,
        flops=2 * far * capacity * tok_rows * width,
        moved=out_grad.size * 4,
    )(token_expert_choice.T, slots.T, combine.T, counts, out_grad)
    raw = hop(payload, "exp", far)
    own = spread(found)
    hidden, gate_factor, up_factor, turned, meta = call(
        functools.partial(factors_body, capacity, n_edp),
        [
            shape(rows, units),
            shape(rows, units, dtype=f32),
            shape(rows, units, dtype=f32),
            shape(n_edp, shard, rows),
            shape(LANES, LANES, dtype=f32),
        ],
        [VMEM] * 3,
        24,
        flops=40 * rows * units,
        moved=16 * rows * units,
        scratch=[pltpu.VMEM((units, rows), bf16)],
        after=[own[0]],
    )(stored_gate_preact[0, 0], stored_up_preact[0, 0], meta)
    weight_core = hop(down_weight[0], "edp", 1)
    weight_y = hop(down_weight[0], "edp", 2, (weight_core, payload))

    def term(k, others, scales, after=()):
        return call(
            functools.partial(term_body, far, cuts[k], 640),
            [shape(shard, sizes[k], dtype=f32)] * 2
            + [shape(shard, sizes[k])]
            + [shape(shard // splits[k], sizes[k])] * splits[k],
            [VMEM] * (1 + 3 * far),
            24,
            flops=2 * rows * units * sizes[k],
            moved=4 * (rows + units) * sizes[k],
            scratch=[pltpu.VMEM((rows, sizes[k]), bf16)],
            after=after,
        )(turned, *own, *others, *scales)

    def cores(send):
        return [hop(x, "edp", 1) for x in send]

    def across(k, mine, from_core, after=()):
        (sent,) = call(add_cores, [shape(shard, sizes[k])], [VMEM] * (1 + splits[k]), 8, after=after)(
            mine, *from_core
        )
        return sent, hop(sent, "edp", 2)

    *found, far_meta = call(
        functools.partial(select_first_body, capacity, topk, cuts[0]),
        [shape(capacity, sizes[0] + LANES)] * far
        + [shape(LANES, LANES, dtype=f32)],
        [VMEM] * 2,
        16,
        flops=2 * far * capacity * tok_rows * sizes[0],
        moved=4 * far * capacity * sizes[0],
        after=[*own[1:], hidden, weight_y],
    )(raw, meta)
    far0 = spread(found)
    weight_both = hop(weight_y, "edp", 1, far_meta)
    weight, own_proj = call(
        functools.partial(project_own_body, far),
        [shape(units, width), shape(far * capacity, units, dtype=f32)],
        [VMEM] * (4 + far),
        32,
    )(down_weight[0], weight_core, weight_y, weight_both, *own)
    first0, weighted = call(
        functools.partial(first_term_body, far, cuts[0], 640),
        [shape(shard, sizes[0]), shape(rows, sizes[0])],
        [VMEM] * (1 + 2 * far),
        24,
        after=[own_proj],
    )(turned, *own, *far0)
    first0 = hop(first0, "edp", 1)
    def more_terms(shards, outs, after=()):
        return call(
            functools.partial(more_terms_body, 640, shards), outs, [VMEM] * 2, 24, after=after
        )(turned, weighted)

    across0, send0 = more_terms([2, 1], [shape(shard, sizes[0], dtype=f32), shape(shard, sizes[0])])
    core0 = hop(send0, "edp", 1)
    sent0, from_y0 = across(0, across0, [first0])
    found = call(
        functools.partial(select_more_body, capacity, topk, cuts[1]),
        [shape(capacity, sizes[1])] * far,
        [VMEM] * 2,
        16,
        flops=2 * far * capacity * tok_rows * sizes[1],
        moved=4 * far * capacity * sizes[1],
        after=[sent0],
    )(raw, far_meta)
    far1 = spread(found)
    half_scratch = [
        pltpu.VMEM((2, far * capacity, units), bf16),
        pltpu.SemaphoreType.DMA((far // 2, 2)),
    ]
    proj, gate_preact_gradient, up_preact_gradient, own_score = call(
        functools.partial(project_far_body, far, cuts[0]),
        [
            shape(far * capacity, units, dtype=f32),
            shape(rows, units),
            shape(rows, units),
            shape(far // 2, 2 * capacity, dtype=f32),
        ],
        [VMEM] * (5 + far),
        24,
        scratch=half_scratch,
        after=[sent0, far1[0], core0],
        out_specs=[VMEM, ANY, ANY, VMEM],
    )(*far0, weight, own_proj, hidden, gate_factor, up_factor)
    (keep0,) = more_terms([0], [shape(shard, sizes[0], dtype=f32)], [proj])
    keep1, across1, *send1 = term(1, far1, far0, [keep0])
    core1 = cores(send1)
    gate_preact_gradient, up_preact_gradient, score = call(
        functools.partial(final_body, far, cuts[1]),
        [shape(rows, units), shape(rows, units), shape(n_exp, capacity, dtype=f32)],
        [VMEM] * (2 * far + 6) + [ANY] * 2,
        24,
        scratch=half_scratch,
        after=[keep1],
        out_specs=[ANY, ANY, VMEM],
        aliases=[(2 * far + 6, 0), (2 * far + 7, 1)],
    )(
        *far1, *far0, weight, proj, hidden, gate_factor, up_factor, own_score,
        gate_preact_gradient, up_preact_gradient,
    )
    _, from_y1 = across(1, across1, core1[1:], [score, core1[0]])
    returned = lax.all_to_all(score, "exp", split_axis=0, concat_axis=0)
    down_matrix_gradient, combine_weight_gradient = call(
        functools.partial(last_body, capacity, n_exp, cuts),
        [shape(shard, width), shape(topk, tok_rows, dtype=f32)],
        [VMEM, VMEM, SMEM] + [VMEM] * (1 + 3 * len(cuts)),
        16,
        scratch=[
            pltpu.VMEM((shard, width), bf16),
            pltpu.VMEM((topk, tok_rows), f32),
            pltpu.SemaphoreType.DMA((len(cuts) + 1,)),
        ],
        out_specs=[ANY, ANY],
    )(
        token_expert_choice.T, slots.T, counts, returned,
        keep0, core0, from_y0, keep1, core1[0], from_y1,
    )
    return (
        gate_preact_gradient[None, None],
        up_preact_gradient[None, None],
        down_matrix_gradient[None],
        combine_weight_gradient.T,
    )


def direct(
    out_grad,
    combine,
    token_expert_choice,
    slots,
    counts,
    down_weight,
    stored_gate_preact,
    stored_up_preact,
):
    experts_here = lax.axis_size("exp")
    capacity = stored_gate_preact.shape[2] // experts_here
    tok_rows = out_grad.shape[0]
    model_width = out_grad.shape[1]
    slot_index = jnp.where(
        slots < capacity, token_expert_choice * capacity + slots, experts_here * capacity
    )
    flat_index = slot_index.reshape(-1)
    row_ids = jnp.broadcast_to(
        jnp.arange(tok_rows, dtype=jnp.int32)[:, None] + 1, slot_index.shape
    ).reshape(-1)
    sender_rows = (
        jnp.zeros((experts_here * capacity,), jnp.int32).at[flat_index].set(row_ids, mode="drop")
    )
    padded_grad = jnp.concatenate([jnp.zeros((1, model_width), out_grad.dtype), out_grad], axis=0)
    send_grad = padded_grad[sender_rows].reshape(experts_here, capacity, model_width)
    send_weight = (
        jnp.zeros((experts_here * capacity,), combine.dtype)
        .at[flat_index]
        .set(combine.reshape(-1), mode="drop")
    )
    send_weight = send_weight.reshape(experts_here, capacity)
    send_count = counts.reshape(experts_here, 1)
    recv_grad, received_weight, recv_count = (
        lax.all_to_all(send_grad, "exp", split_axis=0, concat_axis=0, tiled=True),
        lax.all_to_all(send_weight, "exp", split_axis=0, concat_axis=0, tiled=True),
        lax.all_to_all(send_count, "exp", split_axis=0, concat_axis=0, tiled=True),
    )
    live_mask = (jnp.arange(capacity, dtype=jnp.int32)[None, :] < recv_count).astype(jnp.float32)
    scaled = (live_mask * received_weight.astype(jnp.float32)).reshape(-1)
    live_rows = live_mask.reshape(-1)
    grad_rows = recv_grad.reshape(-1, model_width)
    proj = lax.dot_general(
        grad_rows,
        lax.all_gather(down_weight, "edp", axis=1, tiled=True)[0],
        (((1,), (1,)), ((), ())),
        preferred_element_type=jnp.float32,
    )
    gate_pre = stored_gate_preact[0, 0].astype(jnp.float32)
    up_pre = stored_up_preact[0, 0].astype(jnp.float32)
    sigmoid_gate = jax.nn.sigmoid(gate_pre)
    silu_gate = gate_pre * sigmoid_gate
    hidden = (silu_gate * up_pre).astype(jnp.bfloat16)
    weighted = (scaled[:, None] * grad_rows.astype(jnp.float32)).astype(jnp.bfloat16)
    grad_hidden = scaled[:, None] * proj
    gate_preact_gradient = (
        grad_hidden * up_pre * sigmoid_gate * (1.0 + gate_pre * (1.0 - sigmoid_gate))
    ).astype(jnp.bfloat16)
    up_preact_gradient = (grad_hidden * silu_gate).astype(jnp.bfloat16)
    score = (live_rows * jnp.sum(proj * hidden.astype(jnp.float32), axis=1)).reshape(
        experts_here, capacity
    )
    returned_scores = lax.all_to_all(score, "exp", split_axis=0, concat_axis=0, tiled=True)
    summed = lax.psum_scatter(
        lax.dot_general(
            hidden, weighted, (((0,), (0,)), ((), ())), preferred_element_type=jnp.float32
        ),
        "edp",
        scatter_dimension=0,
        tiled=True,
    )
    returned = jnp.concatenate([returned_scores.reshape(-1), jnp.zeros((1,), jnp.float32)])
    combine_weight_gradient = returned[slot_index]
    down_matrix_gradient = summed.astype(jnp.bfloat16)[None]
    return (
        gate_preact_gradient[None, None],
        up_preact_gradient[None, None],
        down_matrix_gradient,
        combine_weight_gradient,
    )


def solution(mesh):
    n_exp, n_edp = mesh.shape["exp"], mesh.shape["edp"]

    def on_device(*arrays):
        tok_rows = arrays[0].shape[0]
        capacity = arrays[6].shape[2] // n_exp
        if n_exp == 8 and n_edp == 4 and tok_rows == LANES and tok_rows <= 2 * capacity:
            return relayed(*arrays)
        return direct(*arrays)

    return jax.shard_map(
        on_device,
        mesh=mesh,
        in_specs=(
            P(("exp", "edp"), None),
            P(("exp", "edp"), None),
            P(("exp", "edp"), None),
            P(("exp", "edp"), None),
            P(("exp", "edp"), None),
            P("exp", "edp", None),
            P("exp", "edp", None, None),
            P("exp", "edp", None, None),
        ),
        out_specs=(
            P("exp", "edp", None, None),
            P("exp", "edp", None, None),
            P("exp", "edp", None),
            P(("exp", "edp"), None),
        ),
        check_vma=False,
    )
```

time: 87.7 us -> 86.7 us (0.989)
  waiting for transfers between devices: 37.8 us -> 35.3 us
  Pallas kernels: 13.4 us -> 15.1 us
  other arithmetic: 1.01 us -> 0 us
    ppermute x20, waiting for transfers between devices: 37.8 us -> 35.3 us  [hop(): return lax.ppermute(x, axis, flip(lax.axis_size(axis), mask))]
    pallas_call x10, Pallas kernels: 8.09 us -> 9.46 us  [the longest x1 2.93 us: relayed(): call(functools.partial(routing_body, capacity, n_exp), [shape(LANES, LANE...]
    broadcast_in_dim x1 -> x0, other arithmetic: 1.01 us -> none  [relayed(): jnp.concatenate([part0, part1], axis=1)[None]]
    pallas_call x1, Pallas kernels: 0.92 us -> 1.82 us  [relayed(): call(functools.partial(project_far_body, far, cuts[0]), [shape(far * capa...]
  transfers between devices with their start and end apart: 20 -> 20, of which waited for: 7 -> 10; matrix products, arithmetic and copies ran while one was open for 0% -> 0% of each run, Pallas kernels for 12% -> 14%
where the time goes in v2:
time: 86.7 us; the launch traced here: 86.4 us
  waiting for transfers between devices  35.3 us (41%)
  starting transfers between devices  20 us (23%)
  Pallas kernels  15.1 us (17%)
  blocking collectives  11.1 us (13%)
  local copies, waits for them, and re-layouts  4.09 us (5%)
    ppermute x20, waiting for transfers between devices, hop(): return lax.ppermute(x, axis, flip(lax.axis_size(axis), mask))  35.3 us
    ppermute x20, starting transfers between devices, hop(): return lax.ppermute(x, axis, flip(lax.axis_size(axis), mask))  20 us
    all_to_all x1, blocking collectives, relayed(): returned = lax.all_to_all(score, 'exp', split_axis=0, concat_axis=0)  11.1 us
    unnamed x18, local copies, waits for them, and re-layouts  4.09 us
    pallas_call x1, Pallas kernels, relayed(): call(functools.partial(routing_body, capacity, n_exp), [shape(LANES, LANE...  2.93 us
    pallas_call x1, Pallas kernels, relayed(): call(functools.partial(last_body, capacity, n_exp, cuts), [shape(shard, w...  2.12 us
    pallas_call x1, Pallas kernels, relayed(): call(functools.partial(project_far_body, far, cuts[0]), [shape(far * capa...  1.82 us
  transfers between devices with their start and end apart: 20, of which 10 were waited for; matrix products, arithmetic and copies ran while one was open for 0% of the time, Pallas kernels for 14%

profile of v2, /device:TPU:0, one launch (start us, length us, event | category | flops | bytes accessed | tf_op | source)
XLA Modules:
  0.0 86.4 jit_solution(10470476455344037980)
XLA Ops:
  0.6 0.5 collective-permute-start
  1.1 2.9 %shard_map.111 = (f32[128,128]{1,0:T(8,128)}, bf16[128,2688]{1,0:T(8,128)(2,1)}, bf16[64,2560]{1,0:T(8,128)(2,1)}, bf16[64,2560]{1,0:T(8,128)(2,1)}, bf16[64,2560]{1,0:T(8,128)(2,1)}, /*index=5*/bf16[64,2560]{1,0:T(8,128)(2,1)}) custom-call(s32[6,128]{1,0:T(8,128)} %bitcast.19, s32[6,128]{1,0:T(8,128)} %bitcast.21, bf16[6,128]{1,0:T(8,128)(2,1)} %bitcast.27, ...), custom_call_target="tpu_custom_call" | custom-call | flops 167772160 | bytes 1310720 | tf_op jit(solution)/shard_map/pallas_call | solution.py:369
  4.1 0.0 collective-permute-done.refs_1_
  4.1 2.5 %collective-permute-start.1 = (bf16[192,2560]{1,0:T(8,128)(2,1)}, bf16[192,2560]{1,0:T(8,128)(2,1)S(1)}, u32[]{:S(2)}, u32[]{:S(2)}) collective-permute-start(bf16[192,2560]{1,0:T(8,128)(2,1)} %bitcast.15), channel_id=1, source_target_pairs={{0,2},{1,3},{2,0},{3,1},{4,6},{5,7},{6,4},{7,5},{8,10},{9,11},{10,... | collective-permute-start | bytes 2949128 | tf_op jit(solution)/shard_map/ppermute | solution.py:364
  6.6 2.6 %collective-permute-start.5 = (bf16[128,2688]{1,0:T(8,128)(2,1)}, bf16[128,2688]{1,0:T(8,128)(2,1)S(1)}, u32[]{:S(2)}, u32[]{:S(2)}) collective-permute-start(bf16[128,2688]{1,0:T(8,128)(2,1)} %get-tuple-element.49), channel_id=1, source_target_pairs={{0,16},{4,20},{8,24},{12,28},{16,0},{20,4},{24,8},{28,12},{1,17},{... | collective-permute-start | bytes 2064392 | tf_op jit(solution)/shard_map/ppermute | solution.py:364
  9.2 1.5 %collective-permute-start.2 = (bf16[64,2560]{1,0:T(8,128)(2,1)}, bf16[64,2560]{1,0:T(8,128)(2,1)S(1)}, u32[]{:S(2)}, u32[]{:S(2)}) collective-permute-start(bf16[64,2560]{1,0:T(8,128)(2,1)} %get-tuple-element.51), channel_id=1, source_target_pairs={{0,4},{4,0},{8,12},{12,8},{16,20},{20,16},{24,28},{28,24},{1,5},{5... | collective-permute-start | bytes 983048 | tf_op jit(solution)/shard_map/ppermute | solution.py:364
  10.7 1.6 %collective-permute-start.3 = (bf16[64,2560]{1,0:T(8,128)(2,1)}, bf16[64,2560]{1,0:T(8,128)(2,1)S(1)}, u32[]{:S(2)}, u32[]{:S(2)}) collective-permute-start(bf16[64,2560]{1,0:T(8,128)(2,1)} %get-tuple-element.52), channel_id=1, source_target_pairs={{0,8},{4,12},{8,0},{12,4},{16,24},{20,28},{24,16},{28,20},{1,9},{5... | collective-permute-start | bytes 983048 | tf_op jit(solution)/shard_map/ppermute | solution.py:364
  12.3 0.4 collective-permute-start.4
  12.7 1.0 %copy-done = bf16[64,2560]{1,0:T(8,128)(2,1)S(1)} copy-done((bf16[64,2560]{1,0:T(8,128)(2,1)S(1)}, bf16[64,2560]{1,0:T(8,128)(2,1)}, u32[]{:S(2)}) %copy-start) | copy-done | bytes 327704
  13.7 1.1 %copy-done.3 = bf16[1,1,512,768]{3,2,1,0:T(8,128)(2,1)S(1)} copy-done((bf16[1,1,512,768]{3,2,1,0:T(8,128)(2,1)S(1)}, bf16[1,1,512,768]{3,2,1,0:T(8,128)(2,1)}, u32[]{:S(2)}) %copy-start.3) | copy-done | bytes 786456
  14.8 1.1 %copy-done.4 = bf16[1,1,512,768]{3,2,1,0:T(8,128)(2,1)S(1)} copy-done((bf16[1,1,512,768]{3,2,1,0:T(8,128)(2,1)S(1)}, bf16[1,1,512,768]{3,2,1,0:T(8,128)(2,1)}, u32[]{:S(2)}) %copy-start.4) | copy-done | bytes 786456
  15.9 0.8 copy-done.5
  16.8 0.8 shard_map.112
  17.5 1.6 %collective-permute-done.2.refs_0_.refs_5_.refs_3_ = bf16[64,2560]{1,0:T(8,128)(2,1)S(1)} collective-permute-done((bf16[64,2560]{1,0:T(8,128)(2,1)}, bf16[64,2560]{1,0:T(8,128)(2,1)S(1)}, u32[]{:S(2)}, u32[]{:S(2)}) %collective-permute-start.2) | collective-permute-done | bytes 327712 | tf_op jit(solution)/shard_map/ppermute | solution.py:364
  19.1 13.2 %collective-permute-done.3.refs_1_.refs_6_.refs_4_ = bf16[64,2560]{1,0:T(8,128)(2,1)S(1)} collective-permute-done((bf16[64,2560]{1,0:T(8,128)(2,1)}, bf16[64,2560]{1,0:T(8,128)(2,1)S(1)}, u32[]{:S(2)}, u32[]{:S(2)}) %collective-permute-start.3) | collective-permute-done | bytes 327712 | tf_op jit(solution)/shard_map/ppermute | solution.py:364
  32.4 6.3 %collective-permute-done.4.refs_2_.refs_7_.refs_5_ = bf16[64,2560]{1,0:T(8,128)(2,1)S(1)} collective-permute-done((bf16[64,2560]{1,0:T(8,128)(2,1)}, bf16[64,2560]{1,0:T(8,128)(2,1)S(1)}, u32[]{:S(2)}, u32[]{:S(2)}) %collective-permute-start.4) | collective-permute-done | bytes 327712 | tf_op jit(solution)/shard_map/ppermute | solution.py:364
  38.7 1.4 %collective-permute-done.5.refs_5_.refs_1_ = bf16[128,2688]{1,0:T(8,128)(2,1)S(1)} collective-permute-done((bf16[128,2688]{1,0:T(8,128)(2,1)}, bf16[128,2688]{1,0:T(8,128)(2,1)S(1)}, u32[]{:S(2)}, u32[]{:S(2)}) %collective-permute-start.5) | collective-permute-done | bytes 688160 | tf_op jit(solution)/shard_map/ppermute | solution.py:364
  40.1 0.0 collective-permute-done.1.refs_4_.refs_2_
  40.1 0.5 shard_map.113
  40.6 0.1 collective-permute-start.6
  40.7 2.2 %collective-permute-start.7 = (bf16[64,2048]{1,0:T(8,128)(2,1)S(1)}, bf16[64,2048]{1,0:T(8,128)(2,1)S(1)}, u32[]{:S(2)}, u32[]{:S(2)}) collective-permute-start(bf16[64,2048]{1,0:T(8,128)(2,1)S(1)} %get-tuple-element.60), channel_id=1, source_target_pairs={{0,4},{4,0},{8,12},{12,8},{16,20},{20,16},{24,28},{28,24},{1,5},{5... | collective-permute-start | bytes 786440 | tf_op jit(solution)/shard_map/ppermute | solution.py:364
  43.0 0.2 collective-permute-start.8
  43.2 1.3 %collective-permute-start.9 = (bf16[64,2048]{1,0:T(8,128)(2,1)S(1)}, bf16[64,2048]{1,0:T(8,128)(2,1)S(1)}, u32[]{:S(2)}, u32[]{:S(2)}) collective-permute-start(bf16[64,2048]{1,0:T(8,128)(2,1)S(1)} %get-tuple-element.62), channel_id=1, source_target_pairs={{0,12},{4,8},{8,4},{12,0},{16,28},{20,24},{24,20},{28,16},{1,13},{... | collective-permute-start | bytes 786440 | tf_op jit(solution)/shard_map/ppermute | solution.py:364
  44.5 0.0 collective-permute-done.6.refs_3_
  44.5 0.0 copy-done.1
  44.5 0.0 copy-done.2
  44.5 1.5 %shard_map.114 = (bf16[768,2560]{1,0:T(8,128)(2,1)S(1)}, f32[256,768]{1,0:T(8,128)S(1)}) custom-call(bf16[192,2560]{1,0:T(8,128)(2,1)S(1)} %bitcast.16, bf16[192,2560]{1,0:T(8,128)(2,1)S(1)} %collective-permute-done.refs_1_, bf16[192,2560]{1,0:T(8,128)(2,1)S(1)} %collective-permute-done.1.refs_4_.refs_2_, ...), custom_call_target="tpu_custom_call" | custom-call | tf_op jit(solution)/shard_map/pallas_call | solution.py:434
  46.0 3.9 %collective-permute-done.7.refs_7_.refs_4_.refs_11_.refs_6_ = bf16[64,2048]{1,0:T(8,128)(2,1)S(1)} collective-permute-done((bf16[64,2048]{1,0:T(8,128)(2,1)S(1)}, bf16[64,2048]{1,0:T(8,128)(2,1)S(1)}, u32[]{:S(2)}, u32[]{:S(2)}) %collective-permute-start.7) | collective-permute-done | bytes 262176 | tf_op jit(solution)/shard_map/ppermute | solution.py:364
  49.9 2.3 %collective-permute-done.8.refs_8_.refs_5_.refs_12_.refs_7_ = bf16[64,2048]{1,0:T(8,128)(2,1)S(1)} collective-permute-done((bf16[64,2048]{1,0:T(8,128)(2,1)S(1)}, bf16[64,2048]{1,0:T(8,128)(2,1)S(1)}, u32[]{:S(2)}, u32[]{:S(2)}) %collective-permute-start.8) | collective-permute-done | bytes 262176 | tf_op jit(solution)/shard_map/ppermute | solution.py:364
  52.1 4.5 %collective-permute-done.9.refs_9_.refs_6_.refs_13_.refs_8_ = bf16[64,2048]{1,0:T(8,128)(2,1)S(1)} collective-permute-done((bf16[64,2048]{1,0:T(8,128)(2,1)S(1)}, bf16[64,2048]{1,0:T(8,128)(2,1)S(1)}, u32[]{:S(2)}, u32[]{:S(2)}) %collective-permute-start.9) | collective-permute-done | bytes 262176 | tf_op jit(solution)/shard_map/ppermute | solution.py:364
  56.7 0.8 shard_map.115
  57.5 0.1 collective-permute-start.10
  57.6 1.1 %shard_map.116 = (f32[192,1920]{1,0:T(8,128)S(1)}, bf16[192,1920]{1,0:T(8,128)(2,1)S(1)}) custom-call(bf16[4,192,512]{2,1,0:T(8,128)(2,1)S(1)} %get-tuple-element.48.refs_1_.refs_0_, bf16[512,1920]{1,0:T(8,128)(2,1)S(1)} %get-tuple-element.63.refs_1_.refs_2_), custom_call_target="tpu_custom_call" | custom-call | tf_op jit(solution)/shard_map/pallas_call | solution.py:449
  58.7 0.6 collective-permute-start.11
  59.2 0.5 collective-permute-done.10.refs_1_
  59.8 0.1 shard_map.117.refs_0_
  59.9 0.5 collective-permute-start.15
  60.4 0.3 shard_map.118
  60.7 1.8 %collective-permute-start.12 = (bf16[64,640]{1,0:T(8,128)(2,1)S(1)}, bf16[64,640]{1,0:T(8,128)(2,1)S(1)}, u32[]{:S(2)}, u32[]{:S(2)}) collective-permute-start(bf16[64,640]{1,0:T(8,128)(2,1)S(1)} %get-tuple-element.72), channel_id=1, source_target_pairs={{0,4},{4,0},{8,12},{12,8},{16,20},{20,16},{24,28},{28,24},{1,5},{5... | collective-permute-start | bytes 245768 | tf_op jit(solution)/shard_map/ppermute | solution.py:364
  62.5 0.3 collective-permute-start.13
  62.8 1.4 %collective-permute-start.14 = (bf16[64,640]{1,0:T(8,128)(2,1)S(1)}, bf16[64,640]{1,0:T(8,128)(2,1)S(1)}, u32[]{:S(2)}, u32[]{:S(2)}) collective-permute-start(bf16[64,640]{1,0:T(8,128)(2,1)S(1)} %get-tuple-element.74), channel_id=1, source_target_pairs={{0,12},{4,8},{8,4},{12,0},{16,28},{20,24},{24,20},{28,16},{1,13},{... | collective-permute-start | bytes 245768 | tf_op jit(solution)/shard_map/ppermute | solution.py:364
  64.2 0.0 collective-permute-done.11.refs_2_.refs_5_
  64.2 1.8 %shard_map.119 = (f32[256,768]{1,0:T(8,128)S(1)}, bf16[512,768]{1,0:T(8,128)(2,1)}, bf16[512,768]{1,0:T(8,128)(2,1)}, f32[2,128]{1,0:T(2,128)S(1)}) custom-call(bf16[192,1920]{1,0:T(8,128)(2,1)S(1)} %shard_map.117.refs_0_, bf16[64,640]{1,0:T(8,128)(2,1)S(1)} %get-tuple-element.66.refs_1_.refs_6_, ...), custom_call_target="tpu_custom_call" | custom-call | tf_op jit(solution)/shard_map/pallas_call | solution.py:470
  66.1 0.6 shard_map.120.refs_0_.refs_4_
  66.7 0.0 collective-permute-done.12.refs_7_.refs_2_
  66.7 0.6 collective-permute-done.13.refs_8_.refs_3_
  67.4 0.9 collective-permute-done.14.refs_9_.refs_4_
  68.2 0.9 %shard_map.121 = (f32[192,640]{1,0:T(8,128)S(1)}, f32[192,640]{1,0:T(8,128)S(1)}, bf16[192,640]{1,0:T(8,128)(2,1)S(1)}, bf16[96,640]{1,0:T(8,128)(2,1)S(1)}, bf16[96,640]{1,0:T(8,128)(2,1)S(1)}) custom-call(f32[192,1920]{1,0:T(8,128)S(1)} %shard_map.120.refs_0_.refs_4_, bf16[4,192,512]{2,1,0:T(8,128)(2,1)S(1)} %get-tuple-element.48.refs_1_.refs_0_, ...), custom_call_target="tpu_custom_call" | custom-call | flops 503316480 | bytes 3276800 | tf_op jit(solution)/shard_map/pallas_call | solution.py:400
  69.2 0.1 collective-permute-start.16
  69.2 0.5 collective-permute-start.17
  69.7 0.1 collective-permute-start.18
  69.8 1.6 %shard_map.122 = (bf16[512,768]{1,0:T(8,128)(2,1)}, bf16[512,768]{1,0:T(8,128)(2,1)}, f32[8,64]{1,0:T(8,128)S(1)}) custom-call(f32[192,640]{1,0:T(8,128)S(1)} %get-tuple-element.75.refs_0_.refs_7_, bf16[64,640]{1,0:T(8,128)(2,1)S(1)} %get-tuple-element.66.refs_1_.refs_6_, ...), custom_call_target="tpu_custom_call", output_to_operand_aliasing={{0}: (15, {}), {1}: (16, {})} | custom-call | tf_op jit(solution)/shard_map/pallas_call | solution.py:487
  71.4 0.0 collective-permute-done.17.refs_3_
  71.4 0.0 collective-permute-done.18.refs_4_
  71.4 0.0 collective-permute-done.16.refs_1_.refs_8_
  71.4 0.1 shard_map.123
  71.5 1.6 %collective-permute-start.19 = (bf16[192,640]{1,0:T(8,128)(2,1)S(1)}, bf16[192,640]{1,0:T(8,128)(2,1)S(1)}, u32[]{:S(2)}, u32[]{:S(2)}) collective-permute-start(bf16[192,640]{1,0:T(8,128)(2,1)S(1)} %shard_map.123), channel_id=1, source_target_pairs={{0,2},{1,3},{2,0},{3,1},{4,6},{5,7},{6,4},{7,5},{8,10},{9,11},{10,... | collective-permute-start | bytes 737288 | tf_op jit(solution)/shard_map/ppermute | solution.py:364
  73.2 11.1 %all_to_all.11 = f32[8,1,64]{2,1,0:T(1,128)S(1)} all-to-all(f32[8,1,64]{2,1,0:T(1,128)S(1)} %bitcast.23), channel_id=1, replica_groups=mesh['exp'=8,'edp'=4] {'exp'}, dimensions={0} | all-to-all | bytes 4096 | tf_op jit(solution)/shard_map/all_to_all | solution.py:501
  84.2 0.0 collective-permute-done.19.refs_9_
  84.2 0.0 collective-permute-done.15.refs_6_
  84.3 0.0 copy-done.6
  84.3 0.0 copy-done.7
  84.3 0.0 copy-done.8
  84.3 2.1 %shard_map.124 = (bf16[192,2560]{1,0:T(8,128)(2,1)}, f32[6,128]{1,0:T(8,128)}) custom-call(s32[6,128]{1,0:T(8,128)S(1)} %bitcast.20, s32[6,128]{1,0:T(8,128)S(1)} %bitcast.22, s32[1,8]{1,0:T(1,128)S(1)} %copy-done.8, f32[8,64]{1,0:T(8,128)S(1)} %bitcast.24, f32[192,1920]{1,0:T(8,128)S(1)} %shard_map.120.refs_0_.refs_4_, ...), custom_call_target="tpu_custom_call" | custom-call | tf_op jit(solution)/shard_map/pallas_call | solution.py:502
  (9 shorter events, 0.0 us)
Async XLA Ops:
  0.6 3.5 %collective-permute-start = (bf16[192,2560]{1,0:T(8,128)(2,1)}, bf16[192,2560]{1,0:T(8,128)(2,1)S(1)}, u32[]{:S(2)}, u32[]{:S(2)}) collective-permute-start(bf16[192,2560]{1,0:T(8,128)(2,1)} %bitcast.14), channel_id=1, source_target_pairs={{0,1},{1,0},{2,3},{3,2},{4,5},{5,4},{6,7},{7,6},{8,9},{9,8},{10,11... | collective-permute-start | bytes 2949128 | tf_op jit(solution)/shard_map/ppermute | solution.py:364
  4.1 36.0 %collective-permute-start.1 = (bf16[192,2560]{1,0:T(8,128)(2,1)}, bf16[192,2560]{1,0:T(8,128)(2,1)S(1)}, u32[]{:S(2)}, u32[]{:S(2)}) collective-permute-start(bf16[192,2560]{1,0:T(8,128)(2,1)} %bitcast.15), channel_id=1, source_target_pairs={{0,2},{1,3},{2,0},{3,1},{4,6},{5,7},{6,4},{7,5},{8,10},{9,11},{10,... | collective-permute-start | bytes 2949128 | tf_op jit(solution)/shard_map/ppermute | solution.py:364
  6.6 33.5 %collective-permute-start.5 = (bf16[128,2688]{1,0:T(8,128)(2,1)}, bf16[128,2688]{1,0:T(8,128)(2,1)S(1)}, u32[]{:S(2)}, u32[]{:S(2)}) collective-permute-start(bf16[128,2688]{1,0:T(8,128)(2,1)} %get-tuple-element.49), channel_id=1, source_target_pairs={{0,16},{4,20},{8,24},{12,28},{16,0},{20,4},{24,8},{28,12},{1,17},{... | collective-permute-start | bytes 2064392 | tf_op jit(solution)/shard_map/ppermute | solution.py:364
  9.2 9.9 %collective-permute-start.2 = (bf16[64,2560]{1,0:T(8,128)(2,1)}, bf16[64,2560]{1,0:T(8,128)(2,1)S(1)}, u32[]{:S(2)}, u32[]{:S(2)}) collective-permute-start(bf16[64,2560]{1,0:T(8,128)(2,1)} %get-tuple-element.51), channel_id=1, source_target_pairs={{0,4},{4,0},{8,12},{12,8},{16,20},{20,16},{24,28},{28,24},{1,5},{5... | collective-permute-start | bytes 983048 | tf_op jit(solution)/shard_map/ppermute | solution.py:364
  10.7 21.7 %collective-permute-start.3 = (bf16[64,2560]{1,0:T(8,128)(2,1)}, bf16[64,2560]{1,0:T(8,128)(2,1)S(1)}, u32[]{:S(2)}, u32[]{:S(2)}) collective-permute-start(bf16[64,2560]{1,0:T(8,128)(2,1)} %get-tuple-element.52), channel_id=1, source_target_pairs={{0,8},{4,12},{8,0},{12,4},{16,24},{20,28},{24,16},{28,20},{1,9},{5... | collective-permute-start | bytes 983048 | tf_op jit(solution)/shard_map/ppermute | solution.py:364
  12.3 26.4 %collective-permute-start.4 = (bf16[64,2560]{1,0:T(8,128)(2,1)}, bf16[64,2560]{1,0:T(8,128)(2,1)S(1)}, u32[]{:S(2)}, u32[]{:S(2)}) collective-permute-start(bf16[64,2560]{1,0:T(8,128)(2,1)} %get-tuple-element.53), channel_id=1, source_target_pairs={{0,12},{4,8},{8,4},{12,0},{16,28},{20,24},{24,20},{28,16},{1,13},{... | collective-permute-start | bytes 983048 | tf_op jit(solution)/shard_map/ppermute | solution.py:364
  12.7 1.0 %copy-start = (bf16[64,2560]{1,0:T(8,128)(2,1)S(1)}, bf16[64,2560]{1,0:T(8,128)(2,1)}, u32[]{:S(2)}) copy-start(bf16[64,2560]{1,0:T(8,128)(2,1)} %get-tuple-element.46.refs_0_.refs_4_.refs_2_) | copy-start | bytes 983044
  13.7 1.1 %copy-start.3 = (bf16[1,1,512,768]{3,2,1,0:T(8,128)(2,1)S(1)}, bf16[1,1,512,768]{3,2,1,0:T(8,128)(2,1)}, u32[]{:S(2)}) copy-start(bf16[1,1,512,768]{3,2,1,0:T(8,128)(2,1)} %param.14) | copy-start | bytes 2359300
  14.8 1.1 %copy-start.4 = (bf16[1,1,512,768]{3,2,1,0:T(8,128)(2,1)S(1)}, bf16[1,1,512,768]{3,2,1,0:T(8,128)(2,1)}, u32[]{:S(2)}) copy-start(bf16[1,1,512,768]{3,2,1,0:T(8,128)(2,1)} %param.15) | copy-start | bytes 2359300
  15.9 0.8 copy-start.5
  40.1 4.4 %copy-start.1 = (bf16[64,2560]{1,0:T(8,128)(2,1)S(1)}, bf16[64,2560]{1,0:T(8,128)(2,1)}, u32[]{:S(2)}) copy-start(bf16[64,2560]{1,0:T(8,128)(2,1)} %get-tuple-element.46.refs_0_.refs_4_.refs_2_) | copy-start | bytes 983044
  40.1 4.4 %copy-start.2 = (bf16[1,192,2560]{2,1,0:T(8,128)(2,1)S(1)}, bf16[1,192,2560]{2,1,0:T(8,128)(2,1)}, u32[]{:S(2)}) copy-start(bf16[1,192,2560]{2,1,0:T(8,128)(2,1)} %param.13) | copy-start | bytes 2949124
  40.6 3.9 %collective-permute-start.6 = (bf16[192,2560]{1,0:T(8,128)(2,1)S(1)}, bf16[192,2560]{1,0:T(8,128)(2,1)S(1)}, u32[]{:S(2)}, u32[]{:S(2)}) collective-permute-start(bf16[192,2560]{1,0:T(8,128)(2,1)S(1)} %collective-permute-done.1.refs_4_.refs_2_), channel_id=1, source_target_pairs={{0,1},{1,0},{2,3},{3,2},{4,5},{5,4},{6,7},{7,6},{8,9},{9,8},{10,11... | collective-permute-start | bytes 2949128 | tf_op jit(solution)/shard_map/ppermute | solution.py:364
  40.7 9.1 %collective-permute-start.7 = (bf16[64,2048]{1,0:T(8,128)(2,1)S(1)}, bf16[64,2048]{1,0:T(8,128)(2,1)S(1)}, u32[]{:S(2)}, u32[]{:S(2)}) collective-permute-start(bf16[64,2048]{1,0:T(8,128)(2,1)S(1)} %get-tuple-element.60), channel_id=1, source_target_pairs={{0,4},{4,0},{8,12},{12,8},{16,20},{20,16},{24,28},{28,24},{1,5},{5... | collective-permute-start | bytes 786440 | tf_op jit(solution)/shard_map/ppermute | solution.py:364
  43.0 9.2 %collective-permute-start.8 = (bf16[64,2048]{1,0:T(8,128)(2,1)S(1)}, bf16[64,2048]{1,0:T(8,128)(2,1)S(1)}, u32[]{:S(2)}, u32[]{:S(2)}) collective-permute-start(bf16[64,2048]{1,0:T(8,128)(2,1)S(1)} %get-tuple-element.61), channel_id=1, source_target_pairs={{0,8},{4,12},{8,0},{12,4},{16,24},{20,28},{24,16},{28,20},{1,9},{5... | collective-permute-start | bytes 786440 | tf_op jit(solution)/shard_map/ppermute | solution.py:364
  43.2 13.5 %collective-permute-start.9 = (bf16[64,2048]{1,0:T(8,128)(2,1)S(1)}, bf16[64,2048]{1,0:T(8,128)(2,1)S(1)}, u32[]{:S(2)}, u32[]{:S(2)}) collective-permute-start(bf16[64,2048]{1,0:T(8,128)(2,1)S(1)} %get-tuple-element.62), channel_id=1, source_target_pairs={{0,12},{4,8},{8,4},{12,0},{16,28},{20,24},{24,20},{28,16},{1,13},{... | collective-permute-start | bytes 786440 | tf_op jit(solution)/shard_map/ppermute | solution.py:364
  57.5 2.3 %collective-permute-start.10 = (bf16[192,1920]{1,0:T(8,128)(2,1)S(1)}, bf16[192,1920]{1,0:T(8,128)(2,1)S(1)}, u32[]{:S(2)}, u32[]{:S(2)}) collective-permute-start(bf16[192,1920]{1,0:T(8,128)(2,1)S(1)} %get-tuple-element.65), channel_id=1, source_target_pairs={{0,1},{1,0},{2,3},{3,2},{4,5},{5,4},{6,7},{7,6},{8,9},{9,8},{10,11... | collective-permute-start | bytes 2211848 | tf_op jit(solution)/shard_map/ppermute | solution.py:364
  58.7 5.6 %collective-permute-start.11 = (bf16[192,1920]{1,0:T(8,128)(2,1)S(1)}, bf16[192,1920]{1,0:T(8,128)(2,1)S(1)}, u32[]{:S(2)}, u32[]{:S(2)}) collective-permute-start(bf16[192,1920]{1,0:T(8,128)(2,1)S(1)} %get-tuple-element.67), channel_id=1, source_target_pairs={{0,1},{1,0},{2,3},{3,2},{4,5},{5,4},{6,7},{7,6},{8,9},{9,8},{10,11... | collective-permute-start | bytes 2211848 | tf_op jit(solution)/shard_map/ppermute | solution.py:364
  59.9 24.4 %collective-permute-start.15 = (bf16[192,1920]{1,0:T(8,128)(2,1)S(1)}, bf16[192,1920]{1,0:T(8,128)(2,1)S(1)}, u32[]{:S(2)}, u32[]{:S(2)}) collective-permute-start(bf16[192,1920]{1,0:T(8,128)(2,1)S(1)} %shard_map.117.refs_0_), channel_id=1, source_target_pairs={{0,2},{1,3},{2,0},{3,1},{4,6},{5,7},{6,4},{7,5},{8,10},{9,11},{10,... | collective-permute-start | bytes 2211848 | tf_op jit(solution)/shard_map/ppermute | solution.py:364
  60.7 6.0 %collective-permute-start.12 = (bf16[64,640]{1,0:T(8,128)(2,1)S(1)}, bf16[64,640]{1,0:T(8,128)(2,1)S(1)}, u32[]{:S(2)}, u32[]{:S(2)}) collective-permute-start(bf16[64,640]{1,0:T(8,128)(2,1)S(1)} %get-tuple-element.72), channel_id=1, source_target_pairs={{0,4},{4,0},{8,12},{12,8},{16,20},{20,16},{24,28},{28,24},{1,5},{5... | collective-permute-start | bytes 245768 | tf_op jit(solution)/shard_map/ppermute | solution.py:364
  62.5 4.9 %collective-permute-start.13 = (bf16[64,640]{1,0:T(8,128)(2,1)S(1)}, bf16[64,640]{1,0:T(8,128)(2,1)S(1)}, u32[]{:S(2)}, u32[]{:S(2)}) collective-permute-start(bf16[64,640]{1,0:T(8,128)(2,1)S(1)} %get-tuple-element.73), channel_id=1, source_target_pairs={{0,8},{4,12},{8,0},{12,4},{16,24},{20,28},{24,16},{28,20},{1,9},{5... | collective-permute-start | bytes 245768 | tf_op jit(solution)/shard_map/ppermute | solution.py:364
  62.8 5.4 %collective-permute-start.14 = (bf16[64,640]{1,0:T(8,128)(2,1)S(1)}, bf16[64,640]{1,0:T(8,128)(2,1)S(1)}, u32[]{:S(2)}, u32[]{:S(2)}) collective-permute-start(bf16[64,640]{1,0:T(8,128)(2,1)S(1)} %get-tuple-element.74), channel_id=1, source_target_pairs={{0,12},{4,8},{8,4},{12,0},{16,28},{20,24},{24,20},{28,16},{1,13},{... | collective-permute-start | bytes 245768 | tf_op jit(solution)/shard_map/ppermute | solution.py:364
  69.2 2.3 %collective-permute-start.16 = (bf16[192,640]{1,0:T(8,128)(2,1)S(1)}, bf16[192,640]{1,0:T(8,128)(2,1)S(1)}, u32[]{:S(2)}, u32[]{:S(2)}) collective-permute-start(bf16[192,640]{1,0:T(8,128)(2,1)S(1)} %get-tuple-element.82), channel_id=1, source_target_pairs={{0,1},{1,0},{2,3},{3,2},{4,5},{5,4},{6,7},{7,6},{8,9},{9,8},{10,11... | collective-permute-start | bytes 737288 | tf_op jit(solution)/shard_map/ppermute | solution.py:364
  69.2 2.2 %collective-permute-start.17 = (bf16[96,640]{1,0:T(8,128)(2,1)S(1)}, bf16[96,640]{1,0:T(8,128)(2,1)S(1)}, u32[]{:S(2)}, u32[]{:S(2)}) collective-permute-start(bf16[96,640]{1,0:T(8,128)(2,1)S(1)} %get-tuple-element.84), channel_id=1, source_target_pairs={{0,1},{1,0},{2,3},{3,2},{4,5},{5,4},{6,7},{7,6},{8,9},{9,8},{10,11... | collective-permute-start | bytes 368648 | tf_op jit(solution)/shard_map/ppermute | solution.py:364
  69.7 1.7 %collective-permute-start.18 = (bf16[96,640]{1,0:T(8,128)(2,1)S(1)}, bf16[96,640]{1,0:T(8,128)(2,1)S(1)}, u32[]{:S(2)}, u32[]{:S(2)}) collective-permute-start(bf16[96,640]{1,0:T(8,128)(2,1)S(1)} %get-tuple-element.85), channel_id=1, source_target_pairs={{0,1},{1,0},{2,3},{3,2},{4,5},{5,4},{6,7},{7,6},{8,9},{9,8},{10,11... | collective-permute-start | bytes 368648 | tf_op jit(solution)/shard_map/ppermute | solution.py:364
  69.8 14.4 %copy-start.6 = (s32[128,6]{0,1:T(8,128)S(1)}, s32[128,6]{0,1:T(8,128)}, u32[]{:S(2)}) copy-start(s32[128,6]{0,1:T(8,128)} %param.10) | copy-start | bytes 9220
  69.8 14.4 %copy-start.7 = (s32[128,6]{0,1:T(8,128)S(1)}, s32[128,6]{0,1:T(8,128)}, u32[]{:S(2)}) copy-start(s32[128,6]{0,1:T(8,128)} %param.11) | copy-start | bytes 9220
  69.8 14.5 %copy-start.8 = (s32[1,8]{1,0:T(1,128)S(1)}, s32[1,8]{1,0:T(1,128)}, u32[]{:S(2)}) copy-start(s32[1,8]{1,0:T(1,128)} %refs_2_.1) | copy-start | bytes 100
  71.5 12.7 %collective-permute-start.19 = (bf16[192,640]{1,0:T(8,128)(2,1)S(1)}, bf16[192,640]{1,0:T(8,128)(2,1)S(1)}, u32[]{:S(2)}, u32[]{:S(2)}) collective-permute-start(bf16[192,640]{1,0:T(8,128)(2,1)S(1)} %shard_map.123), channel_id=1, source_target_pairs={{0,2},{1,3},{2,0},{3,1},{4,6},{5,7},{6,4},{7,5},{8,10},{9,11},{10,... | collective-permute-start | bytes 737288 | tf_op jit(solution)/shard_map/ppermute | solution.py:364

commit v3 on v2

--- a/solution.py
+++ b/solution.py
@@ -22,7 +22,7 @@
 BLOCK = pl.BlockSpec()
 ANY = pl.BlockSpec(memory_space=pl.ANY)
 LANES = 128
-CODE, WEIGHT, CHOICE, SLOT = 0, 8, 16, 24
+CODE, WEIGHT, META_ROWS = 0, 8, 16
 
 
 def call(body, outs, specs, megabytes, flops=0, moved=0, scratch=(), after=(), out_specs=None, aliases=()):
@@ -43,10 +43,9 @@
 
 
 def routing_body(
-    capacity, n_exp, choice_ref, slot_ref, combine_ref, counts_ref, tok_ref, meta_ref, raw_ref, *outs
+    capacity, n_exp, choice_ref, slot_ref, combine_ref, counts_ref, tok_ref, meta_ref, *outs
 ):
     topk = choice_ref.shape[0]
-    columns = tok_ref.shape[1]
     choice = choice_ref[...]
     slot = slot_ref[...]
     limit = jnp.zeros_like(slot)
@@ -57,10 +56,6 @@
     meta_ref[...] = jnp.zeros_like(meta_ref)
     meta_ref[CODE : CODE + topk, :] = jnp.where(kept, choice * capacity + slot, -1).astype(jnp.float32)
     meta_ref[WEIGHT : WEIGHT + topk, :] = jnp.where(live, combine_ref[...].astype(jnp.float32), 0.0)
-    meta_ref[CHOICE : CHOICE + topk, :] = choice.astype(jnp.float32)
-    meta_ref[SLOT : SLOT + topk, :] = slot.astype(jnp.float32)
-    raw_ref[:, :columns] = tok_ref[...]
-    raw_ref[:, columns:] = meta_ref[...].T.astype(jnp.bfloat16)
     select(capacity, topk, meta_ref, tok_ref[...], outs)
 
 
@@ -98,15 +93,7 @@
             out[:, columns:] = jnp.where(lane < LANES // 2, weight, own_weight).astype(jnp.bfloat16)
 
 
-def select_first_body(capacity, topk, cut, raw_ref, own_meta_ref, *refs):
-    *outs, meta_ref = refs
-    columns = raw_ref.shape[1] - LANES
-    block = raw_ref[:, columns:].astype(jnp.float32).T
-    slot = block[SLOT : SLOT + 8]
-    meta_ref[...] = block
-    meta_ref[CODE : CODE + 8, :] = jnp.where(
-        slot < capacity, block[CHOICE : CHOICE + 8] * capacity + slot, -1.0
-    )
+def select_first_body(capacity, topk, cut, raw_ref, meta_ref, own_meta_ref, *outs):
     select(capacity, topk, meta_ref, raw_ref[:, cut[0] : cut[1]], outs, own_meta_ref)
 
 
@@ -151,17 +138,29 @@
         sum_ref[rows, :] = (across_ref[rows, :] + ref[...].astype(jnp.float32)).astype(jnp.bfloat16)
 
 
-def last_body(capacity, n_exp, cuts, choice_ref, slot_ref, counts_ref, score_ref, *refs):
-    sums, (out_ref, weight_ref, held, held_weight, sems) = refs[: 3 * len(cuts)], refs[3 * len(cuts) :]
+def summed_out(cut, sums, out_ref, held, sem):
+    keep_ref, from_core_ref, from_y_ref = sums
+    held[...] = (
+        keep_ref[...] + from_core_ref[...].astype(jnp.float32) + from_y_ref[...].astype(jnp.float32)
+    ).astype(jnp.bfloat16)
+    copy = pltpu.make_async_copy(held, out_ref.at[:, pl.ds(cut[0], cut[1] - cut[0])], sem)
+    copy.start()
+    return copy
+
+
+def last_body(cut, *refs):
+    *sums, _, out_ref, held, sem = refs
+    summed_out(cut, sums, out_ref, held, sem).wait()
+
+
+def returned_body(capacity, n_exp, cut, choice_ref, slot_ref, counts_ref, score_ref, far_half_ref, *refs):
+    sums, refs = refs[:3], refs[5:]
+    out_ref, weight_ref, gate_ref, up_ref, held, held_weight, sems, half_sems = refs
+    far = n_exp // 2
     copies = []
-    for k, (a, b) in enumerate(cuts):
-        keep_ref, from_core_ref, from_y_ref = sums[3 * k : 3 * k + 3]
-        held[:, a:b] = (
-            keep_ref[...] + from_core_ref[...].astype(jnp.float32) + from_y_ref[...].astype(jnp.float32)
-        ).astype(jnp.bfloat16)
-        lanes = pl.ds(a, b - a)
-        copies.append(pltpu.make_async_copy(held.at[:, lanes], out_ref.at[:, lanes], sems.at[k]))
-        copies[-1].start()
+    for m in range(0, far, 2):
+        copies += copies_out(far, m, far, far_half_ref, (gate_ref, up_ref), half_sems)
+    copies.append(summed_out(cut, sums, out_ref, held, sems.at[0]))
     topk, tokens = choice_ref.shape
     choice = choice_ref[...]
     slot = slot_ref[...]
@@ -177,15 +176,17 @@
     split = jnp.concatenate([high, middle, low], axis=0)
     rank = lax.broadcasted_iota(jnp.int32, (capacity, tokens), 0)
     expert = lax.broadcasted_iota(jnp.int32, (n_exp, tokens), 0)
+    onehot = jnp.concatenate(
+        [jnp.where(rank == slot[k : k + 1, :], 1.0, 0.0).astype(jnp.bfloat16) for k in range(topk)], axis=1
+    )
+    parts = jnp.dot(split, onehot, preferred_element_type=jnp.float32)
+    every = parts[:n_exp] + parts[n_exp : 2 * n_exp] + parts[2 * n_exp :]
     found = []
     for k in range(topk):
-        onehot = jnp.where(rank == slot[k : k + 1, :], 1.0, 0.0).astype(jnp.bfloat16)
-        parts = jnp.dot(split, onehot, preferred_element_type=jnp.float32)
-        every = parts[:n_exp] + parts[n_exp : 2 * n_exp] + parts[2 * n_exp :]
-        mine = jnp.where(expert == choice[k : k + 1, :], every, 0.0)
+        mine = jnp.where(expert == choice[k : k + 1, :], every[:, k * tokens : (k + 1) * tokens], 0.0)
         found.append(jnp.sum(mine, axis=0, keepdims=True))
     held_weight[...] = jnp.where(live, jnp.concatenate(found, axis=0), 0.0)
-    copies.append(pltpu.make_async_copy(held_weight, weight_ref, sems.at[len(cuts)]))
+    copies.append(pltpu.make_async_copy(held_weight, weight_ref, sems.at[1]))
     copies[-1].start()
     for copy in copies:
         copy.wait()
@@ -266,10 +267,10 @@
     proj_ref[...] = nt(jnp.concatenate([p[...] for p in own], axis=0), weight_ref[...])
 
 
-def finish_half(first, far, proj, weights, hidden_ref, gate_factor_ref, up_factor_ref, outs, held, sems):
+def finish_half(first, far, proj, weights, hidden_ref, gate_factor_ref, up_factor_ref, held, then):
     here = lax.axis_index("exp")
     count = 2 * (proj.shape[0] // far)
-    scores, copies = [], []
+    scores = []
     for m in range(0, far, 2):
         near = slice(m * count // 2, m * count // 2 + count)
         at = slice((first + m) * count // 2, (first + m) * count // 2 + count)
@@ -277,29 +278,35 @@
             proj[near], weights[near], hidden_ref[at, :], gate_factor_ref[at, :], up_factor_ref[at, :]
         )
         scores.append(score)
-        lower = pl.multiple_of(((here ^ (first + m)) // 2) * count, count)
         for i in range(2):
             mine = slice(i * count // 2, (i + 1) * count // 2)
             within = pl.multiple_of(lax.rem(here ^ i, 2) * (count // 2), count // 2)
             there = pl.ds(m // 2 * count + within, count // 2)
             held[0, there, :] = gate[mine]
             held[1, there, :] = up[mine]
-        for i, out in enumerate(outs):
-            copy = pltpu.make_async_copy(
-                held.at[i, pl.ds(m // 2 * count, count), :], out.at[pl.ds(lower, count), :], sems.at[m // 2, i]
-            )
-            copy.start()
-            copies.append(copy)
-    return scores, copies
+        then(m)
+    return scores
+
+
+def copies_out(first, m, far, held, outs, sems):
+    count = 2 * (held.shape[1] // far)
+    lower = pl.multiple_of(((lax.axis_index("exp") ^ (first + m)) // 2) * count, count)
+    copies = []
+    for i, out in enumerate(outs):
+        source = held.at[i, pl.ds(m // 2 * count, count), :]
+        copies.append(pltpu.make_async_copy(source, out.at[pl.ds(lower, count), :], sems.at[m // 2, i]))
+        copies[-1].start()
+    return copies
 
 
 def project_far_body(far, cut, *refs):
     pieces, refs = refs[:far], refs[far:]
     weight_ref, own_proj_ref, hidden_ref, gate_factor_ref, up_factor_ref, *outs = refs
     proj_ref, gate_ref, up_ref, score_ref, held, sems = outs
-    scores, copies = finish_half(
+    copies = []
+    scores = finish_half(
         0, far, own_proj_ref[...], weights_of(pieces, True), hidden_ref, gate_factor_ref, up_factor_ref,
-        (gate_ref, up_ref), held, sems,
+        held, lambda m: copies.extend(copies_out(0, m, far, held, (gate_ref, up_ref), sems)),
     )
     for i, score in enumerate(scores):
         score_ref[i : i + 1, :] = score
@@ -312,23 +319,21 @@
 def final_body(far, cut, *refs):
     pieces, scales, refs = refs[:far], refs[far : 2 * far], refs[2 * far :]
     (
-        weight_ref, proj_ref, hidden_ref, gate_factor_ref, up_factor_ref, own_score_ref, _, _,
-        gate_ref, up_ref, score_ref, held, sems,
+        weight_ref, proj_ref, hidden_ref, gate_factor_ref, up_factor_ref, own_score_ref,
+        score_ref, held,
     ) = refs
     here = lax.axis_index("exp")
     capacity = pieces[0].shape[0]
     rows = jnp.concatenate([p[...] for p in pieces], axis=0)
     proj = proj_ref[...] + nt(rows, weight_ref[:, cut[0] : cut[1]])
-    scores, copies = finish_half(
+    scores = finish_half(
         far, far, proj, weights_of(scales, False), hidden_ref, gate_factor_ref, up_factor_ref,
-        (gate_ref, up_ref), held, sems,
+        held, lambda m: None,
     )
     for m in range(0, far, 2):
         for first, score in ((far + m, scores[m // 2]), (m, own_score_ref[m // 2 : m // 2 + 1, :])):
             for i in range(2):
                 score_ref[pl.ds(here ^ (first + i), 1), :] = score[:, i * capacity : (i + 1) * capacity]
-    for copy in copies:
-        copy.wait()
 
 
 def relayed(
@@ -366,16 +371,15 @@
     def spread(found):
         return [found[0]] + [hop(found[m], "exp", m) for m in range(1, far)]
 
-    meta, payload, *found = call(
+    meta, *found = call(
         functools.partial(routing_body, capacity, n_exp),
-        [shape(LANES, LANES, dtype=f32), shape(tok_rows, width + LANES)]
-        + [shape(capacity, width)] * far,
+        [shape(META_ROWS, LANES, dtype=f32)] + [shape(capacity, width)] * far,
         [BLOCK, BLOCK, BLOCK, SMEM, BLOCK],
         56,
         flops=2 * far * capacity * tok_rows * width,
         moved=out_grad.size * 4,
     )(token_expert_choice.T, slots.T, combine.T, counts, out_grad)
-    raw = hop(payload, "exp", far)
+    raw = hop(out_grad, "exp", far)
     own = spread(found)
     hidden, gate_factor, up_factor, turned, meta = call(
         functools.partial(factors_body, capacity, n_edp),
@@ -384,7 +388,7 @@
             shape(rows, units, dtype=f32),
             shape(rows, units, dtype=f32),
             shape(n_edp, shard, rows),
-            shape(LANES, LANES, dtype=f32),
+            shape(META_ROWS, LANES, dtype=f32),
         ],
         [VMEM] * 3,
         24,
@@ -393,8 +397,8 @@
         scratch=[pltpu.VMEM((units, rows), bf16)],
         after=[own[0]],
     )(stored_gate_preact[0, 0], stored_up_preact[0, 0], meta)
-    weight_core = hop(down_weight[0], "edp", 1)
-    weight_y = hop(down_weight[0], "edp", 2, (weight_core, payload))
+    weight_y = hop(down_weight[0], "edp", 2)
+    far_meta = hop(meta, "exp", far, own[1])
 
     def term(k, others, scales, after=()):
         return call(
@@ -419,18 +423,18 @@
         )
         return sent, hop(sent, "edp", 2)
 
-    *found, far_meta = call(
+    found = call(
         functools.partial(select_first_body, capacity, topk, cuts[0]),
-        [shape(capacity, sizes[0] + LANES)] * far
-        + [shape(LANES, LANES, dtype=f32)],
-        [VMEM] * 2,
+        [shape(capacity, sizes[0] + LANES)] * far,
+        [VMEM] * 3,
         16,
         flops=2 * far * capacity * tok_rows * sizes[0],
         moved=4 * far * capacity * sizes[0],
         after=[*own[1:], hidden, weight_y],
-    )(raw, meta)
+    )(raw, far_meta, meta)
     far0 = spread(found)
-    weight_both = hop(weight_y, "edp", 1, far_meta)
+    weight_core = hop(down_weight[0], "edp", 1, found[0])
+    weight_both = hop(weight_y, "edp", 1, found[0])
     weight, own_proj = call(
         functools.partial(project_own_body, far),
         [shape(units, width), shape(far * capacity, units, dtype=f32)],
@@ -484,36 +488,41 @@
     (keep0,) = more_terms([0], [shape(shard, sizes[0], dtype=f32)], [proj])
     keep1, across1, *send1 = term(1, far1, far0, [keep0])
     core1 = cores(send1)
-    gate_preact_gradient, up_preact_gradient, score = call(
+    score, far_half = call(
         functools.partial(final_body, far, cuts[1]),
-        [shape(rows, units), shape(rows, units), shape(n_exp, capacity, dtype=f32)],
-        [VMEM] * (2 * far + 6) + [ANY] * 2,
+        [shape(n_exp, capacity, dtype=f32), shape(2, far * capacity, units)],
+        [VMEM] * (2 * far + 6),
         24,
-        scratch=half_scratch,
         after=[keep1],
-        out_specs=[ANY, ANY, VMEM],
-        aliases=[(2 * far + 6, 0), (2 * far + 7, 1)],
-    )(
-        *far1, *far0, weight, proj, hidden, gate_factor, up_factor, own_score,
-        gate_preact_gradient, up_preact_gradient,
-    )
+    )(*far1, *far0, weight, proj, hidden, gate_factor, up_factor, own_score)
     _, from_y1 = across(1, across1, core1[1:], [score, core1[0]])
     returned = lax.all_to_all(score, "exp", split_axis=0, concat_axis=0)
-    down_matrix_gradient, combine_weight_gradient = call(
-        functools.partial(last_body, capacity, n_exp, cuts),
-        [shape(shard, width), shape(topk, tok_rows, dtype=f32)],
-        [VMEM, VMEM, SMEM] + [VMEM] * (1 + 3 * len(cuts)),
+    down_matrix_gradient, combine_weight_gradient, gate_preact_gradient, up_preact_gradient = call(
+        functools.partial(returned_body, capacity, n_exp, cuts[0]),
+        [shape(shard, width), shape(topk, tok_rows, dtype=f32), shape(rows, units), shape(rows, units)],
+        [VMEM, VMEM, SMEM] + [VMEM] * 5 + [ANY] * 2,
         16,
         scratch=[
-            pltpu.VMEM((shard, width), bf16),
+            pltpu.VMEM((shard, sizes[0]), bf16),
             pltpu.VMEM((topk, tok_rows), f32),
-            pltpu.SemaphoreType.DMA((len(cuts) + 1,)),
+            pltpu.SemaphoreType.DMA((2,)),
+            half_scratch[1],
         ],
-        out_specs=[ANY, ANY],
+        out_specs=[ANY] * 4,
+        aliases=[(8, 2), (9, 3)],
     )(
-        token_expert_choice.T, slots.T, counts, returned,
-        keep0, core0, from_y0, keep1, core1[0], from_y1,
-    )
+        token_expert_choice.T, slots.T, counts, returned, far_half, keep0, core0, from_y0,
+        gate_preact_gradient, up_preact_gradient,
+    )
+    (down_matrix_gradient,) = call(
+        functools.partial(last_body, cuts[1]),
+        [shape(shard, width)],
+        [VMEM] * 3 + [ANY],
+        8,
+        scratch=[pltpu.VMEM((shard, sizes[1]), bf16), pltpu.SemaphoreType.DMA],
+        out_specs=[ANY],
+        aliases=[(3, 0)],
+    )(keep1, core1[0], from_y1, down_matrix_gradient)
     return (
         gate_preact_gradient[None, None],
         up_preact_gradient[None, None],

time: 86.7 us -> 85.1 us (0.982)
  blocking collectives: 11.1 us -> 10.1 us
    all_to_all x1, blocking collectives: 11.1 us -> 10.1 us  [relayed(): returned = lax.all_to_all(score, 'exp', split_axis=0, concat_axis=0)]
    ppermute x20 -> x21, waiting for transfers between devices: 35.3 us -> 34.8 us  [hop(): return lax.ppermute(x, axis, flip(lax.axis_size(axis), mask))]
    pallas_call x3 -> x4, Pallas kernels: 6.64 us -> 6.28 us  [the longest x1 2.68 us: relayed(): call(functools.partial(routing_body, capacity, n_exp), [shape(META_ROWS,...]
    ppermute x20 -> x21, starting transfers between devices: 20 us -> 19.7 us  [hop(): return lax.ppermute(x, axis, flip(lax.axis_size(axis), mask))]
  transfers between devices with their start and end apart: 20 -> 21, of which waited for: 10 -> 10; matrix products, arithmetic and copies ran while one was open for 0% -> 0% of each run, Pallas kernels for 14% -> 15%
where the time goes in v3:
time: 85.1 us; the launch traced here: 84.7 us
  waiting for transfers between devices  34.8 us (41%)
  starting transfers between devices  19.7 us (23%)
  Pallas kernels  14.7 us (17%)
  blocking collectives  10.1 us (12%)
  local copies, waits for them, and re-layouts  4.62 us (5%)
    ppermute x21, waiting for transfers between devices, hop(): return lax.ppermute(x, axis, flip(lax.axis_size(axis), mask))  34.8 us
    ppermute x21, starting transfers between devices, hop(): return lax.ppermute(x, axis, flip(lax.axis_size(axis), mask))  19.7 us
    all_to_all x1, blocking collectives, relayed(): returned = lax.all_to_all(score, 'exp', split_axis=0, concat_axis=0)  10.1 us
    unnamed x18, local copies, waits for them, and re-layouts  4.62 us
    pallas_call x1, Pallas kernels, relayed(): call(functools.partial(routing_body, capacity, n_exp), [shape(META_ROWS,...  2.68 us
    pallas_call x1, Pallas kernels, relayed(): call(functools.partial(returned_body, capacity, n_exp, cuts[0]), [shape(s...  2.08 us
    pallas_call x1, Pallas kernels, relayed(): call(functools.partial(project_far_body, far, cuts[0]), [shape(far * capa...  1.82 us
    pallas_call x2, Pallas kernels, more_terms(): call(functools.partial(more_terms_body, 640, shards), outs, [VMEM] * 2, 2...  1.72 us
  transfers between devices with their start and end apart: 21, of which 10 were waited for; matrix products, arithmetic and copies ran while one was open for 0% of the time, Pallas kernels for 15%

profile of v3, /device:TPU:0, one launch (start us, length us, event | category | flops | bytes accessed | tf_op | source)
XLA Modules:
  0.0 84.7 jit_solution(4542486873994331512)
XLA Ops:
  0.6 3.0 %collective-permute-start.3 = (bf16[192,2560]{1,0:T(8,128)(2,1)}, bf16[192,2560]{1,0:T(8,128)(2,1)S(1)}, u32[]{:S(2)}, u32[]{:S(2)}) collective-permute-start(bf16[192,2560]{1,0:T(8,128)(2,1)} %bitcast.14), channel_id=1, source_target_pairs={{0,2},{1,3},{2,0},{3,1},{4,6},{5,7},{6,4},{7,5},{8,10},{9,11},{10,... | collective-permute-start | bytes 2949128 | tf_op jit(solution)/shard_map/ppermute | solution.py:369
  3.7 2.6 %collective-permute-start.4 = (bf16[128,2560]{1,0:T(8,128)(2,1)}, bf16[128,2560]{1,0:T(8,128)(2,1)S(1)}, u32[]{:S(2)}, u32[]{:S(2)}) collective-permute-start(bf16[128,2560]{1,0:T(8,128)(2,1)} %refs_4_.1), channel_id=1, source_target_pairs={{0,16},{4,20},{8,24},{12,28},{16,0},{20,4},{24,8},{28,12},{1,17},{... | collective-permute-start | bytes 1966088 | tf_op jit(solution)/shard_map/ppermute | solution.py:369
  6.3 2.7 %shard_map.111 = (f32[16,128]{1,0:T(8,128)}, bf16[64,2560]{1,0:T(8,128)(2,1)}, bf16[64,2560]{1,0:T(8,128)(2,1)}, bf16[64,2560]{1,0:T(8,128)(2,1)}, bf16[64,2560]{1,0:T(8,128)(2,1)}) custom-call(s32[6,128]{1,0:T(8,128)} %bitcast.19, s32[6,128]{1,0:T(8,128)} %bitcast.21, bf16[6,128]{1,0:T(8,128)(2,1)} %bitcast.28, s32[1,8]{1,0:T(1,128)} %refs_2_.1, ...), custom_call_target="tpu_custom_call" | custom-call | flops 167772160 | bytes 1310720 | tf_op jit(solution)/shard_map/pallas_call | solution.py:374
  8.9 1.5 %collective-permute-start = (bf16[64,2560]{1,0:T(8,128)(2,1)}, bf16[64,2560]{1,0:T(8,128)(2,1)S(1)}, u32[]{:S(2)}, u32[]{:S(2)}) collective-permute-start(bf16[64,2560]{1,0:T(8,128)(2,1)} %get-tuple-element.49), channel_id=1, source_target_pairs={{0,4},{4,0},{8,12},{12,8},{16,20},{20,16},{24,28},{28,24},{1,5},{5... | collective-permute-start | bytes 983048 | tf_op jit(solution)/shard_map/ppermute | solution.py:369
  10.4 1.6 %collective-permute-start.1 = (bf16[64,2560]{1,0:T(8,128)(2,1)}, bf16[64,2560]{1,0:T(8,128)(2,1)S(1)}, u32[]{:S(2)}, u32[]{:S(2)}) collective-permute-start(bf16[64,2560]{1,0:T(8,128)(2,1)} %get-tuple-element.50), channel_id=1, source_target_pairs={{0,8},{4,12},{8,0},{12,4},{16,24},{20,28},{24,16},{28,20},{1,9},{5... | collective-permute-start | bytes 983048 | tf_op jit(solution)/shard_map/ppermute | solution.py:369
  12.0 0.4 collective-permute-start.2
  12.4 1.0 %copy-done = bf16[64,2560]{1,0:T(8,128)(2,1)S(1)} copy-done((bf16[64,2560]{1,0:T(8,128)(2,1)S(1)}, bf16[64,2560]{1,0:T(8,128)(2,1)}, u32[]{:S(2)}) %copy-start) | copy-done | bytes 327704
  13.4 1.1 %copy-done.3 = bf16[1,1,512,768]{3,2,1,0:T(8,128)(2,1)S(1)} copy-done((bf16[1,1,512,768]{3,2,1,0:T(8,128)(2,1)S(1)}, bf16[1,1,512,768]{3,2,1,0:T(8,128)(2,1)}, u32[]{:S(2)}) %copy-start.3) | copy-done | bytes 786456
  14.5 1.1 %copy-done.4 = bf16[1,1,512,768]{3,2,1,0:T(8,128)(2,1)S(1)} copy-done((bf16[1,1,512,768]{3,2,1,0:T(8,128)(2,1)S(1)}, bf16[1,1,512,768]{3,2,1,0:T(8,128)(2,1)}, u32[]{:S(2)}) %copy-start.4) | copy-done | bytes 786456
  15.7 0.7 copy-done.7
  16.4 0.8 shard_map.112
  17.1 1.8 %collective-permute-done.refs_0_.refs_5_.refs_3_ = bf16[64,2560]{1,0:T(8,128)(2,1)S(1)} collective-permute-done((bf16[64,2560]{1,0:T(8,128)(2,1)}, bf16[64,2560]{1,0:T(8,128)(2,1)S(1)}, u32[]{:S(2)}, u32[]{:S(2)}) %collective-permute-start) | collective-permute-done | bytes 327712 | tf_op jit(solution)/shard_map/ppermute | solution.py:369
  18.9 0.0 collective-permute-start.5
  18.9 9.9 %collective-permute-done.1.refs_1_.refs_6_.refs_4_ = bf16[64,2560]{1,0:T(8,128)(2,1)S(1)} collective-permute-done((bf16[64,2560]{1,0:T(8,128)(2,1)}, bf16[64,2560]{1,0:T(8,128)(2,1)S(1)}, u32[]{:S(2)}, u32[]{:S(2)}) %collective-permute-start.1) | collective-permute-done | bytes 327712 | tf_op jit(solution)/shard_map/ppermute | solution.py:369
  28.8 10.5 %collective-permute-done.2.refs_2_.refs_7_.refs_5_ = bf16[64,2560]{1,0:T(8,128)(2,1)S(1)} collective-permute-done((bf16[64,2560]{1,0:T(8,128)(2,1)}, bf16[64,2560]{1,0:T(8,128)(2,1)S(1)}, u32[]{:S(2)}, u32[]{:S(2)}) %collective-permute-start.2) | collective-permute-done | bytes 327712 | tf_op jit(solution)/shard_map/ppermute | solution.py:369
  39.3 0.0 collective-permute-done.5.refs_6_.refs_2_
  39.4 0.0 collective-permute-done.4.refs_5_.refs_1_
  39.4 0.0 collective-permute-done.3.refs_4_.refs_2_
  39.4 0.0 copy-start.2
  39.4 0.0 copy-start.1
  39.4 0.4 shard_map.113
  39.8 0.1 collective-permute-start.7
  39.9 0.7 copy-done.2
  40.6 0.0 collective-permute-start.6
  40.6 0.0 collective-permute-start.10
  40.6 1.5 %collective-permute-start.8 = (bf16[64,2048]{1,0:T(8,128)(2,1)S(1)}, bf16[64,2048]{1,0:T(8,128)(2,1)S(1)}, u32[]{:S(2)}, u32[]{:S(2)}) collective-permute-start(bf16[64,2048]{1,0:T(8,128)(2,1)S(1)} %get-tuple-element.59), channel_id=1, source_target_pairs={{0,4},{4,0},{8,12},{12,8},{16,20},{20,16},{24,28},{28,24},{1,5},{5... | collective-permute-start | bytes 786440 | tf_op jit(solution)/shard_map/ppermute | solution.py:369
  42.1 2.0 %collective-permute-start.9 = (bf16[64,2048]{1,0:T(8,128)(2,1)S(1)}, bf16[64,2048]{1,0:T(8,128)(2,1)S(1)}, u32[]{:S(2)}, u32[]{:S(2)}) collective-permute-start(bf16[64,2048]{1,0:T(8,128)(2,1)S(1)} %get-tuple-element.60), channel_id=1, source_target_pairs={{0,8},{4,12},{8,0},{12,4},{16,24},{20,28},{24,16},{28,20},{1,9},{5... | collective-permute-start | bytes 786440 | tf_op jit(solution)/shard_map/ppermute | solution.py:369
  44.1 0.0 collective-permute-done.7.refs_3_
  44.1 0.0 collective-permute-done.6.refs_1_
  44.1 1.5 %shard_map.114 = (bf16[768,2560]{1,0:T(8,128)(2,1)S(1)}, f32[256,768]{1,0:T(8,128)S(1)}) custom-call(bf16[192,2560]{1,0:T(8,128)(2,1)S(1)} %bitcast.16, bf16[192,2560]{1,0:T(8,128)(2,1)S(1)} %collective-permute-done.6.refs_1_, bf16[192,2560]{1,0:T(8,128)(2,1)S(1)} %collective-permute-done.3.refs_4_.refs_2_, ...), custom_call_target="tpu_custom_call" | custom-call | tf_op jit(solution)/shard_map/pallas_call | solution.py:438
  45.5 5.1 %collective-permute-done.10.refs_9_.refs_6_.refs_13_.refs_8_ = bf16[64,2048]{1,0:T(8,128)(2,1)S(1)} collective-permute-done((bf16[64,2048]{1,0:T(8,128)(2,1)S(1)}, bf16[64,2048]{1,0:T(8,128)(2,1)S(1)}, u32[]{:S(2)}, u32[]{:S(2)}) %collective-permute-start.10) | collective-permute-done | bytes 262176 | tf_op jit(solution)/shard_map/ppermute | solution.py:369
  50.6 4.3 %collective-permute-done.8.refs_7_.refs_4_.refs_11_.refs_6_ = bf16[64,2048]{1,0:T(8,128)(2,1)S(1)} collective-permute-done((bf16[64,2048]{1,0:T(8,128)(2,1)S(1)}, bf16[64,2048]{1,0:T(8,128)(2,1)S(1)}, u32[]{:S(2)}, u32[]{:S(2)}) %collective-permute-start.8) | collective-permute-done | bytes 262176 | tf_op jit(solution)/shard_map/ppermute | solution.py:369
  54.9 1.0 %collective-permute-done.9.refs_8_.refs_5_.refs_12_.refs_7_ = bf16[64,2048]{1,0:T(8,128)(2,1)S(1)} collective-permute-done((bf16[64,2048]{1,0:T(8,128)(2,1)S(1)}, bf16[64,2048]{1,0:T(8,128)(2,1)S(1)}, u32[]{:S(2)}, u32[]{:S(2)}) %collective-permute-start.9) | collective-permute-done | bytes 262176 | tf_op jit(solution)/shard_map/ppermute | solution.py:369
  55.9 0.8 shard_map.115
  56.7 0.1 collective-permute-start.11
  56.8 1.1 %shard_map.116 = (f32[192,1920]{1,0:T(8,128)S(1)}, bf16[192,1920]{1,0:T(8,128)(2,1)S(1)}) custom-call(bf16[4,192,512]{2,1,0:T(8,128)(2,1)S(1)} %get-tuple-element.48.refs_1_.refs_0_, bf16[512,1920]{1,0:T(8,128)(2,1)S(1)} %get-tuple-element.62.refs_1_.refs_2_), custom_call_target="tpu_custom_call" | custom-call | tf_op jit(solution)/shard_map/pallas_call | solution.py:453
  57.9 0.6 collective-permute-start.12
  58.5 0.5 collective-permute-done.11.refs_1_
  59.0 0.1 shard_map.117.refs_0_
  59.1 0.5 collective-permute-start.16
  59.6 0.3 shard_map.118
  59.9 0.7 collective-permute-start.13
  60.6 0.3 collective-permute-start.14
  60.8 2.6 %collective-permute-start.15 = (bf16[64,640]{1,0:T(8,128)(2,1)S(1)}, bf16[64,640]{1,0:T(8,128)(2,1)S(1)}, u32[]{:S(2)}, u32[]{:S(2)}) collective-permute-start(bf16[64,640]{1,0:T(8,128)(2,1)S(1)} %get-tuple-element.73), channel_id=1, source_target_pairs={{0,12},{4,8},{8,4},{12,0},{16,28},{20,24},{24,20},{28,16},{1,13},{... | collective-permute-start | bytes 245768 | tf_op jit(solution)/shard_map/ppermute | solution.py:369
  63.5 0.0 collective-permute-done.12.refs_2_.refs_6_
  63.5 1.8 %shard_map.119 = (f32[256,768]{1,0:T(8,128)S(1)}, bf16[512,768]{1,0:T(8,128)(2,1)}, bf16[512,768]{1,0:T(8,128)(2,1)}, f32[2,128]{1,0:T(2,128)S(1)}) custom-call(bf16[192,1920]{1,0:T(8,128)(2,1)S(1)} %shard_map.117.refs_0_, bf16[64,640]{1,0:T(8,128)(2,1)S(1)} %get-tuple-element.65.refs_1_.refs_6_, ...), custom_call_target="tpu_custom_call" | custom-call | tf_op jit(solution)/shard_map/pallas_call | solution.py:474
  65.3 0.6 shard_map.120.refs_0_.refs_5_
  65.9 0.0 collective-permute-done.13.refs_7_.refs_2_
  65.9 0.0 collective-permute-done.14.refs_8_.refs_3_
  66.0 1.2 %collective-permute-done.15.refs_9_.refs_4_ = bf16[64,640]{1,0:T(8,128)(2,1)S(1)} collective-permute-done((bf16[64,640]{1,0:T(8,128)(2,1)S(1)}, bf16[64,640]{1,0:T(8,128)(2,1)S(1)}, u32[]{:S(2)}, u32[]{:S(2)}) %collective-permute-start.15) | collective-permute-done | bytes 81952 | tf_op jit(solution)/shard_map/ppermute | solution.py:369
  67.1 0.9 %shard_map.121 = (f32[192,640]{1,0:T(8,128)S(1)}, f32[192,640]{1,0:T(8,128)S(1)}, bf16[192,640]{1,0:T(8,128)(2,1)S(1)}, bf16[96,640]{1,0:T(8,128)(2,1)S(1)}, bf16[96,640]{1,0:T(8,128)(2,1)S(1)}) custom-call(f32[192,1920]{1,0:T(8,128)S(1)} %shard_map.120.refs_0_.refs_5_, bf16[4,192,512]{2,1,0:T(8,128)(2,1)S(1)} %get-tuple-element.48.refs_1_.refs_0_, ...), custom_call_target="tpu_custom_call" | custom-call | flops 503316480 | bytes 3276800 | tf_op jit(solution)/shard_map/pallas_call | solution.py:404
  68.1 0.1 collective-permute-start.17
  68.1 0.5 collective-permute-start.18
  68.6 0.1 collective-permute-start.19
  68.7 0.7 shard_map.122
  69.5 0.4 collective-permute-done.18.refs_3_
  69.8 0.2 collective-permute-done.19.refs_4_
  70.0 0.0 collective-permute-done.17.refs_1_
  70.0 0.1 shard_map.124
  70.1 1.6 %collective-permute-start.20 = (bf16[192,640]{1,0:T(8,128)(2,1)S(1)}, bf16[192,640]{1,0:T(8,128)(2,1)S(1)}, u32[]{:S(2)}, u32[]{:S(2)}) collective-permute-start(bf16[192,640]{1,0:T(8,128)(2,1)S(1)} %shard_map.124), channel_id=1, source_target_pairs={{0,2},{1,3},{2,0},{3,1},{4,6},{5,7},{6,4},{7,5},{8,10},{9,11},{10,... | collective-permute-start | bytes 737288 | tf_op jit(solution)/shard_map/ppermute | solution.py:369
  71.7 10.1 %all_to_all.11 = f32[8,1,64]{2,1,0:T(1,128)S(1)} all-to-all(f32[8,1,64]{2,1,0:T(1,128)S(1)} %bitcast.23), channel_id=1, replica_groups=mesh['exp'=8,'edp'=4] {'exp'}, dimensions={0} | all-to-all | bytes 4096 | tf_op jit(solution)/shard_map/all_to_all | solution.py:499
  81.8 0.0 collective-permute-done.16.refs_7_
  81.8 2.1 %shard_map.123 = (bf16[192,2560]{1,0:T(8,128)(2,1)}, f32[6,128]{1,0:T(8,128)}, bf16[512,768]{1,0:T(8,128)(2,1)}, bf16[512,768]{1,0:T(8,128)(2,1)}) custom-call(s32[6,128]{1,0:T(8,128)S(1)} %bitcast.20, s32[6,128]{1,0:T(8,128)S(1)} %bitcast.22, s32[1,8]{1,0:T(1,128)S(1)} %copy-done.8, ...), custom_call_target="tpu_custom_call", output_to_operand_aliasing={{2}: (8, {}), {3}: (9, {})} | custom-call | tf_op jit(solution)/shard_map/pallas_call | solution.py:500
  83.9 0.8 shard_map.125
  (12 shorter events, 0.0 us)
Async XLA Ops:
  0.6 38.7 %collective-permute-start.3 = (bf16[192,2560]{1,0:T(8,128)(2,1)}, bf16[192,2560]{1,0:T(8,128)(2,1)S(1)}, u32[]{:S(2)}, u32[]{:S(2)}) collective-permute-start(bf16[192,2560]{1,0:T(8,128)(2,1)} %bitcast.14), channel_id=1, source_target_pairs={{0,2},{1,3},{2,0},{3,1},{4,6},{5,7},{6,4},{7,5},{8,10},{9,11},{10,... | collective-permute-start | bytes 2949128 | tf_op jit(solution)/shard_map/ppermute | solution.py:369
  3.7 35.7 %collective-permute-start.4 = (bf16[128,2560]{1,0:T(8,128)(2,1)}, bf16[128,2560]{1,0:T(8,128)(2,1)S(1)}, u32[]{:S(2)}, u32[]{:S(2)}) collective-permute-start(bf16[128,2560]{1,0:T(8,128)(2,1)} %refs_4_.1), channel_id=1, source_target_pairs={{0,16},{4,20},{8,24},{12,28},{16,0},{20,4},{24,8},{28,12},{1,17},{... | collective-permute-start | bytes 1966088 | tf_op jit(solution)/shard_map/ppermute | solution.py:369
  8.9 10.0 %collective-permute-start = (bf16[64,2560]{1,0:T(8,128)(2,1)}, bf16[64,2560]{1,0:T(8,128)(2,1)S(1)}, u32[]{:S(2)}, u32[]{:S(2)}) collective-permute-start(bf16[64,2560]{1,0:T(8,128)(2,1)} %get-tuple-element.49), channel_id=1, source_target_pairs={{0,4},{4,0},{8,12},{12,8},{16,20},{20,16},{24,28},{28,24},{1,5},{5... | collective-permute-start | bytes 983048 | tf_op jit(solution)/shard_map/ppermute | solution.py:369
  10.4 18.4 %collective-permute-start.1 = (bf16[64,2560]{1,0:T(8,128)(2,1)}, bf16[64,2560]{1,0:T(8,128)(2,1)S(1)}, u32[]{:S(2)}, u32[]{:S(2)}) collective-permute-start(bf16[64,2560]{1,0:T(8,128)(2,1)} %get-tuple-element.50), channel_id=1, source_target_pairs={{0,8},{4,12},{8,0},{12,4},{16,24},{20,28},{24,16},{28,20},{1,9},{5... | collective-permute-start | bytes 983048 | tf_op jit(solution)/shard_map/ppermute | solution.py:369
  12.0 27.3 %collective-permute-start.2 = (bf16[64,2560]{1,0:T(8,128)(2,1)}, bf16[64,2560]{1,0:T(8,128)(2,1)S(1)}, u32[]{:S(2)}, u32[]{:S(2)}) collective-permute-start(bf16[64,2560]{1,0:T(8,128)(2,1)} %get-tuple-element.51), channel_id=1, source_target_pairs={{0,12},{4,8},{8,4},{12,0},{16,28},{20,24},{24,20},{28,16},{1,13},{... | collective-permute-start | bytes 983048 | tf_op jit(solution)/shard_map/ppermute | solution.py:369
  12.4 1.0 %copy-start = (bf16[64,2560]{1,0:T(8,128)(2,1)S(1)}, bf16[64,2560]{1,0:T(8,128)(2,1)}, u32[]{:S(2)}) copy-start(bf16[64,2560]{1,0:T(8,128)(2,1)} %get-tuple-element.46.refs_0_.refs_4_.refs_2_) | copy-start | bytes 983044
  13.4 1.1 %copy-start.3 = (bf16[1,1,512,768]{3,2,1,0:T(8,128)(2,1)S(1)}, bf16[1,1,512,768]{3,2,1,0:T(8,128)(2,1)}, u32[]{:S(2)}) copy-start(bf16[1,1,512,768]{3,2,1,0:T(8,128)(2,1)} %param.14) | copy-start | bytes 2359300
  14.5 1.1 %copy-start.4 = (bf16[1,1,512,768]{3,2,1,0:T(8,128)(2,1)S(1)}, bf16[1,1,512,768]{3,2,1,0:T(8,128)(2,1)}, u32[]{:S(2)}) copy-start(bf16[1,1,512,768]{3,2,1,0:T(8,128)(2,1)} %param.15) | copy-start | bytes 2359300
  15.7 0.7 copy-start.7
  18.9 20.5 %collective-permute-start.5 = (f32[16,128]{1,0:T(8,128)S(1)}, f32[16,128]{1,0:T(8,128)S(1)}, u32[]{:S(2)}, u32[]{:S(2)}) collective-permute-start(f32[16,128]{1,0:T(8,128)S(1)} %get-tuple-element.54.refs_7_), channel_id=1, source_target_pairs={{0,16},{4,20},{8,24},{12,28},{16,0},{20,4},{24,8},{28,12},{1,17},{... | collective-permute-start | bytes 24584 | tf_op jit(solution)/shard_map/ppermute | solution.py:369
  39.4 1.2 %copy-start.2 = (bf16[1,192,2560]{2,1,0:T(8,128)(2,1)S(1)}, bf16[1,192,2560]{2,1,0:T(8,128)(2,1)}, u32[]{:S(2)}) copy-start(bf16[1,192,2560]{2,1,0:T(8,128)(2,1)} %param.13) | copy-start | bytes 2949124
  39.4 4.7 %copy-start.1 = (bf16[64,2560]{1,0:T(8,128)(2,1)S(1)}, bf16[64,2560]{1,0:T(8,128)(2,1)}, u32[]{:S(2)}) copy-start(bf16[64,2560]{1,0:T(8,128)(2,1)} %get-tuple-element.46.refs_0_.refs_4_.refs_2_) | copy-start | bytes 983044
  39.8 4.2 %collective-permute-start.7 = (bf16[192,2560]{1,0:T(8,128)(2,1)S(1)}, bf16[192,2560]{1,0:T(8,128)(2,1)S(1)}, u32[]{:S(2)}, u32[]{:S(2)}) collective-permute-start(bf16[192,2560]{1,0:T(8,128)(2,1)S(1)} %collective-permute-done.3.refs_4_.refs_2_), channel_id=1, source_target_pairs={{0,1},{1,0},{2,3},{3,2},{4,5},{5,4},{6,7},{7,6},{8,9},{9,8},{10,11... | collective-permute-start | bytes 2949128 | tf_op jit(solution)/shard_map/ppermute | solution.py:369
  40.6 3.5 %collective-permute-start.6 = (bf16[192,2560]{1,0:T(8,128)(2,1)S(1)}, bf16[192,2560]{1,0:T(8,128)(2,1)S(1)}, u32[]{:S(2)}, u32[]{:S(2)}) collective-permute-start(bf16[192,2560]{1,0:T(8,128)(2,1)S(1)} %bitcast.15), channel_id=1, source_target_pairs={{0,1},{1,0},{2,3},{3,2},{4,5},{5,4},{6,7},{7,6},{8,9},{9,8},{10,11... | collective-permute-start | bytes 2949128 | tf_op jit(solution)/shard_map/ppermute | solution.py:369
  40.6 10.0 %collective-permute-start.10 = (bf16[64,2048]{1,0:T(8,128)(2,1)S(1)}, bf16[64,2048]{1,0:T(8,128)(2,1)S(1)}, u32[]{:S(2)}, u32[]{:S(2)}) collective-permute-start(bf16[64,2048]{1,0:T(8,128)(2,1)S(1)} %get-tuple-element.61), channel_id=1, source_target_pairs={{0,12},{4,8},{8,4},{12,0},{16,28},{20,24},{24,20},{28,16},{1,13},{... | collective-permute-start | bytes 786440 | tf_op jit(solution)/shard_map/ppermute | solution.py:369
  40.6 14.3 %collective-permute-start.8 = (bf16[64,2048]{1,0:T(8,128)(2,1)S(1)}, bf16[64,2048]{1,0:T(8,128)(2,1)S(1)}, u32[]{:S(2)}, u32[]{:S(2)}) collective-permute-start(bf16[64,2048]{1,0:T(8,128)(2,1)S(1)} %get-tuple-element.59), channel_id=1, source_target_pairs={{0,4},{4,0},{8,12},{12,8},{16,20},{20,16},{24,28},{28,24},{1,5},{5... | collective-permute-start | bytes 786440 | tf_op jit(solution)/shard_map/ppermute | solution.py:369
  42.1 13.8 %collective-permute-start.9 = (bf16[64,2048]{1,0:T(8,128)(2,1)S(1)}, bf16[64,2048]{1,0:T(8,128)(2,1)S(1)}, u32[]{:S(2)}, u32[]{:S(2)}) collective-permute-start(bf16[64,2048]{1,0:T(8,128)(2,1)S(1)} %get-tuple-element.60), channel_id=1, source_target_pairs={{0,8},{4,12},{8,0},{12,4},{16,24},{20,28},{24,16},{28,20},{1,9},{5... | collective-permute-start | bytes 786440 | tf_op jit(solution)/shard_map/ppermute | solution.py:369
  56.7 2.3 %collective-permute-start.11 = (bf16[192,1920]{1,0:T(8,128)(2,1)S(1)}, bf16[192,1920]{1,0:T(8,128)(2,1)S(1)}, u32[]{:S(2)}, u32[]{:S(2)}) collective-permute-start(bf16[192,1920]{1,0:T(8,128)(2,1)S(1)} %get-tuple-element.64), channel_id=1, source_target_pairs={{0,1},{1,0},{2,3},{3,2},{4,5},{5,4},{6,7},{7,6},{8,9},{9,8},{10,11... | collective-permute-start | bytes 2211848 | tf_op jit(solution)/shard_map/ppermute | solution.py:369
  57.9 5.6 %collective-permute-start.12 = (bf16[192,1920]{1,0:T(8,128)(2,1)S(1)}, bf16[192,1920]{1,0:T(8,128)(2,1)S(1)}, u32[]{:S(2)}, u32[]{:S(2)}) collective-permute-start(bf16[192,1920]{1,0:T(8,128)(2,1)S(1)} %get-tuple-element.66), channel_id=1, source_target_pairs={{0,1},{1,0},{2,3},{3,2},{4,5},{5,4},{6,7},{7,6},{8,9},{9,8},{10,11... | collective-permute-start | bytes 2211848 | tf_op jit(solution)/shard_map/ppermute | solution.py:369
  59.1 22.7 %collective-permute-start.16 = (bf16[192,1920]{1,0:T(8,128)(2,1)S(1)}, bf16[192,1920]{1,0:T(8,128)(2,1)S(1)}, u32[]{:S(2)}, u32[]{:S(2)}) collective-permute-start(bf16[192,1920]{1,0:T(8,128)(2,1)S(1)} %shard_map.117.refs_0_), channel_id=1, source_target_pairs={{0,2},{1,3},{2,0},{3,1},{4,6},{5,7},{6,4},{7,5},{8,10},{9,11},{10,... | collective-permute-start | bytes 2211848 | tf_op jit(solution)/shard_map/ppermute | solution.py:369
  59.9 6.0 %collective-permute-start.13 = (bf16[64,640]{1,0:T(8,128)(2,1)S(1)}, bf16[64,640]{1,0:T(8,128)(2,1)S(1)}, u32[]{:S(2)}, u32[]{:S(2)}) collective-permute-start(bf16[64,640]{1,0:T(8,128)(2,1)S(1)} %get-tuple-element.71), channel_id=1, source_target_pairs={{0,4},{4,0},{8,12},{12,8},{16,20},{20,16},{24,28},{28,24},{1,5},{5... | collective-permute-start | bytes 245768 | tf_op jit(solution)/shard_map/ppermute | solution.py:369
  60.6 5.4 %collective-permute-start.14 = (bf16[64,640]{1,0:T(8,128)(2,1)S(1)}, bf16[64,640]{1,0:T(8,128)(2,1)S(1)}, u32[]{:S(2)}, u32[]{:S(2)}) collective-permute-start(bf16[64,640]{1,0:T(8,128)(2,1)S(1)} %get-tuple-element.72), channel_id=1, source_target_pairs={{0,8},{4,12},{8,0},{12,4},{16,24},{20,28},{24,16},{28,20},{1,9},{5... | collective-permute-start | bytes 245768 | tf_op jit(solution)/shard_map/ppermute | solution.py:369
  60.8 6.3 %collective-permute-start.15 = (bf16[64,640]{1,0:T(8,128)(2,1)S(1)}, bf16[64,640]{1,0:T(8,128)(2,1)S(1)}, u32[]{:S(2)}, u32[]{:S(2)}) collective-permute-start(bf16[64,640]{1,0:T(8,128)(2,1)S(1)} %get-tuple-element.73), channel_id=1, source_target_pairs={{0,12},{4,8},{8,4},{12,0},{16,28},{20,24},{24,20},{28,16},{1,13},{... | collective-permute-start | bytes 245768 | tf_op jit(solution)/shard_map/ppermute | solution.py:369
  68.1 1.9 %collective-permute-start.17 = (bf16[192,640]{1,0:T(8,128)(2,1)S(1)}, bf16[192,640]{1,0:T(8,128)(2,1)S(1)}, u32[]{:S(2)}, u32[]{:S(2)}) collective-permute-start(bf16[192,640]{1,0:T(8,128)(2,1)S(1)} %get-tuple-element.82), channel_id=1, source_target_pairs={{0,1},{1,0},{2,3},{3,2},{4,5},{5,4},{6,7},{7,6},{8,9},{9,8},{10,11... | collective-permute-start | bytes 737288 | tf_op jit(solution)/shard_map/ppermute | solution.py:369
  68.1 1.7 %collective-permute-start.18 = (bf16[96,640]{1,0:T(8,128)(2,1)S(1)}, bf16[96,640]{1,0:T(8,128)(2,1)S(1)}, u32[]{:S(2)}, u32[]{:S(2)}) collective-permute-start(bf16[96,640]{1,0:T(8,128)(2,1)S(1)} %get-tuple-element.84), channel_id=1, source_target_pairs={{0,1},{1,0},{2,3},{3,2},{4,5},{5,4},{6,7},{7,6},{8,9},{9,8},{10,11... | collective-permute-start | bytes 368648 | tf_op jit(solution)/shard_map/ppermute | solution.py:369
  68.6 1.4 %collective-permute-start.19 = (bf16[96,640]{1,0:T(8,128)(2,1)S(1)}, bf16[96,640]{1,0:T(8,128)(2,1)S(1)}, u32[]{:S(2)}, u32[]{:S(2)}) collective-permute-start(bf16[96,640]{1,0:T(8,128)(2,1)S(1)} %get-tuple-element.85), channel_id=1, source_target_pairs={{0,1},{1,0},{2,3},{3,2},{4,5},{5,4},{6,7},{7,6},{8,9},{9,8},{10,11... | collective-permute-start | bytes 368648 | tf_op jit(solution)/shard_map/ppermute | solution.py:369
  68.7 13.1 %copy-start.5 = (s32[128,6]{0,1:T(8,128)S(1)}, s32[128,6]{0,1:T(8,128)}, u32[]{:S(2)}) copy-start(s32[128,6]{0,1:T(8,128)} %param.10) | copy-start | bytes 9220
  68.7 13.1 %copy-start.6 = (s32[128,6]{0,1:T(8,128)S(1)}, s32[128,6]{0,1:T(8,128)}, u32[]{:S(2)}) copy-start(s32[128,6]{0,1:T(8,128)} %param.11) | copy-start | bytes 9220
  68.7 13.1 %copy-start.8 = (s32[1,8]{1,0:T(1,128)S(1)}, s32[1,8]{1,0:T(1,128)}, u32[]{:S(2)}) copy-start(s32[1,8]{1,0:T(1,128)} %refs_2_.1) | copy-start | bytes 100
  70.1 13.9 %collective-permute-start.20 = (bf16[192,640]{1,0:T(8,128)(2,1)S(1)}, bf16[192,640]{1,0:T(8,128)(2,1)S(1)}, u32[]{:S(2)}, u32[]{:S(2)}) collective-permute-start(bf16[192,640]{1,0:T(8,128)(2,1)S(1)} %shard_map.124), channel_id=1, source_target_pairs={{0,2},{1,3},{2,0},{3,1},{4,6},{5,7},{6,4},{7,5},{8,10},{9,11},{10,... | collective-permute-start | bytes 737288 | tf_op jit(solution)/shard_map/ppermute | solution.py:369

commit v4 on v3

--- a/solution.py
+++ b/solution.py
@@ -22,7 +22,7 @@
 BLOCK = pl.BlockSpec()
 ANY = pl.BlockSpec(memory_space=pl.ANY)
 LANES = 128
-CODE, WEIGHT, META_ROWS = 0, 8, 16
+CODE, WEIGHT, LIVE, META_ROWS = 0, 8, 16, 24
 
 
 def call(body, outs, specs, megabytes, flops=0, moved=0, scratch=(), after=(), out_specs=None, aliases=()):
@@ -43,7 +43,7 @@
 
 
 def routing_body(
-    capacity, n_exp, choice_ref, slot_ref, combine_ref, counts_ref, tok_ref, meta_ref, *outs
+    capacity, n_exp, far, choice_ref, slot_ref, combine_ref, counts_ref, tok_ref, meta_ref, *outs
 ):
     topk = choice_ref.shape[0]
     choice = choice_ref[...]
@@ -56,7 +56,8 @@
     meta_ref[...] = jnp.zeros_like(meta_ref)
     meta_ref[CODE : CODE + topk, :] = jnp.where(kept, choice * capacity + slot, -1).astype(jnp.float32)
     meta_ref[WEIGHT : WEIGHT + topk, :] = jnp.where(live, combine_ref[...].astype(jnp.float32), 0.0)
-    select(capacity, topk, meta_ref, tok_ref[...], outs)
+    meta_ref[LIVE : LIVE + topk, :] = jnp.where(live, 1.0, 0.0)
+    select(capacity, topk, meta_ref, tok_ref[...], outs, first=far - len(outs))
 
 
 def places(target, capacity):
@@ -79,10 +80,10 @@
     return jnp.sum(weight, axis=1, keepdims=True)
 
 
-def select(capacity, topk, meta, rows, outs, own_meta=None):
+def select(capacity, topk, meta, rows, outs, own_meta=None, first=0):
     here = lax.axis_index("exp")
     columns = rows.shape[1]
-    wants = [places((here ^ m) * capacity, capacity) for m in range(len(outs))]
+    wants = [places((here ^ (first + m)) * capacity, capacity) for m in range(len(outs))]
     onehot = jnp.concatenate([pick(meta, topk, w) for w in wants], axis=0).astype(jnp.bfloat16)
     chosen = jnp.dot(onehot, rows, preferred_element_type=jnp.float32).astype(jnp.bfloat16)
     for m, out in enumerate(outs):
@@ -93,6 +94,10 @@
             out[:, columns:] = jnp.where(lane < LANES // 2, weight, own_weight).astype(jnp.bfloat16)
 
 
+def select_own_body(capacity, topk, meta_ref, tok_ref, *outs):
+    select(capacity, topk, meta_ref, tok_ref[...], outs)
+
+
 def select_first_body(capacity, topk, cut, raw_ref, meta_ref, own_meta_ref, *outs):
     select(capacity, topk, meta_ref, raw_ref[:, cut[0] : cut[1]], outs, own_meta_ref)
 
@@ -107,8 +112,8 @@
 
 
 def factors_body(
-    capacity, n_edp, gate_ref, up_ref, meta_ref,
-    hidden_ref, gate_factor_ref, up_factor_ref, turned_ref, meta_out_ref, scratch,
+    capacity, n_edp, gate_ref, up_ref, meta_ref, shard_ref,
+    hidden_ref, gate_factor_ref, up_factor_ref, turned_ref, meta_out_ref, shard_out_ref, scratch,
 ):
     data = lax.axis_index("edp")
     rows, units = gate_ref.shape
@@ -124,6 +129,7 @@
         gate_factor_ref[at, :] = up_pre * sigmoid_gate * (1.0 + gate_pre * (1.0 - sigmoid_gate))
         up_factor_ref[at, :] = silu_gate
     meta_out_ref[...] = meta_ref[...]
+    shard_out_ref[...] = shard_ref[...]
     scratch[...] = hidden_ref[...].T
     for n in range(n_edp):
         turned_ref[n] = scratch[pl.ds(pl.multiple_of((data ^ n) * shard, 64), shard), :]
@@ -153,7 +159,7 @@
     summed_out(cut, sums, out_ref, held, sem).wait()
 
 
-def returned_body(capacity, n_exp, cut, choice_ref, slot_ref, counts_ref, score_ref, far_half_ref, *refs):
+def returned_body(capacity, n_exp, cut, choice_ref, slot_ref, meta_ref, score_ref, far_half_ref, *refs):
     sums, refs = refs[:3], refs[5:]
     out_ref, weight_ref, gate_ref, up_ref, held, held_weight, sems, half_sems = refs
     far = n_exp // 2
@@ -164,10 +170,7 @@
     topk, tokens = choice_ref.shape
     choice = choice_ref[...]
     slot = slot_ref[...]
-    limit = jnp.zeros_like(slot)
-    for expert in range(n_exp):
-        limit = jnp.where(choice == expert, counts_ref[0, expert], limit)
-    live = (slot < capacity) & (slot < limit)
+    live = meta_ref[LIVE : LIVE + topk, :] > 0.0
     table = score_ref[...]
     high = table.astype(jnp.bfloat16)
     rest = table - high.astype(jnp.float32)
@@ -372,16 +375,16 @@
         return [found[0]] + [hop(found[m], "exp", m) for m in range(1, far)]
 
     meta, *found = call(
-        functools.partial(routing_body, capacity, n_exp),
-        [shape(META_ROWS, LANES, dtype=f32)] + [shape(capacity, width)] * far,
+        functools.partial(routing_body, capacity, n_exp, far),
+        [shape(META_ROWS, LANES, dtype=f32)] + [shape(capacity, width)] * (far // 2),
         [BLOCK, BLOCK, BLOCK, SMEM, BLOCK],
         56,
         flops=2 * far * capacity * tok_rows * width,
         moved=out_grad.size * 4,
     )(token_expert_choice.T, slots.T, combine.T, counts, out_grad)
     raw = hop(out_grad, "exp", far)
-    own = spread(found)
-    hidden, gate_factor, up_factor, turned, meta = call(
+    own = [hop(x, "exp", far // 2 + m) for m, x in enumerate(found)]
+    hidden, gate_factor, up_factor, turned, meta, weight_here = call(
         functools.partial(factors_body, capacity, n_edp),
         [
             shape(rows, units),
@@ -389,16 +392,25 @@
             shape(rows, units, dtype=f32),
             shape(n_edp, shard, rows),
             shape(META_ROWS, LANES, dtype=f32),
+            shape(shard, width),
         ],
-        [VMEM] * 3,
+        [VMEM] * 4,
         24,
         flops=40 * rows * units,
         moved=16 * rows * units,
         scratch=[pltpu.VMEM((units, rows), bf16)],
-        after=[own[0]],
-    )(stored_gate_preact[0, 0], stored_up_preact[0, 0], meta)
+    )(stored_gate_preact[0, 0], stored_up_preact[0, 0], meta, down_weight[0])
     weight_y = hop(down_weight[0], "edp", 2)
-    far_meta = hop(meta, "exp", far, own[1])
+    far_meta = hop(meta, "exp", far, own[0])
+
+    found = call(
+        functools.partial(select_own_body, capacity, topk),
+        [shape(capacity, width)] * (far // 2),
+        [VMEM] * 2,
+        16,
+        after=[hidden],
+    )(meta, out_grad)
+    own = [found[0]] + [hop(found[m], "exp", m) for m in range(1, far // 2)] + own
 
     def term(k, others, scales, after=()):
         return call(
@@ -433,14 +445,14 @@
         after=[*own[1:], hidden, weight_y],
     )(raw, far_meta, meta)
     far0 = spread(found)
-    weight_core = hop(down_weight[0], "edp", 1, found[0])
+    weight_core = hop(weight_here, "edp", 1, own[far - 1])
     weight_both = hop(weight_y, "edp", 1, found[0])
     weight, own_proj = call(
         functools.partial(project_own_body, far),
         [shape(units, width), shape(far * capacity, units, dtype=f32)],
         [VMEM] * (4 + far),
         32,
-    )(down_weight[0], weight_core, weight_y, weight_both, *own)
+    )(weight_here, weight_core, weight_y, weight_both, *own)
     first0, weighted = call(
         functools.partial(first_term_body, far, cuts[0], 640),
         [shape(shard, sizes[0]), shape(rows, sizes[0])],
@@ -500,7 +512,7 @@
     down_matrix_gradient, combine_weight_gradient, gate_preact_gradient, up_preact_gradient = call(
         functools.partial(returned_body, capacity, n_exp, cuts[0]),
         [shape(shard, width), shape(topk, tok_rows, dtype=f32), shape(rows, units), shape(rows, units)],
-        [VMEM, VMEM, SMEM] + [VMEM] * 5 + [ANY] * 2,
+        [VMEM] * 8 + [ANY] * 2,
         16,
         scratch=[
             pltpu.VMEM((shard, sizes[0]), bf16),
@@ -511,7 +523,7 @@
         out_specs=[ANY] * 4,
         aliases=[(8, 2), (9, 3)],
     )(
-        token_expert_choice.T, slots.T, counts, returned, far_half, keep0, core0, from_y0,
+        token_expert_choice.T, slots.T, meta, returned, far_half, keep0, core0, from_y0,
         gate_preact_gradient, up_preact_gradient,
     )
     (down_matrix_gradient,) = call(

time: 85.1 us -> 83.2 us (0.978)
  waiting for transfers between devices: 34.8 us -> 30.5 us
  starting transfers between devices: 19.7 us -> 22.4 us
    ppermute x21, waiting for transfers between devices: 34.8 us -> 30.5 us  [hop(): return lax.ppermute(x, axis, flip(lax.axis_size(axis), mask))]
    ppermute x21, starting transfers between devices: 19.7 us -> 22.4 us  [hop(): return lax.ppermute(x, axis, flip(lax.axis_size(axis), mask))]
    unnamed x18 -> x14, local copies, waits for them, and re-layouts: 4.62 us -> 4.18 us
    pallas_call x1 -> x2, Pallas kernels: 2.68 us -> 2.71 us  [the longest x1 2.38 us: relayed(): call(functools.partial(routing_body, capacity, n_exp, far), [shape(META_R...]
  transfers between devices with their start and end apart: 21 -> 21, of which waited for: 10 -> 9; matrix products, arithmetic and copies ran while one was open for 0% -> 0% of each run, Pallas kernels for 15% -> 15%
where the time goes in v4:
time: 83.2 us; the launch traced here: 82.8 us
  waiting for transfers between devices  30.5 us (37%)
  starting transfers between devices  22.4 us (27%)
  Pallas kernels  14.2 us (17%)
  blocking collectives  10.8 us (13%)
  local copies, waits for them, and re-layouts  4.18 us (5%)
    ppermute x21, waiting for transfers between devices, hop(): return lax.ppermute(x, axis, flip(lax.axis_size(axis), mask))  30.5 us
    ppermute x21, starting transfers between devices, hop(): return lax.ppermute(x, axis, flip(lax.axis_size(axis), mask))  22.4 us
    all_to_all x1, blocking collectives, relayed(): returned = lax.all_to_all(score, 'exp', split_axis=0, concat_axis=0)  10.8 us
    unnamed x14, local copies, waits for them, and re-layouts  4.18 us
    pallas_call x1, Pallas kernels, relayed(): call(functools.partial(routing_body, capacity, n_exp, far), [shape(META_R...  2.38 us
    pallas_call x1, Pallas kernels, relayed(): call(functools.partial(project_far_body, far, cuts[0]), [shape(far * capa...  1.82 us
    pallas_call x2, Pallas kernels, more_terms(): call(functools.partial(more_terms_body, 640, shards), outs, [VMEM] * 2, 2...  1.72 us
  transfers between devices with their start and end apart: 21, of which 9 were waited for; matrix products, arithmetic and copies ran while one was open for 0% of the time, Pallas kernels for 15%

profile of v4, /device:TPU:0, one launch (start us, length us, event | category | flops | bytes accessed | tf_op | source)
XLA Modules:
  0.0 82.8 jit_solution(14043710499284792823)
XLA Ops:
  0.6 3.0 %collective-permute-start.2 = (bf16[192,2560]{1,0:T(8,128)(2,1)}, bf16[192,2560]{1,0:T(8,128)(2,1)S(1)}, u32[]{:S(2)}, u32[]{:S(2)}) collective-permute-start(bf16[192,2560]{1,0:T(8,128)(2,1)} %bitcast.14), channel_id=1, source_target_pairs={{0,2},{1,3},{2,0},{3,1},{4,6},{5,7},{6,4},{7,5},{8,10},{9,11},{10,... | collective-permute-start | bytes 2949128 | tf_op jit(solution)/shard_map/ppermute | solution.py:372
  3.7 2.6 %collective-permute-start.5 = (bf16[128,2560]{1,0:T(8,128)(2,1)}, bf16[128,2560]{1,0:T(8,128)(2,1)S(1)}, u32[]{:S(2)}, u32[]{:S(2)}) collective-permute-start(bf16[128,2560]{1,0:T(8,128)(2,1)} %refs_2_.1), channel_id=1, source_target_pairs={{0,16},{4,20},{8,24},{12,28},{16,0},{20,4},{24,8},{28,12},{1,17},{... | collective-permute-start | bytes 1966088 | tf_op jit(solution)/shard_map/ppermute | solution.py:372
  6.3 2.4 %shard_map.111 = (f32[24,128]{1,0:T(8,128)}, bf16[64,2560]{1,0:T(8,128)(2,1)}, bf16[64,2560]{1,0:T(8,128)(2,1)}) custom-call(s32[6,128]{1,0:T(8,128)} %bitcast.19, s32[6,128]{1,0:T(8,128)} %bitcast.21, bf16[6,128]{1,0:T(8,128)(2,1)} %bitcast.27, s32[1,8]{1,0:T(1,128)} %refs_3_.1, bf16[128,2560]{1,0:T(8,128)(2,1)} %refs_2_.1), custom_call_target="tpu_custom_call" | custom-call | flops 167772160 | bytes 1310720 | tf_op jit(solution)/shard_map/pallas_call | solution.py:377
  8.6 1.6 %collective-permute-start.4 = (bf16[64,2560]{1,0:T(8,128)(2,1)}, bf16[64,2560]{1,0:T(8,128)(2,1)S(1)}, u32[]{:S(2)}, u32[]{:S(2)}) collective-permute-start(bf16[64,2560]{1,0:T(8,128)(2,1)} %get-tuple-element.55), channel_id=1, source_target_pairs={{0,8},{4,12},{8,0},{12,4},{16,24},{20,28},{24,16},{28,20},{1,9},{5... | collective-permute-start | bytes 983048 | tf_op jit(solution)/shard_map/ppermute | solution.py:372
  10.2 1.4 %collective-permute-start = (bf16[64,2560]{1,0:T(8,128)(2,1)}, bf16[64,2560]{1,0:T(8,128)(2,1)S(1)}, u32[]{:S(2)}, u32[]{:S(2)}) collective-permute-start(bf16[64,2560]{1,0:T(8,128)(2,1)} %get-tuple-element.51), channel_id=1, source_target_pairs={{0,12},{4,8},{8,4},{12,0},{16,28},{20,24},{24,20},{28,16},{1,13},{... | collective-permute-start | bytes 983048 | tf_op jit(solution)/shard_map/ppermute | solution.py:372
  11.6 1.2 %copy-done.1 = bf16[1,192,2560]{2,1,0:T(8,128)(2,1)S(1)} copy-done((bf16[1,192,2560]{2,1,0:T(8,128)(2,1)S(1)}, bf16[1,192,2560]{2,1,0:T(8,128)(2,1)}, u32[]{:S(2)}) %copy-start.1) | copy-done | bytes 983064
  12.8 1.1 %copy-done.2 = bf16[1,1,512,768]{3,2,1,0:T(8,128)(2,1)S(1)} copy-done((bf16[1,1,512,768]{3,2,1,0:T(8,128)(2,1)S(1)}, bf16[1,1,512,768]{3,2,1,0:T(8,128)(2,1)}, u32[]{:S(2)}) %copy-start.2) | copy-done | bytes 786456
  13.9 1.1 %copy-done.3 = bf16[1,1,512,768]{3,2,1,0:T(8,128)(2,1)S(1)} copy-done((bf16[1,1,512,768]{3,2,1,0:T(8,128)(2,1)S(1)}, bf16[1,1,512,768]{3,2,1,0:T(8,128)(2,1)}, u32[]{:S(2)}) %copy-start.3) | copy-done | bytes 786456
  15.1 0.7 copy-done.6
  15.8 0.8 shard_map.112
  16.6 0.0 copy-done
  16.6 0.3 shard_map.113
  16.9 0.6 collective-permute-start.3
  17.5 11.3 %collective-permute-done.4.refs_1_.refs_6_.refs_4_ = bf16[64,2560]{1,0:T(8,128)(2,1)S(1)} collective-permute-done((bf16[64,2560]{1,0:T(8,128)(2,1)}, bf16[64,2560]{1,0:T(8,128)(2,1)S(1)}, u32[]{:S(2)}, u32[]{:S(2)}) %collective-permute-start.4) | collective-permute-done | bytes 327712 | tf_op jit(solution)/shard_map/ppermute | solution.py:372
  28.8 2.2 %collective-permute-start.6 = (f32[24,128]{1,0:T(8,128)S(1)}, f32[24,128]{1,0:T(8,128)S(1)}, u32[]{:S(2)}, u32[]{:S(2)}) collective-permute-start(f32[24,128]{1,0:T(8,128)S(1)} %get-tuple-element.56.refs_1_.refs_7_.refs_2_), channel_id=1, source_target_pairs={{0,16},{4,20},{8,24},{12,28},{16,0},{20,4},{24,8},{28,12},{1,17},{... | collective-permute-start | bytes 36872 | tf_op jit(solution)/shard_map/ppermute | solution.py:372
  31.0 7.9 %collective-permute-done.refs_2_.refs_7_.refs_5_ = bf16[64,2560]{1,0:T(8,128)(2,1)S(1)} collective-permute-done((bf16[64,2560]{1,0:T(8,128)(2,1)}, bf16[64,2560]{1,0:T(8,128)(2,1)S(1)}, u32[]{:S(2)}, u32[]{:S(2)}) %collective-permute-start) | collective-permute-done | bytes 327712 | tf_op jit(solution)/shard_map/ppermute | solution.py:372
  38.9 0.0 collective-permute-start.1
  38.9 0.0 collective-permute-done.3.refs_0_.refs_5_.refs_3_
  38.9 0.0 collective-permute-done.6.refs_6_.refs_2_
  38.9 0.0 collective-permute-done.5.refs_5_.refs_1_
  38.9 0.0 collective-permute-done.2.refs_4_.refs_2_
  39.0 0.4 shard_map.114
  39.4 0.6 collective-permute-start.7
  40.0 0.0 collective-permute-start.10
  40.0 0.5 collective-permute-start.8
  40.5 3.0 %collective-permute-start.9 = (bf16[64,2048]{1,0:T(8,128)(2,1)S(1)}, bf16[64,2048]{1,0:T(8,128)(2,1)S(1)}, u32[]{:S(2)}, u32[]{:S(2)}) collective-permute-start(bf16[64,2048]{1,0:T(8,128)(2,1)S(1)} %get-tuple-element.62), channel_id=1, source_target_pairs={{0,8},{4,12},{8,0},{12,4},{16,24},{20,28},{24,16},{28,20},{1,9},{5... | collective-permute-start | bytes 786440 | tf_op jit(solution)/shard_map/ppermute | solution.py:372
  43.4 0.0 collective-permute-done.1.refs_1_
  43.4 0.0 collective-permute-done.7.refs_3_
  43.4 1.5 %shard_map.115 = (bf16[768,2560]{1,0:T(8,128)(2,1)S(1)}, f32[256,768]{1,0:T(8,128)S(1)}) custom-call(bf16[192,2560]{1,0:T(8,128)(2,1)S(1)} %get-tuple-element.52.refs_0_, bf16[192,2560]{1,0:T(8,128)(2,1)S(1)} %collective-permute-done.1.refs_1_, bf16[192,2560]{1,0:T(8,128)(2,1)S(1)} %collective-permute-done.2.refs_4_.refs_2_, ...), custom_call_target="tpu_custom_call" | custom-call | tf_op jit(solution)/shard_map/pallas_call | solution.py:450
  44.9 5.1 %collective-permute-done.10.refs_9_.refs_6_.refs_13_.refs_8_ = bf16[64,2048]{1,0:T(8,128)(2,1)S(1)} collective-permute-done((bf16[64,2048]{1,0:T(8,128)(2,1)S(1)}, bf16[64,2048]{1,0:T(8,128)(2,1)S(1)}, u32[]{:S(2)}, u32[]{:S(2)}) %collective-permute-start.10) | collective-permute-done | bytes 262176 | tf_op jit(solution)/shard_map/ppermute | solution.py:372
  50.1 3.9 %collective-permute-done.8.refs_7_.refs_4_.refs_11_.refs_6_ = bf16[64,2048]{1,0:T(8,128)(2,1)S(1)} collective-permute-done((bf16[64,2048]{1,0:T(8,128)(2,1)S(1)}, bf16[64,2048]{1,0:T(8,128)(2,1)S(1)}, u32[]{:S(2)}, u32[]{:S(2)}) %collective-permute-start.8) | collective-permute-done | bytes 262176 | tf_op jit(solution)/shard_map/ppermute | solution.py:372
  53.9 0.0 collective-permute-done.9.refs_8_.refs_5_.refs_12_.refs_7_
  53.9 0.8 %shard_map.116 = (bf16[192,1920]{1,0:T(8,128)(2,1)S(1)}, bf16[512,1920]{1,0:T(8,128)(2,1)S(1)}) custom-call(f32[256,768]{1,0:T(8,128)S(1)} %get-tuple-element.60.refs_0_.refs_8_, bf16[4,192,512]{2,1,0:T(8,128)(2,1)S(1)} %get-tuple-element.49.refs_1_.refs_0_, bf16[64,2560]{1,0:T(8,128)(2,1)S(1)} %get-tuple-element.59.refs_4_.refs_2_, ...), custom_call_target="tpu_custom_call" | custom-call | tf_op jit(solution)/shard_map/pallas_call | solution.py:456
  54.8 0.1 collective-permute-start.11
  54.9 1.1 %shard_map.117 = (f32[192,1920]{1,0:T(8,128)S(1)}, bf16[192,1920]{1,0:T(8,128)(2,1)S(1)}) custom-call(bf16[4,192,512]{2,1,0:T(8,128)(2,1)S(1)} %get-tuple-element.49.refs_1_.refs_0_, bf16[512,1920]{1,0:T(8,128)(2,1)S(1)} %get-tuple-element.64.refs_1_.refs_2_), custom_call_target="tpu_custom_call" | custom-call | tf_op jit(solution)/shard_map/pallas_call | solution.py:465
  56.0 0.6 collective-permute-start.12
  56.5 0.5 collective-permute-done.11.refs_1_
  57.1 0.1 shard_map.118.refs_0_
  57.2 0.6 collective-permute-start.16
  57.8 0.3 shard_map.119
  58.0 1.5 %collective-permute-start.13 = (bf16[64,640]{1,0:T(8,128)(2,1)S(1)}, bf16[64,640]{1,0:T(8,128)(2,1)S(1)}, u32[]{:S(2)}, u32[]{:S(2)}) collective-permute-start(bf16[64,640]{1,0:T(8,128)(2,1)S(1)} %get-tuple-element.73), channel_id=1, source_target_pairs={{0,4},{4,0},{8,12},{12,8},{16,20},{20,16},{24,28},{28,24},{1,5},{5... | collective-permute-start | bytes 245768 | tf_op jit(solution)/shard_map/ppermute | solution.py:372
  59.5 0.2 collective-permute-start.14
  59.7 1.8 %collective-permute-start.15 = (bf16[64,640]{1,0:T(8,128)(2,1)S(1)}, bf16[64,640]{1,0:T(8,128)(2,1)S(1)}, u32[]{:S(2)}, u32[]{:S(2)}) collective-permute-start(bf16[64,640]{1,0:T(8,128)(2,1)S(1)} %get-tuple-element.75), channel_id=1, source_target_pairs={{0,12},{4,8},{8,4},{12,0},{16,28},{20,24},{24,20},{28,16},{1,13},{... | collective-permute-start | bytes 245768 | tf_op jit(solution)/shard_map/ppermute | solution.py:372
  61.6 0.0 collective-permute-done.12.refs_2_.refs_6_
  61.6 1.8 %shard_map.120 = (f32[256,768]{1,0:T(8,128)S(1)}, bf16[512,768]{1,0:T(8,128)(2,1)}, bf16[512,768]{1,0:T(8,128)(2,1)}, f32[2,128]{1,0:T(2,128)S(1)}) custom-call(bf16[192,1920]{1,0:T(8,128)(2,1)S(1)} %shard_map.118.refs_0_, bf16[64,640]{1,0:T(8,128)(2,1)S(1)} %get-tuple-element.67.refs_1_.refs_6_, ...), custom_call_target="tpu_custom_call" | custom-call | tf_op jit(solution)/shard_map/pallas_call | solution.py:486
  63.4 0.6 shard_map.121.refs_0_.refs_5_
  64.0 0.0 collective-permute-done.13.refs_7_.refs_2_
  64.0 0.3 collective-permute-done.14.refs_8_.refs_3_
  64.3 0.9 %collective-permute-done.15.refs_9_.refs_4_ = bf16[64,640]{1,0:T(8,128)(2,1)S(1)} collective-permute-done((bf16[64,640]{1,0:T(8,128)(2,1)S(1)}, bf16[64,640]{1,0:T(8,128)(2,1)S(1)}, u32[]{:S(2)}, u32[]{:S(2)}) %collective-permute-start.15) | collective-permute-done | bytes 81952 | tf_op jit(solution)/shard_map/ppermute | solution.py:372
  65.2 0.9 %shard_map.122 = (f32[192,640]{1,0:T(8,128)S(1)}, f32[192,640]{1,0:T(8,128)S(1)}, bf16[192,640]{1,0:T(8,128)(2,1)S(1)}, bf16[96,640]{1,0:T(8,128)(2,1)S(1)}, bf16[96,640]{1,0:T(8,128)(2,1)S(1)}) custom-call(f32[192,1920]{1,0:T(8,128)S(1)} %shard_map.121.refs_0_.refs_5_, bf16[4,192,512]{2,1,0:T(8,128)(2,1)S(1)} %get-tuple-element.49.refs_1_.refs_0_, ...), custom_call_target="tpu_custom_call" | custom-call | flops 503316480 | bytes 3276800 | tf_op jit(solution)/shard_map/pallas_call | solution.py:416
  66.2 0.1 collective-permute-start.17
  66.2 0.5 collective-permute-start.18
  66.7 0.1 collective-permute-start.19
  66.8 0.7 shard_map.123
  67.6 0.4 collective-permute-done.18.refs_3_
  67.9 0.2 collective-permute-done.19.refs_4_
  68.1 0.0 collective-permute-done.17.refs_1_
  68.1 0.1 shard_map.125
  68.1 1.6 %collective-permute-start.20 = (bf16[192,640]{1,0:T(8,128)(2,1)S(1)}, bf16[192,640]{1,0:T(8,128)(2,1)S(1)}, u32[]{:S(2)}, u32[]{:S(2)}) collective-permute-start(bf16[192,640]{1,0:T(8,128)(2,1)S(1)} %shard_map.125), channel_id=1, source_target_pairs={{0,2},{1,3},{2,0},{3,1},{4,6},{5,7},{6,4},{7,5},{8,10},{9,11},{10,... | collective-permute-start | bytes 737288 | tf_op jit(solution)/shard_map/ppermute | solution.py:372
  69.7 10.8 %all_to_all.11 = f32[8,1,64]{2,1,0:T(1,128)S(1)} all-to-all(f32[8,1,64]{2,1,0:T(1,128)S(1)} %bitcast.18), channel_id=1, replica_groups=mesh['exp'=8,'edp'=4] {'exp'}, dimensions={0} | all-to-all | bytes 4096 | tf_op jit(solution)/shard_map/all_to_all | solution.py:511
  80.5 0.0 collective-permute-done.16.refs_7_
  80.5 1.5 %shard_map.124 = (bf16[192,2560]{1,0:T(8,128)(2,1)}, f32[6,128]{1,0:T(8,128)}, bf16[512,768]{1,0:T(8,128)(2,1)}, bf16[512,768]{1,0:T(8,128)(2,1)}) custom-call(s32[6,128]{1,0:T(8,128)S(1)} %bitcast.20, s32[6,128]{1,0:T(8,128)S(1)} %bitcast.22, f32[24,128]{1,0:T(8,128)S(1)} %get-tuple-element.56.refs_1_.refs_7_.refs_2_, ...), custom_call_target="tpu_custom_call", output_to_operand_aliasing={{2}: (8, {}), {3}: (9, {})} | custom-call | tf_op jit(solution)/shard_map/pallas_call | solution.py:512
  82.0 0.0 collective-permute-done.20.refs_2_
  82.1 0.8 shard_map.126
  (9 shorter events, 0.0 us)
Async XLA Ops:
  0.6 38.3 %collective-permute-start.2 = (bf16[192,2560]{1,0:T(8,128)(2,1)}, bf16[192,2560]{1,0:T(8,128)(2,1)S(1)}, u32[]{:S(2)}, u32[]{:S(2)}) collective-permute-start(bf16[192,2560]{1,0:T(8,128)(2,1)} %bitcast.14), channel_id=1, source_target_pairs={{0,2},{1,3},{2,0},{3,1},{4,6},{5,7},{6,4},{7,5},{8,10},{9,11},{10,... | collective-permute-start | bytes 2949128 | tf_op jit(solution)/shard_map/ppermute | solution.py:372
  3.7 35.3 %collective-permute-start.5 = (bf16[128,2560]{1,0:T(8,128)(2,1)}, bf16[128,2560]{1,0:T(8,128)(2,1)S(1)}, u32[]{:S(2)}, u32[]{:S(2)}) collective-permute-start(bf16[128,2560]{1,0:T(8,128)(2,1)} %refs_2_.1), channel_id=1, source_target_pairs={{0,16},{4,20},{8,24},{12,28},{16,0},{20,4},{24,8},{28,12},{1,17},{... | collective-permute-start | bytes 1966088 | tf_op jit(solution)/shard_map/ppermute | solution.py:372
  6.3 10.3 %copy-start = (bf16[128,2560]{1,0:T(8,128)(2,1)S(1)}, bf16[128,2560]{1,0:T(8,128)(2,1)}, u32[]{:S(2)}) copy-start(bf16[128,2560]{1,0:T(8,128)(2,1)} %refs_2_.1) | copy-start | bytes 1966084
  8.6 20.2 %collective-permute-start.4 = (bf16[64,2560]{1,0:T(8,128)(2,1)}, bf16[64,2560]{1,0:T(8,128)(2,1)S(1)}, u32[]{:S(2)}, u32[]{:S(2)}) collective-permute-start(bf16[64,2560]{1,0:T(8,128)(2,1)} %get-tuple-element.55), channel_id=1, source_target_pairs={{0,8},{4,12},{8,0},{12,4},{16,24},{20,28},{24,16},{28,20},{1,9},{5... | collective-permute-start | bytes 983048 | tf_op jit(solution)/shard_map/ppermute | solution.py:372
  10.2 28.7 %collective-permute-start = (bf16[64,2560]{1,0:T(8,128)(2,1)}, bf16[64,2560]{1,0:T(8,128)(2,1)S(1)}, u32[]{:S(2)}, u32[]{:S(2)}) collective-permute-start(bf16[64,2560]{1,0:T(8,128)(2,1)} %get-tuple-element.51), channel_id=1, source_target_pairs={{0,12},{4,8},{8,4},{12,0},{16,28},{20,24},{24,20},{28,16},{1,13},{... | collective-permute-start | bytes 983048 | tf_op jit(solution)/shard_map/ppermute | solution.py:372
  11.6 1.2 %copy-start.1 = (bf16[1,192,2560]{2,1,0:T(8,128)(2,1)S(1)}, bf16[1,192,2560]{2,1,0:T(8,128)(2,1)}, u32[]{:S(2)}) copy-start(bf16[1,192,2560]{2,1,0:T(8,128)(2,1)} %param.13) | copy-start | bytes 2949124
  12.8 1.1 %copy-start.2 = (bf16[1,1,512,768]{3,2,1,0:T(8,128)(2,1)S(1)}, bf16[1,1,512,768]{3,2,1,0:T(8,128)(2,1)}, u32[]{:S(2)}) copy-start(bf16[1,1,512,768]{3,2,1,0:T(8,128)(2,1)} %param.14) | copy-start | bytes 2359300
  13.9 1.1 %copy-start.3 = (bf16[1,1,512,768]{3,2,1,0:T(8,128)(2,1)S(1)}, bf16[1,1,512,768]{3,2,1,0:T(8,128)(2,1)}, u32[]{:S(2)}) copy-start(bf16[1,1,512,768]{3,2,1,0:T(8,128)(2,1)} %param.15) | copy-start | bytes 2359300
  15.1 0.7 copy-start.6
  16.9 22.0 %collective-permute-start.3 = (bf16[64,2560]{1,0:T(8,128)(2,1)S(1)}, bf16[64,2560]{1,0:T(8,128)(2,1)S(1)}, u32[]{:S(2)}, u32[]{:S(2)}) collective-permute-start(bf16[64,2560]{1,0:T(8,128)(2,1)S(1)} %get-tuple-element.54), channel_id=1, source_target_pairs={{0,4},{4,0},{8,12},{12,8},{16,20},{20,16},{24,28},{28,24},{1,5},{5... | collective-permute-start | bytes 983048 | tf_op jit(solution)/shard_map/ppermute | solution.py:372
  28.8 10.1 %collective-permute-start.6 = (f32[24,128]{1,0:T(8,128)S(1)}, f32[24,128]{1,0:T(8,128)S(1)}, u32[]{:S(2)}, u32[]{:S(2)}) collective-permute-start(f32[24,128]{1,0:T(8,128)S(1)} %get-tuple-element.56.refs_1_.refs_7_.refs_2_), channel_id=1, source_target_pairs={{0,16},{4,20},{8,24},{12,28},{16,0},{20,4},{24,8},{28,12},{1,17},{... | collective-permute-start | bytes 36872 | tf_op jit(solution)/shard_map/ppermute | solution.py:372
  38.9 4.5 %collective-permute-start.1 = (bf16[192,2560]{1,0:T(8,128)(2,1)S(1)}, bf16[192,2560]{1,0:T(8,128)(2,1)S(1)}, u32[]{:S(2)}, u32[]{:S(2)}) collective-permute-start(bf16[192,2560]{1,0:T(8,128)(2,1)S(1)} %get-tuple-element.52.refs_0_), channel_id=1, source_target_pairs={{0,1},{1,0},{2,3},{3,2},{4,5},{5,4},{6,7},{7,6},{8,9},{9,8},{10,11... | collective-permute-start | bytes 2949128 | tf_op jit(solution)/shard_map/ppermute | solution.py:372
  39.4 4.1 %collective-permute-start.7 = (bf16[192,2560]{1,0:T(8,128)(2,1)S(1)}, bf16[192,2560]{1,0:T(8,128)(2,1)S(1)}, u32[]{:S(2)}, u32[]{:S(2)}) collective-permute-start(bf16[192,2560]{1,0:T(8,128)(2,1)S(1)} %collective-permute-done.2.refs_4_.refs_2_), channel_id=1, source_target_pairs={{0,1},{1,0},{2,3},{3,2},{4,5},{5,4},{6,7},{7,6},{8,9},{9,8},{10,11... | collective-permute-start | bytes 2949128 | tf_op jit(solution)/shard_map/ppermute | solution.py:372
  40.0 10.1 %collective-permute-start.10 = (bf16[64,2048]{1,0:T(8,128)(2,1)S(1)}, bf16[64,2048]{1,0:T(8,128)(2,1)S(1)}, u32[]{:S(2)}, u32[]{:S(2)}) collective-permute-start(bf16[64,2048]{1,0:T(8,128)(2,1)S(1)} %get-tuple-element.63), channel_id=1, source_target_pairs={{0,12},{4,8},{8,4},{12,0},{16,28},{20,24},{24,20},{28,16},{1,13},{... | collective-permute-start | bytes 786440 | tf_op jit(solution)/shard_map/ppermute | solution.py:372
  40.0 14.0 %collective-permute-start.8 = (bf16[64,2048]{1,0:T(8,128)(2,1)S(1)}, bf16[64,2048]{1,0:T(8,128)(2,1)S(1)}, u32[]{:S(2)}, u32[]{:S(2)}) collective-permute-start(bf16[64,2048]{1,0:T(8,128)(2,1)S(1)} %get-tuple-element.61), channel_id=1, source_target_pairs={{0,4},{4,0},{8,12},{12,8},{16,20},{20,16},{24,28},{28,24},{1,5},{5... | collective-permute-start | bytes 786440 | tf_op jit(solution)/shard_map/ppermute | solution.py:372
  40.5 13.5 %collective-permute-start.9 = (bf16[64,2048]{1,0:T(8,128)(2,1)S(1)}, bf16[64,2048]{1,0:T(8,128)(2,1)S(1)}, u32[]{:S(2)}, u32[]{:S(2)}) collective-permute-start(bf16[64,2048]{1,0:T(8,128)(2,1)S(1)} %get-tuple-element.62), channel_id=1, source_target_pairs={{0,8},{4,12},{8,0},{12,4},{16,24},{20,28},{24,16},{28,20},{1,9},{5... | collective-permute-start | bytes 786440 | tf_op jit(solution)/shard_map/ppermute | solution.py:372
  54.8 2.3 %collective-permute-start.11 = (bf16[192,1920]{1,0:T(8,128)(2,1)S(1)}, bf16[192,1920]{1,0:T(8,128)(2,1)S(1)}, u32[]{:S(2)}, u32[]{:S(2)}) collective-permute-start(bf16[192,1920]{1,0:T(8,128)(2,1)S(1)} %get-tuple-element.66), channel_id=1, source_target_pairs={{0,1},{1,0},{2,3},{3,2},{4,5},{5,4},{6,7},{7,6},{8,9},{9,8},{10,11... | collective-permute-start | bytes 2211848 | tf_op jit(solution)/shard_map/ppermute | solution.py:372
  56.0 5.6 %collective-permute-start.12 = (bf16[192,1920]{1,0:T(8,128)(2,1)S(1)}, bf16[192,1920]{1,0:T(8,128)(2,1)S(1)}, u32[]{:S(2)}, u32[]{:S(2)}) collective-permute-start(bf16[192,1920]{1,0:T(8,128)(2,1)S(1)} %get-tuple-element.68), channel_id=1, source_target_pairs={{0,1},{1,0},{2,3},{3,2},{4,5},{5,4},{6,7},{7,6},{8,9},{9,8},{10,11... | collective-permute-start | bytes 2211848 | tf_op jit(solution)/shard_map/ppermute | solution.py:372
  57.2 23.3 %collective-permute-start.16 = (bf16[192,1920]{1,0:T(8,128)(2,1)S(1)}, bf16[192,1920]{1,0:T(8,128)(2,1)S(1)}, u32[]{:S(2)}, u32[]{:S(2)}) collective-permute-start(bf16[192,1920]{1,0:T(8,128)(2,1)S(1)} %shard_map.118.refs_0_), channel_id=1, source_target_pairs={{0,2},{1,3},{2,0},{3,1},{4,6},{5,7},{6,4},{7,5},{8,10},{9,11},{10,... | collective-permute-start | bytes 2211848 | tf_op jit(solution)/shard_map/ppermute | solution.py:372
  58.0 6.0 %collective-permute-start.13 = (bf16[64,640]{1,0:T(8,128)(2,1)S(1)}, bf16[64,640]{1,0:T(8,128)(2,1)S(1)}, u32[]{:S(2)}, u32[]{:S(2)}) collective-permute-start(bf16[64,640]{1,0:T(8,128)(2,1)S(1)} %get-tuple-element.73), channel_id=1, source_target_pairs={{0,4},{4,0},{8,12},{12,8},{16,20},{20,16},{24,28},{28,24},{1,5},{5... | collective-permute-start | bytes 245768 | tf_op jit(solution)/shard_map/ppermute | solution.py:372
  59.5 4.8 %collective-permute-start.14 = (bf16[64,640]{1,0:T(8,128)(2,1)S(1)}, bf16[64,640]{1,0:T(8,128)(2,1)S(1)}, u32[]{:S(2)}, u32[]{:S(2)}) collective-permute-start(bf16[64,640]{1,0:T(8,128)(2,1)S(1)} %get-tuple-element.74), channel_id=1, source_target_pairs={{0,8},{4,12},{8,0},{12,4},{16,24},{20,28},{24,16},{28,20},{1,9},{5... | collective-permute-start | bytes 245768 | tf_op jit(solution)/shard_map/ppermute | solution.py:372
  59.7 5.5 %collective-permute-start.15 = (bf16[64,640]{1,0:T(8,128)(2,1)S(1)}, bf16[64,640]{1,0:T(8,128)(2,1)S(1)}, u32[]{:S(2)}, u32[]{:S(2)}) collective-permute-start(bf16[64,640]{1,0:T(8,128)(2,1)S(1)} %get-tuple-element.75), channel_id=1, source_target_pairs={{0,12},{4,8},{8,4},{12,0},{16,28},{20,24},{24,20},{28,16},{1,13},{... | collective-permute-start | bytes 245768 | tf_op jit(solution)/shard_map/ppermute | solution.py:372
  66.2 1.9 %collective-permute-start.17 = (bf16[192,640]{1,0:T(8,128)(2,1)S(1)}, bf16[192,640]{1,0:T(8,128)(2,1)S(1)}, u32[]{:S(2)}, u32[]{:S(2)}) collective-permute-start(bf16[192,640]{1,0:T(8,128)(2,1)S(1)} %get-tuple-element.84), channel_id=1, source_target_pairs={{0,1},{1,0},{2,3},{3,2},{4,5},{5,4},{6,7},{7,6},{8,9},{9,8},{10,11... | collective-permute-start | bytes 737288 | tf_op jit(solution)/shard_map/ppermute | solution.py:372
  66.2 1.7 %collective-permute-start.18 = (bf16[96,640]{1,0:T(8,128)(2,1)S(1)}, bf16[96,640]{1,0:T(8,128)(2,1)S(1)}, u32[]{:S(2)}, u32[]{:S(2)}) collective-permute-start(bf16[96,640]{1,0:T(8,128)(2,1)S(1)} %get-tuple-element.86), channel_id=1, source_target_pairs={{0,1},{1,0},{2,3},{3,2},{4,5},{5,4},{6,7},{7,6},{8,9},{9,8},{10,11... | collective-permute-start | bytes 368648 | tf_op jit(solution)/shard_map/ppermute | solution.py:372
  66.7 1.4 %collective-permute-start.19 = (bf16[96,640]{1,0:T(8,128)(2,1)S(1)}, bf16[96,640]{1,0:T(8,128)(2,1)S(1)}, u32[]{:S(2)}, u32[]{:S(2)}) collective-permute-start(bf16[96,640]{1,0:T(8,128)(2,1)S(1)} %get-tuple-element.87), channel_id=1, source_target_pairs={{0,1},{1,0},{2,3},{3,2},{4,5},{5,4},{6,7},{7,6},{8,9},{9,8},{10,11... | collective-permute-start | bytes 368648 | tf_op jit(solution)/shard_map/ppermute | solution.py:372
  66.8 13.7 %copy-start.4 = (s32[128,6]{0,1:T(8,128)S(1)}, s32[128,6]{0,1:T(8,128)}, u32[]{:S(2)}) copy-start(s32[128,6]{0,1:T(8,128)} %param.10) | copy-start | bytes 9220
  66.8 13.7 %copy-start.5 = (s32[128,6]{0,1:T(8,128)S(1)}, s32[128,6]{0,1:T(8,128)}, u32[]{:S(2)}) copy-start(s32[128,6]{0,1:T(8,128)} %param.11) | copy-start | bytes 9220
  68.1 13.9 %collective-permute-start.20 = (bf16[192,640]{1,0:T(8,128)(2,1)S(1)}, bf16[192,640]{1,0:T(8,128)(2,1)S(1)}, u32[]{:S(2)}, u32[]{:S(2)}) collective-permute-start(bf16[192,640]{1,0:T(8,128)(2,1)S(1)} %shard_map.125), channel_id=1, source_target_pairs={{0,2},{1,3},{2,0},{3,1},{4,6},{5,7},{6,4},{7,5},{8,10},{9,11},{10,... | collective-permute-start | bytes 737288 | tf_op jit(solution)/shard_map/ppermute | solution.py:372

commit v5 on v4

--- a/solution.py
+++ b/solution.py
@@ -202,11 +202,10 @@
         shift = cut[0] if half == 0 else 0
         for m in range(far):
             at = pl.ds((half * far + m) * capacity, capacity)
-            scale = jnp.broadcast_to(weights_of(scales[m : m + 1], half == 0), (capacity, LANES))
+            scale = weights_of(scales[m : m + 1], half == 0).astype(jnp.bfloat16)
+            scale = jnp.broadcast_to(scale, (capacity, LANES))
             for i in range(0, columns, LANES):
-                weighted[at, i : i + LANES] = (
-                    scale * pieces[m][:, shift + i : shift + i + LANES].astype(jnp.float32)
-                ).astype(jnp.bfloat16)
+                weighted[at, i : i + LANES] = scale * pieces[m][:, shift + i : shift + i + LANES]
 
 
 def terms(tile, turned_ref, weighted, outs):
@@ -453,12 +452,21 @@
         [VMEM] * (4 + far),
         32,
     )(weight_here, weight_core, weight_y, weight_both, *own)
+    more = call(
+        functools.partial(select_more_body, capacity, topk, cuts[1]),
+        [shape(capacity, sizes[1])] * far,
+        [VMEM] * 2,
+        16,
+        flops=2 * far * capacity * tok_rows * sizes[1],
+        moved=4 * far * capacity * sizes[1],
+        after=far0[:1],
+    )(raw, far_meta)
     first0, weighted = call(
         functools.partial(first_term_body, far, cuts[0], 640),
         [shape(shard, sizes[0]), shape(rows, sizes[0])],
         [VMEM] * (1 + 2 * far),
         24,
-        after=[own_proj],
+        after=[own_proj, more[0]],
     )(turned, *own, *far0)
     first0 = hop(first0, "edp", 1)
     def more_terms(shards, outs, after=()):
@@ -469,16 +477,7 @@
     across0, send0 = more_terms([2, 1], [shape(shard, sizes[0], dtype=f32), shape(shard, sizes[0])])
     core0 = hop(send0, "edp", 1)
     sent0, from_y0 = across(0, across0, [first0])
-    found = call(
-        functools.partial(select_more_body, capacity, topk, cuts[1]),
-        [shape(capacity, sizes[1])] * far,
-        [VMEM] * 2,
-        16,
-        flops=2 * far * capacity * tok_rows * sizes[1],
-        moved=4 * far * capacity * sizes[1],
-        after=[sent0],
-    )(raw, far_meta)
-    far1 = spread(found)
+    far1 = [more[0]] + [hop(more[m], "exp", m, sent0) for m in range(1, far)]
     half_scratch = [
         pltpu.VMEM((2, far * capacity, units), bf16),
         pltpu.SemaphoreType.DMA((far // 2, 2)),

time: 83.2 us -> 82.5 us (level)
  transfers between devices with their start and end apart: 21 -> 21, of which waited for: 9 -> 10; matrix products, arithmetic and copies ran while one was open for 0% -> 0% of each run, Pallas kernels for 15% -> 15%
where the time goes in v5:
time: 82.5 us; the launch traced here: 82.2 us
  waiting for transfers between devices  30.4 us (37%)
  starting transfers between devices  22.4 us (27%)
  Pallas kernels  14.1 us (17%)
  blocking collectives  10.3 us (12%)
  local copies, waits for them, and re-layouts  4.18 us (5%)
    ppermute x21, waiting for transfers between devices, hop(): return lax.ppermute(x, axis, flip(lax.axis_size(axis), mask))  30.4 us
    ppermute x21, starting transfers between devices, hop(): return lax.ppermute(x, axis, flip(lax.axis_size(axis), mask))  22.4 us
    all_to_all x1, blocking collectives, relayed(): returned = lax.all_to_all(score, 'exp', split_axis=0, concat_axis=0)  10.3 us
    unnamed x14, local copies, waits for them, and re-layouts  4.18 us
    pallas_call x1, Pallas kernels, relayed(): call(functools.partial(routing_body, capacity, n_exp, far), [shape(META_R...  2.38 us
    pallas_call x1, Pallas kernels, relayed(): call(functools.partial(project_far_body, far, cuts[0]), [shape(far * capa...  1.82 us
    pallas_call x2, Pallas kernels, more_terms(): call(functools.partial(more_terms_body, 640, shards), outs, [VMEM] * 2, 2...  1.72 us
  transfers between devices with their start and end apart: 21, of which 10 were waited for; matrix products, arithmetic and copies ran while one was open for 0% of the time, Pallas kernels for 15%

profile of v5, /device:TPU:0, one launch (start us, length us, event | category | flops | bytes accessed | tf_op | source)
XLA Modules:
  0.0 82.2 jit_solution(12728248723180867436)
XLA Ops:
  0.6 3.0 %collective-permute-start.2 = (bf16[192,2560]{1,0:T(8,128)(2,1)}, bf16[192,2560]{1,0:T(8,128)(2,1)S(1)}, u32[]{:S(2)}, u32[]{:S(2)}) collective-permute-start(bf16[192,2560]{1,0:T(8,128)(2,1)} %bitcast.14), channel_id=1, source_target_pairs={{0,2},{1,3},{2,0},{3,1},{4,6},{5,7},{6,4},{7,5},{8,10},{9,11},{10,... | collective-permute-start | bytes 2949128 | tf_op jit(solution)/shard_map/ppermute | solution.py:371
  3.7 2.6 %collective-permute-start.5 = (bf16[128,2560]{1,0:T(8,128)(2,1)}, bf16[128,2560]{1,0:T(8,128)(2,1)S(1)}, u32[]{:S(2)}, u32[]{:S(2)}) collective-permute-start(bf16[128,2560]{1,0:T(8,128)(2,1)} %refs_2_.1), channel_id=1, source_target_pairs={{0,16},{4,20},{8,24},{12,28},{16,0},{20,4},{24,8},{28,12},{1,17},{... | collective-permute-start | bytes 1966088 | tf_op jit(solution)/shard_map/ppermute | solution.py:371
  6.3 2.4 %shard_map.111 = (f32[24,128]{1,0:T(8,128)}, bf16[64,2560]{1,0:T(8,128)(2,1)}, bf16[64,2560]{1,0:T(8,128)(2,1)}) custom-call(s32[6,128]{1,0:T(8,128)} %bitcast.19, s32[6,128]{1,0:T(8,128)} %bitcast.21, bf16[6,128]{1,0:T(8,128)(2,1)} %bitcast.27, s32[1,8]{1,0:T(1,128)} %refs_3_.1, bf16[128,2560]{1,0:T(8,128)(2,1)} %refs_2_.1), custom_call_target="tpu_custom_call" | custom-call | flops 167772160 | bytes 1310720 | tf_op jit(solution)/shard_map/pallas_call | solution.py:376
  8.6 1.6 %collective-permute-start.4 = (bf16[64,2560]{1,0:T(8,128)(2,1)}, bf16[64,2560]{1,0:T(8,128)(2,1)S(1)}, u32[]{:S(2)}, u32[]{:S(2)}) collective-permute-start(bf16[64,2560]{1,0:T(8,128)(2,1)} %get-tuple-element.58), channel_id=1, source_target_pairs={{0,8},{4,12},{8,0},{12,4},{16,24},{20,28},{24,16},{28,20},{1,9},{5... | collective-permute-start | bytes 983048 | tf_op jit(solution)/shard_map/ppermute | solution.py:371
  10.2 1.4 %collective-permute-start = (bf16[64,2560]{1,0:T(8,128)(2,1)}, bf16[64,2560]{1,0:T(8,128)(2,1)S(1)}, u32[]{:S(2)}, u32[]{:S(2)}) collective-permute-start(bf16[64,2560]{1,0:T(8,128)(2,1)} %get-tuple-element.54), channel_id=1, source_target_pairs={{0,12},{4,8},{8,4},{12,0},{16,28},{20,24},{24,20},{28,16},{1,13},{... | collective-permute-start | bytes 983048 | tf_op jit(solution)/shard_map/ppermute | solution.py:371
  11.6 1.2 %copy-done.1 = bf16[1,192,2560]{2,1,0:T(8,128)(2,1)S(1)} copy-done((bf16[1,192,2560]{2,1,0:T(8,128)(2,1)S(1)}, bf16[1,192,2560]{2,1,0:T(8,128)(2,1)}, u32[]{:S(2)}) %copy-start.1) | copy-done | bytes 983064
  12.8 1.1 %copy-done.2 = bf16[1,1,512,768]{3,2,1,0:T(8,128)(2,1)S(1)} copy-done((bf16[1,1,512,768]{3,2,1,0:T(8,128)(2,1)S(1)}, bf16[1,1,512,768]{3,2,1,0:T(8,128)(2,1)}, u32[]{:S(2)}) %copy-start.2) | copy-done | bytes 786456
  13.9 1.1 %copy-done.3 = bf16[1,1,512,768]{3,2,1,0:T(8,128)(2,1)S(1)} copy-done((bf16[1,1,512,768]{3,2,1,0:T(8,128)(2,1)S(1)}, bf16[1,1,512,768]{3,2,1,0:T(8,128)(2,1)}, u32[]{:S(2)}) %copy-start.3) | copy-done | bytes 786456
  15.1 0.7 copy-done.6
  15.8 0.8 shard_map.112
  16.6 0.0 copy-done
  16.6 0.3 shard_map.113
  16.9 0.6 collective-permute-start.3
  17.5 11.3 %collective-permute-done.4.refs_1_.refs_6_.refs_5_.refs_4_ = bf16[64,2560]{1,0:T(8,128)(2,1)S(1)} collective-permute-done((bf16[64,2560]{1,0:T(8,128)(2,1)}, bf16[64,2560]{1,0:T(8,128)(2,1)S(1)}, u32[]{:S(2)}, u32[]{:S(2)}) %collective-permute-start.4) | collective-permute-done | bytes 327712 | tf_op jit(solution)/shard_map/ppermute | solution.py:371
  28.8 2.2 %collective-permute-start.6 = (f32[24,128]{1,0:T(8,128)S(1)}, f32[24,128]{1,0:T(8,128)S(1)}, u32[]{:S(2)}, u32[]{:S(2)}) collective-permute-start(f32[24,128]{1,0:T(8,128)S(1)} %get-tuple-element.59.refs_1_.refs_7_.refs_2_), channel_id=1, source_target_pairs={{0,16},{4,20},{8,24},{12,28},{16,0},{20,4},{24,8},{28,12},{1,17},{... | collective-permute-start | bytes 36872 | tf_op jit(solution)/shard_map/ppermute | solution.py:371
  31.0 7.9 %collective-permute-done.refs_2_.refs_7_.refs_6_.refs_5_ = bf16[64,2560]{1,0:T(8,128)(2,1)S(1)} collective-permute-done((bf16[64,2560]{1,0:T(8,128)(2,1)}, bf16[64,2560]{1,0:T(8,128)(2,1)S(1)}, u32[]{:S(2)}, u32[]{:S(2)}) %collective-permute-start) | collective-permute-done | bytes 327712 | tf_op jit(solution)/shard_map/ppermute | solution.py:371
  38.9 0.0 collective-permute-start.1
  38.9 0.0 collective-permute-done.3.refs_0_.refs_5_.refs_4_.refs_3_
  38.9 0.0 collective-permute-done.6.refs_6_.refs_2_
  38.9 0.0 collective-permute-done.5.refs_5_.refs_1_
  38.9 0.0 collective-permute-done.2.refs_4_.refs_2_
  39.0 0.4 shard_map.114
  39.4 0.6 collective-permute-start.7
  40.0 0.0 collective-permute-start.10
  40.0 0.5 collective-permute-start.8
  40.5 3.0 %collective-permute-start.9 = (bf16[64,2048]{1,0:T(8,128)(2,1)S(1)}, bf16[64,2048]{1,0:T(8,128)(2,1)S(1)}, u32[]{:S(2)}, u32[]{:S(2)}) collective-permute-start(bf16[64,2048]{1,0:T(8,128)(2,1)S(1)} %get-tuple-element.66), channel_id=1, source_target_pairs={{0,8},{4,12},{8,0},{12,4},{16,24},{20,28},{24,16},{28,20},{1,9},{5... | collective-permute-start | bytes 786440 | tf_op jit(solution)/shard_map/ppermute | solution.py:371
  43.4 0.3 shard_map.116
  43.7 0.0 collective-permute-done.1.refs_1_
  43.7 0.0 collective-permute-done.7.refs_3_
  43.7 1.5 %shard_map.115 = (bf16[768,2560]{1,0:T(8,128)(2,1)S(1)}, f32[256,768]{1,0:T(8,128)S(1)}) custom-call(bf16[192,2560]{1,0:T(8,128)(2,1)S(1)} %get-tuple-element.55.refs_0_, bf16[192,2560]{1,0:T(8,128)(2,1)S(1)} %collective-permute-done.1.refs_1_, bf16[192,2560]{1,0:T(8,128)(2,1)S(1)} %collective-permute-done.2.refs_4_.refs_2_, ...), custom_call_target="tpu_custom_call" | custom-call | tf_op jit(solution)/shard_map/pallas_call | solution.py:449
  45.2 4.9 %collective-permute-done.10.refs_10_.refs_6_.refs_13_.refs_8_ = bf16[64,2048]{1,0:T(8,128)(2,1)S(1)} collective-permute-done((bf16[64,2048]{1,0:T(8,128)(2,1)S(1)}, bf16[64,2048]{1,0:T(8,128)(2,1)S(1)}, u32[]{:S(2)}, u32[]{:S(2)}) %collective-permute-start.10) | collective-permute-done | bytes 262176 | tf_op jit(solution)/shard_map/ppermute | solution.py:371
  50.1 3.9 %collective-permute-done.8.refs_8_.refs_4_.refs_11_.refs_6_ = bf16[64,2048]{1,0:T(8,128)(2,1)S(1)} collective-permute-done((bf16[64,2048]{1,0:T(8,128)(2,1)S(1)}, bf16[64,2048]{1,0:T(8,128)(2,1)S(1)}, u32[]{:S(2)}, u32[]{:S(2)}) %collective-permute-start.8) | collective-permute-done | bytes 262176 | tf_op jit(solution)/shard_map/ppermute | solution.py:371
  53.9 0.0 collective-permute-done.9.refs_9_.refs_5_.refs_12_.refs_7_
  53.9 0.8 shard_map.117
  54.7 0.1 collective-permute-start.11
  54.8 1.1 %shard_map.118 = (f32[192,1920]{1,0:T(8,128)S(1)}, bf16[192,1920]{1,0:T(8,128)(2,1)S(1)}) custom-call(bf16[4,192,512]{2,1,0:T(8,128)(2,1)S(1)} %get-tuple-element.52.refs_2_.refs_0_.refs_1_, bf16[512,1920]{1,0:T(8,128)(2,1)S(1)} %get-tuple-element.68.refs_1_.refs_2_), custom_call_target="tpu_custom_call" | custom-call | tf_op jit(solution)/shard_map/pallas_call | solution.py:473
  55.9 0.6 collective-permute-start.12
  56.5 0.5 collective-permute-done.11.refs_1_
  57.0 0.1 shard_map.119.refs_0_
  57.1 0.6 collective-permute-start.16
  57.7 1.1 %collective-permute-start.15 = (bf16[64,640]{1,0:T(8,128)(2,1)S(1)}, bf16[64,640]{1,0:T(8,128)(2,1)S(1)}, u32[]{:S(2)}, u32[]{:S(2)}) collective-permute-start(bf16[64,640]{1,0:T(8,128)(2,1)S(1)} %get-tuple-element.81), channel_id=1, source_target_pairs={{0,12},{4,8},{8,4},{12,0},{16,28},{20,24},{24,20},{28,16},{1,13},{... | collective-permute-start | bytes 245768 | tf_op jit(solution)/shard_map/ppermute | solution.py:371
  58.8 1.8 %collective-permute-start.14 = (bf16[64,640]{1,0:T(8,128)(2,1)S(1)}, bf16[64,640]{1,0:T(8,128)(2,1)S(1)}, u32[]{:S(2)}, u32[]{:S(2)}) collective-permute-start(bf16[64,640]{1,0:T(8,128)(2,1)S(1)} %get-tuple-element.79), channel_id=1, source_target_pairs={{0,8},{4,12},{8,0},{12,4},{16,24},{20,28},{24,16},{28,20},{1,9},{5... | collective-permute-start | bytes 245768 | tf_op jit(solution)/shard_map/ppermute | solution.py:371
  60.6 0.6 collective-permute-start.13
  61.2 0.0 collective-permute-done.12.refs_2_.refs_6_
  61.2 1.8 %shard_map.120 = (f32[256,768]{1,0:T(8,128)S(1)}, bf16[512,768]{1,0:T(8,128)(2,1)}, bf16[512,768]{1,0:T(8,128)(2,1)}, f32[2,128]{1,0:T(2,128)S(1)}) custom-call(bf16[192,1920]{1,0:T(8,128)(2,1)S(1)} %shard_map.119.refs_0_, bf16[64,640]{1,0:T(8,128)(2,1)S(1)} %get-tuple-element.64.refs_1_.refs_6_, ...), custom_call_target="tpu_custom_call" | custom-call | tf_op jit(solution)/shard_map/pallas_call | solution.py:485
  63.0 0.6 shard_map.121.refs_0_.refs_5_
  63.7 0.1 collective-permute-done.15.refs_9_.refs_4_
  63.8 0.7 collective-permute-done.14.refs_8_.refs_3_
  64.5 0.5 collective-permute-done.13.refs_7_.refs_2_
  65.0 0.9 %shard_map.122 = (f32[192,640]{1,0:T(8,128)S(1)}, f32[192,640]{1,0:T(8,128)S(1)}, bf16[192,640]{1,0:T(8,128)(2,1)S(1)}, bf16[96,640]{1,0:T(8,128)(2,1)S(1)}, bf16[96,640]{1,0:T(8,128)(2,1)S(1)}) custom-call(f32[192,1920]{1,0:T(8,128)S(1)} %shard_map.121.refs_0_.refs_5_, bf16[4,192,512]{2,1,0:T(8,128)(2,1)S(1)} %get-tuple-element.52.refs_2_.refs_0_.refs_1_, ...), custom_call_target="tpu_custom_call" | custom-call | flops 503316480 | bytes 3276800 | tf_op jit(solution)/shard_map/pallas_call | solution.py:415
  66.0 0.1 collective-permute-start.17
  66.0 0.5 collective-permute-start.18
  66.5 0.1 collective-permute-start.19
  66.6 0.7 shard_map.123
  67.3 0.4 collective-permute-done.18.refs_3_
  67.7 0.2 collective-permute-done.19.refs_4_
  67.9 0.0 collective-permute-done.17.refs_1_
  67.9 0.1 shard_map.125
  68.0 1.6 %collective-permute-start.20 = (bf16[192,640]{1,0:T(8,128)(2,1)S(1)}, bf16[192,640]{1,0:T(8,128)(2,1)S(1)}, u32[]{:S(2)}, u32[]{:S(2)}) collective-permute-start(bf16[192,640]{1,0:T(8,128)(2,1)S(1)} %shard_map.125), channel_id=1, source_target_pairs={{0,2},{1,3},{2,0},{3,1},{4,6},{5,7},{6,4},{7,5},{8,10},{9,11},{10,... | collective-permute-start | bytes 737288 | tf_op jit(solution)/shard_map/ppermute | solution.py:371
  69.5 10.3 %all_to_all.11 = f32[8,1,64]{2,1,0:T(1,128)S(1)} all-to-all(f32[8,1,64]{2,1,0:T(1,128)S(1)} %bitcast.18), channel_id=1, replica_groups=mesh['exp'=8,'edp'=4] {'exp'}, dimensions={0} | all-to-all | bytes 4096 | tf_op jit(solution)/shard_map/all_to_all | solution.py:510
  79.8 0.0 collective-permute-done.16.refs_7_
  79.8 1.5 %shard_map.124 = (bf16[192,2560]{1,0:T(8,128)(2,1)}, f32[6,128]{1,0:T(8,128)}, bf16[512,768]{1,0:T(8,128)(2,1)}, bf16[512,768]{1,0:T(8,128)(2,1)}) custom-call(s32[6,128]{1,0:T(8,128)S(1)} %bitcast.20, s32[6,128]{1,0:T(8,128)S(1)} %bitcast.22, f32[24,128]{1,0:T(8,128)S(1)} %get-tuple-element.59.refs_1_.refs_7_.refs_2_, ...), custom_call_target="tpu_custom_call", output_to_operand_aliasing={{2}: (8, {}), {3}: (9, {})} | custom-call | tf_op jit(solution)/shard_map/pallas_call | solution.py:511
  81.4 0.0 collective-permute-done.20.refs_2_
  81.4 0.8 shard_map.126
  (9 shorter events, 0.0 us)
Async XLA Ops:
  0.6 38.3 %collective-permute-start.2 = (bf16[192,2560]{1,0:T(8,128)(2,1)}, bf16[192,2560]{1,0:T(8,128)(2,1)S(1)}, u32[]{:S(2)}, u32[]{:S(2)}) collective-permute-start(bf16[192,2560]{1,0:T(8,128)(2,1)} %bitcast.14), channel_id=1, source_target_pairs={{0,2},{1,3},{2,0},{3,1},{4,6},{5,7},{6,4},{7,5},{8,10},{9,11},{10,... | collective-permute-start | bytes 2949128 | tf_op jit(solution)/shard_map/ppermute | solution.py:371
  3.7 35.3 %collective-permute-start.5 = (bf16[128,2560]{1,0:T(8,128)(2,1)}, bf16[128,2560]{1,0:T(8,128)(2,1)S(1)}, u32[]{:S(2)}, u32[]{:S(2)}) collective-permute-start(bf16[128,2560]{1,0:T(8,128)(2,1)} %refs_2_.1), channel_id=1, source_target_pairs={{0,16},{4,20},{8,24},{12,28},{16,0},{20,4},{24,8},{28,12},{1,17},{... | collective-permute-start | bytes 1966088 | tf_op jit(solution)/shard_map/ppermute | solution.py:371
  6.3 10.3 %copy-start = (bf16[128,2560]{1,0:T(8,128)(2,1)S(1)}, bf16[128,2560]{1,0:T(8,128)(2,1)}, u32[]{:S(2)}) copy-start(bf16[128,2560]{1,0:T(8,128)(2,1)} %refs_2_.1) | copy-start | bytes 1966084
  8.6 20.2 %collective-permute-start.4 = (bf16[64,2560]{1,0:T(8,128)(2,1)}, bf16[64,2560]{1,0:T(8,128)(2,1)S(1)}, u32[]{:S(2)}, u32[]{:S(2)}) collective-permute-start(bf16[64,2560]{1,0:T(8,128)(2,1)} %get-tuple-element.58), channel_id=1, source_target_pairs={{0,8},{4,12},{8,0},{12,4},{16,24},{20,28},{24,16},{28,20},{1,9},{5... | collective-permute-start | bytes 983048 | tf_op jit(solution)/shard_map/ppermute | solution.py:371
  10.2 28.7 %collective-permute-start = (bf16[64,2560]{1,0:T(8,128)(2,1)}, bf16[64,2560]{1,0:T(8,128)(2,1)S(1)}, u32[]{:S(2)}, u32[]{:S(2)}) collective-permute-start(bf16[64,2560]{1,0:T(8,128)(2,1)} %get-tuple-element.54), channel_id=1, source_target_pairs={{0,12},{4,8},{8,4},{12,0},{16,28},{20,24},{24,20},{28,16},{1,13},{... | collective-permute-start | bytes 983048 | tf_op jit(solution)/shard_map/ppermute | solution.py:371
  11.6 1.2 %copy-start.1 = (bf16[1,192,2560]{2,1,0:T(8,128)(2,1)S(1)}, bf16[1,192,2560]{2,1,0:T(8,128)(2,1)}, u32[]{:S(2)}) copy-start(bf16[1,192,2560]{2,1,0:T(8,128)(2,1)} %param.13) | copy-start | bytes 2949124
  12.8 1.1 %copy-start.2 = (bf16[1,1,512,768]{3,2,1,0:T(8,128)(2,1)S(1)}, bf16[1,1,512,768]{3,2,1,0:T(8,128)(2,1)}, u32[]{:S(2)}) copy-start(bf16[1,1,512,768]{3,2,1,0:T(8,128)(2,1)} %param.14) | copy-start | bytes 2359300
  13.9 1.1 %copy-start.3 = (bf16[1,1,512,768]{3,2,1,0:T(8,128)(2,1)S(1)}, bf16[1,1,512,768]{3,2,1,0:T(8,128)(2,1)}, u32[]{:S(2)}) copy-start(bf16[1,1,512,768]{3,2,1,0:T(8,128)(2,1)} %param.15) | copy-start | bytes 2359300
  15.1 0.7 copy-start.6
  16.9 22.0 %collective-permute-start.3 = (bf16[64,2560]{1,0:T(8,128)(2,1)S(1)}, bf16[64,2560]{1,0:T(8,128)(2,1)S(1)}, u32[]{:S(2)}, u32[]{:S(2)}) collective-permute-start(bf16[64,2560]{1,0:T(8,128)(2,1)S(1)} %get-tuple-element.57), channel_id=1, source_target_pairs={{0,4},{4,0},{8,12},{12,8},{16,20},{20,16},{24,28},{28,24},{1,5},{5... | collective-permute-start | bytes 983048 | tf_op jit(solution)/shard_map/ppermute | solution.py:371
  28.8 10.1 %collective-permute-start.6 = (f32[24,128]{1,0:T(8,128)S(1)}, f32[24,128]{1,0:T(8,128)S(1)}, u32[]{:S(2)}, u32[]{:S(2)}) collective-permute-start(f32[24,128]{1,0:T(8,128)S(1)} %get-tuple-element.59.refs_1_.refs_7_.refs_2_), channel_id=1, source_target_pairs={{0,16},{4,20},{8,24},{12,28},{16,0},{20,4},{24,8},{28,12},{1,17},{... | collective-permute-start | bytes 36872 | tf_op jit(solution)/shard_map/ppermute | solution.py:371
  38.9 4.8 %collective-permute-start.1 = (bf16[192,2560]{1,0:T(8,128)(2,1)S(1)}, bf16[192,2560]{1,0:T(8,128)(2,1)S(1)}, u32[]{:S(2)}, u32[]{:S(2)}) collective-permute-start(bf16[192,2560]{1,0:T(8,128)(2,1)S(1)} %get-tuple-element.55.refs_0_), channel_id=1, source_target_pairs={{0,1},{1,0},{2,3},{3,2},{4,5},{5,4},{6,7},{7,6},{8,9},{9,8},{10,11... | collective-permute-start | bytes 2949128 | tf_op jit(solution)/shard_map/ppermute | solution.py:371
  39.4 4.3 %collective-permute-start.7 = (bf16[192,2560]{1,0:T(8,128)(2,1)S(1)}, bf16[192,2560]{1,0:T(8,128)(2,1)S(1)}, u32[]{:S(2)}, u32[]{:S(2)}) collective-permute-start(bf16[192,2560]{1,0:T(8,128)(2,1)S(1)} %collective-permute-done.2.refs_4_.refs_2_), channel_id=1, source_target_pairs={{0,1},{1,0},{2,3},{3,2},{4,5},{5,4},{6,7},{7,6},{8,9},{9,8},{10,11... | collective-permute-start | bytes 2949128 | tf_op jit(solution)/shard_map/ppermute | solution.py:371
  40.0 10.1 %collective-permute-start.10 = (bf16[64,2048]{1,0:T(8,128)(2,1)S(1)}, bf16[64,2048]{1,0:T(8,128)(2,1)S(1)}, u32[]{:S(2)}, u32[]{:S(2)}) collective-permute-start(bf16[64,2048]{1,0:T(8,128)(2,1)S(1)} %get-tuple-element.67), channel_id=1, source_target_pairs={{0,12},{4,8},{8,4},{12,0},{16,28},{20,24},{24,20},{28,16},{1,13},{... | collective-permute-start | bytes 786440 | tf_op jit(solution)/shard_map/ppermute | solution.py:371
  40.0 14.0 %collective-permute-start.8 = (bf16[64,2048]{1,0:T(8,128)(2,1)S(1)}, bf16[64,2048]{1,0:T(8,128)(2,1)S(1)}, u32[]{:S(2)}, u32[]{:S(2)}) collective-permute-start(bf16[64,2048]{1,0:T(8,128)(2,1)S(1)} %get-tuple-element.65), channel_id=1, source_target_pairs={{0,4},{4,0},{8,12},{12,8},{16,20},{20,16},{24,28},{28,24},{1,5},{5... | collective-permute-start | bytes 786440 | tf_op jit(solution)/shard_map/ppermute | solution.py:371
  40.5 13.5 %collective-permute-start.9 = (bf16[64,2048]{1,0:T(8,128)(2,1)S(1)}, bf16[64,2048]{1,0:T(8,128)(2,1)S(1)}, u32[]{:S(2)}, u32[]{:S(2)}) collective-permute-start(bf16[64,2048]{1,0:T(8,128)(2,1)S(1)} %get-tuple-element.66), channel_id=1, source_target_pairs={{0,8},{4,12},{8,0},{12,4},{16,24},{20,28},{24,16},{28,20},{1,9},{5... | collective-permute-start | bytes 786440 | tf_op jit(solution)/shard_map/ppermute | solution.py:371
  54.7 2.3 %collective-permute-start.11 = (bf16[192,1920]{1,0:T(8,128)(2,1)S(1)}, bf16[192,1920]{1,0:T(8,128)(2,1)S(1)}, u32[]{:S(2)}, u32[]{:S(2)}) collective-permute-start(bf16[192,1920]{1,0:T(8,128)(2,1)S(1)} %get-tuple-element.70), channel_id=1, source_target_pairs={{0,1},{1,0},{2,3},{3,2},{4,5},{5,4},{6,7},{7,6},{8,9},{9,8},{10,11... | collective-permute-start | bytes 2211848 | tf_op jit(solution)/shard_map/ppermute | solution.py:371
  55.9 5.3 %collective-permute-start.12 = (bf16[192,1920]{1,0:T(8,128)(2,1)S(1)}, bf16[192,1920]{1,0:T(8,128)(2,1)S(1)}, u32[]{:S(2)}, u32[]{:S(2)}) collective-permute-start(bf16[192,1920]{1,0:T(8,128)(2,1)S(1)} %get-tuple-element.71), channel_id=1, source_target_pairs={{0,1},{1,0},{2,3},{3,2},{4,5},{5,4},{6,7},{7,6},{8,9},{9,8},{10,11... | collective-permute-start | bytes 2211848 | tf_op jit(solution)/shard_map/ppermute | solution.py:371
  57.1 22.7 %collective-permute-start.16 = (bf16[192,1920]{1,0:T(8,128)(2,1)S(1)}, bf16[192,1920]{1,0:T(8,128)(2,1)S(1)}, u32[]{:S(2)}, u32[]{:S(2)}) collective-permute-start(bf16[192,1920]{1,0:T(8,128)(2,1)S(1)} %shard_map.119.refs_0_), channel_id=1, source_target_pairs={{0,2},{1,3},{2,0},{3,1},{4,6},{5,7},{6,4},{7,5},{8,10},{9,11},{10,... | collective-permute-start | bytes 2211848 | tf_op jit(solution)/shard_map/ppermute | solution.py:371
  57.7 6.1 %collective-permute-start.15 = (bf16[64,640]{1,0:T(8,128)(2,1)S(1)}, bf16[64,640]{1,0:T(8,128)(2,1)S(1)}, u32[]{:S(2)}, u32[]{:S(2)}) collective-permute-start(bf16[64,640]{1,0:T(8,128)(2,1)S(1)} %get-tuple-element.81), channel_id=1, source_target_pairs={{0,12},{4,8},{8,4},{12,0},{16,28},{20,24},{24,20},{28,16},{1,13},{... | collective-permute-start | bytes 245768 | tf_op jit(solution)/shard_map/ppermute | solution.py:371
  58.8 5.7 %collective-permute-start.14 = (bf16[64,640]{1,0:T(8,128)(2,1)S(1)}, bf16[64,640]{1,0:T(8,128)(2,1)S(1)}, u32[]{:S(2)}, u32[]{:S(2)}) collective-permute-start(bf16[64,640]{1,0:T(8,128)(2,1)S(1)} %get-tuple-element.79), channel_id=1, source_target_pairs={{0,8},{4,12},{8,0},{12,4},{16,24},{20,28},{24,16},{28,20},{1,9},{5... | collective-permute-start | bytes 245768 | tf_op jit(solution)/shard_map/ppermute | solution.py:371
  60.6 4.4 %collective-permute-start.13 = (bf16[64,640]{1,0:T(8,128)(2,1)S(1)}, bf16[64,640]{1,0:T(8,128)(2,1)S(1)}, u32[]{:S(2)}, u32[]{:S(2)}) collective-permute-start(bf16[64,640]{1,0:T(8,128)(2,1)S(1)} %get-tuple-element.77), channel_id=1, source_target_pairs={{0,4},{4,0},{8,12},{12,8},{16,20},{20,16},{24,28},{28,24},{1,5},{5... | collective-permute-start | bytes 245768 | tf_op jit(solution)/shard_map/ppermute | solution.py:371
  66.0 1.9 %collective-permute-start.17 = (bf16[192,640]{1,0:T(8,128)(2,1)S(1)}, bf16[192,640]{1,0:T(8,128)(2,1)S(1)}, u32[]{:S(2)}, u32[]{:S(2)}) collective-permute-start(bf16[192,640]{1,0:T(8,128)(2,1)S(1)} %get-tuple-element.90), channel_id=1, source_target_pairs={{0,1},{1,0},{2,3},{3,2},{4,5},{5,4},{6,7},{7,6},{8,9},{9,8},{10,11... | collective-permute-start | bytes 737288 | tf_op jit(solution)/shard_map/ppermute | solution.py:371
  66.0 1.7 %collective-permute-start.18 = (bf16[96,640]{1,0:T(8,128)(2,1)S(1)}, bf16[96,640]{1,0:T(8,128)(2,1)S(1)}, u32[]{:S(2)}, u32[]{:S(2)}) collective-permute-start(bf16[96,640]{1,0:T(8,128)(2,1)S(1)} %get-tuple-element.92), channel_id=1, source_target_pairs={{0,1},{1,0},{2,3},{3,2},{4,5},{5,4},{6,7},{7,6},{8,9},{9,8},{10,11... | collective-permute-start | bytes 368648 | tf_op jit(solution)/shard_map/ppermute | solution.py:371
  66.5 1.4 %collective-permute-start.19 = (bf16[96,640]{1,0:T(8,128)(2,1)S(1)}, bf16[96,640]{1,0:T(8,128)(2,1)S(1)}, u32[]{:S(2)}, u32[]{:S(2)}) collective-permute-start(bf16[96,640]{1,0:T(8,128)(2,1)S(1)} %get-tuple-element.93), channel_id=1, source_target_pairs={{0,1},{1,0},{2,3},{3,2},{4,5},{5,4},{6,7},{7,6},{8,9},{9,8},{10,11... | collective-permute-start | bytes 368648 | tf_op jit(solution)/shard_map/ppermute | solution.py:371
  66.6 13.2 %copy-start.4 = (s32[128,6]{0,1:T(8,128)S(1)}, s32[128,6]{0,1:T(8,128)}, u32[]{:S(2)}) copy-start(s32[128,6]{0,1:T(8,128)} %param.10) | copy-start | bytes 9220
  66.6 13.2 %copy-start.5 = (s32[128,6]{0,1:T(8,128)S(1)}, s32[128,6]{0,1:T(8,128)}, u32[]{:S(2)}) copy-start(s32[128,6]{0,1:T(8,128)} %param.11) | copy-start | bytes 9220
  68.0 13.4 %collective-permute-start.20 = (bf16[192,640]{1,0:T(8,128)(2,1)S(1)}, bf16[192,640]{1,0:T(8,128)(2,1)S(1)}, u32[]{:S(2)}, u32[]{:S(2)}) collective-permute-start(bf16[192,640]{1,0:T(8,128)(2,1)S(1)} %shard_map.125), channel_id=1, source_target_pairs={{0,2},{1,3},{2,0},{3,1},{4,6},{5,7},{6,4},{7,5},{8,10},{9,11},{10,... | collective-permute-start | bytes 737288 | tf_op jit(solution)/shard_map/ppermute | solution.py:371

commit v6 on v5

--- a/solution.py
+++ b/solution.py
@@ -195,46 +195,52 @@
         copy.wait()
 
 
-def weigh(far, cut, own, others, scales, weighted):
-    capacity = own[0].shape[0]
-    columns = cut[1] - cut[0]
+def weighted_rows(far, start, tile, cut, own, others, scales):
+    blocks = []
     for half, pieces in enumerate((own, others)):
-        shift = cut[0] if half == 0 else 0
+        first = start + (cut[0] if half == 0 else 0)
         for m in range(far):
-            at = pl.ds((half * far + m) * capacity, capacity)
             scale = weights_of(scales[m : m + 1], half == 0).astype(jnp.bfloat16)
-            scale = jnp.broadcast_to(scale, (capacity, LANES))
-            for i in range(0, columns, LANES):
-                weighted[at, i : i + LANES] = scale * pieces[m][:, shift + i : shift + i + LANES]
-
-
-def terms(tile, turned_ref, weighted, outs):
-    for i in range(weighted.shape[1] // tile):
-        lanes = pl.ds(i * tile, tile)
-        for n, refs in outs:
-            term = jnp.dot(turned_ref[n], weighted[:, lanes], preferred_element_type=jnp.float32)
-            high = term.shape[0] // len(refs)
-            for j, ref in enumerate(refs):
-                ref[:, lanes] = term[j * high : (j + 1) * high].astype(ref.dtype)
+            blocks.append(jnp.broadcast_to(scale, (scale.shape[0], tile)) * pieces[m][:, first : first + tile])
+    return jnp.concatenate(blocks, axis=0)
+
+
+def terms(turned_ref, rows, lanes, outs):
+    first = outs[0][0]
+    refs = [ref for _, some in outs for ref in some]
+    shard, depth = turned_ref.shape[1:]
+    left = turned_ref[first : first + len(outs)].reshape(len(outs) * shard, depth)
+    term = jnp.dot(left, rows, preferred_element_type=jnp.float32)
+    at = 0
+    for ref in refs:
+        ref[:, lanes] = term[at : at + ref.shape[0]].astype(ref.dtype)
+        at += ref.shape[0]
 
 
 def first_term_body(far, cut, tile, turned_ref, *refs):
     own, others, (send_ref, weighted) = refs[:far], refs[far : 2 * far], refs[2 * far :]
-    weigh(far, cut, own, others, others, weighted)
-    terms(tile, turned_ref, weighted, [(3, [send_ref])])
+    for start in range(0, cut[1] - cut[0], tile):
+        lanes = pl.ds(start, tile)
+        rows = weighted_rows(far, start, tile, cut, own, others, others)
+        weighted[:, lanes] = rows
+        terms(turned_ref, rows, lanes, [(3, [send_ref])])
 
 
 def more_terms_body(tile, shards, turned_ref, weighted, *refs):
-    terms(tile, turned_ref, weighted, [(n, [ref]) for n, ref in zip(shards, refs)])
+    for start in range(0, weighted.shape[1], tile):
+        lanes = pl.ds(start, tile)
+        terms(turned_ref, weighted[:, lanes], lanes, [(n, [ref]) for n, ref in zip(shards, refs)])
 
 
 def term_body(far, cut, tile, turned_ref, *refs):
-    own, others, scales, (own_ref, across_ref, send_ref, *send_across_refs, weighted) = (
+    own, others, scales, (own_ref, across_ref, send_ref, *send_across_refs) = (
         refs[:far], refs[far : 2 * far], refs[2 * far : 3 * far], refs[3 * far :]
     )
-    weigh(far, cut, own, others, scales, weighted)
-    outs = [(3, send_across_refs), (2, [across_ref]), (1, [send_ref]), (0, [own_ref])]
-    terms(tile, turned_ref, weighted, outs)
+    for start in range(0, cut[1] - cut[0], tile):
+        lanes = pl.ds(start, tile)
+        rows = weighted_rows(far, start, tile, cut, own, others, scales)
+        outs = [(0, [own_ref]), (1, [send_ref]), (2, [across_ref]), (3, send_across_refs)]
+        terms(turned_ref, rows, lanes, outs)
 
 
 def nt(a, b):
@@ -359,7 +365,7 @@
     far = n_exp // 2
     cuts = column_cuts(width)
     sizes = [b - a for a, b in cuts]
-    splits = [1, 2]
+    splits = [1, 1]
     bf16, f32 = jnp.bfloat16, jnp.float32
 
     def shape(*dims, dtype=bf16):
@@ -413,7 +419,7 @@
 
     def term(k, others, scales, after=()):
         return call(
-            functools.partial(term_body, far, cuts[k], 640),
+            functools.partial(term_body, far, cuts[k], sizes[k]),
             [shape(shard, sizes[k], dtype=f32)] * 2
             + [shape(shard, sizes[k])]
             + [shape(shard // splits[k], sizes[k])] * splits[k],
@@ -421,7 +427,6 @@
             24,
             flops=2 * rows * units * sizes[k],
             moved=4 * (rows + units) * sizes[k],
-            scratch=[pltpu.VMEM((rows, sizes[k]), bf16)],
             after=after,
         )(turned, *own, *others, *scales)
 
@@ -462,7 +467,7 @@
         after=far0[:1],
     )(raw, far_meta)
     first0, weighted = call(
-        functools.partial(first_term_body, far, cuts[0], 640),
+        functools.partial(first_term_body, far, cuts[0], sizes[0]),
         [shape(shard, sizes[0]), shape(rows, sizes[0])],
         [VMEM] * (1 + 2 * far),
         24,
@@ -471,10 +476,10 @@
     first0 = hop(first0, "edp", 1)
     def more_terms(shards, outs, after=()):
         return call(
-            functools.partial(more_terms_body, 640, shards), outs, [VMEM] * 2, 24, after=after
+            functools.partial(more_terms_body, sizes[0], shards), outs, [VMEM] * 2, 24, after=after
         )(turned, weighted)
 
-    across0, send0 = more_terms([2, 1], [shape(shard, sizes[0], dtype=f32), shape(shard, sizes[0])])
+    send0, across0 = more_terms([1, 2], [shape(shard, sizes[0]), shape(shard, sizes[0], dtype=f32)])
     core0 = hop(send0, "edp", 1)
     sent0, from_y0 = across(0, across0, [first0])
     far1 = [more[0]] + [hop(more[m], "exp", m, sent0) for m in range(1, far)]

time: 82.5 us -> 82.4 us (level)
    ppermute x21 -> x20, waiting for transfers between devices: 30.4 us -> 30.6 us  [hop(): return lax.ppermute(x, axis, flip(lax.axis_size(axis), mask))]
    ppermute x21 -> x20, starting transfers between devices: 22.4 us -> 22.3 us  [hop(): return lax.ppermute(x, axis, flip(lax.axis_size(axis), mask))]
  transfers between devices with their start and end apart: 21 -> 20, of which waited for: 10 -> 10; matrix products, arithmetic and copies ran while one was open for 0% -> 0% of each run, Pallas kernels for 15% -> 15%
where the time goes in v6:
time: 82.4 us; the launch traced here: 82 us
  waiting for transfers between devices  30.6 us (37%)
  starting transfers between devices  22.3 us (27%)
  Pallas kernels  13.9 us (17%)
  blocking collectives  10.3 us (12%)
  local copies, waits for them, and re-layouts  4.18 us (5%)
    ppermute x20, waiting for transfers between devices, hop(): return lax.ppermute(x, axis, flip(lax.axis_size(axis), mask))  30.6 us
    ppermute x20, starting transfers between devices, hop(): return lax.ppermute(x, axis, flip(lax.axis_size(axis), mask))  22.3 us
    all_to_all x1, blocking collectives, relayed(): returned = lax.all_to_all(score, 'exp', split_axis=0, concat_axis=0)  10.3 us
    unnamed x14, local copies, waits for them, and re-layouts  4.18 us
    pallas_call x1, Pallas kernels, relayed(): call(functools.partial(routing_body, capacity, n_exp, far), [shape(META_R...  2.38 us
    pallas_call x1, Pallas kernels, relayed(): call(functools.partial(project_far_body, far, cuts[0]), [shape(far * capa...  1.82 us
  transfers between devices with their start and end apart: 20, of which 10 were waited for; matrix products, arithmetic and copies ran while one was open for 0% of the time, Pallas kernels for 15%

profile of v6, /device:TPU:0, one launch (start us, length us, event | category | flops | bytes accessed | tf_op | source)
XLA Modules:
  0.0 82.0 jit_solution(394492633808247020)
XLA Ops:
  0.6 3.0 %collective-permute-start.2 = (bf16[192,2560]{1,0:T(8,128)(2,1)}, bf16[192,2560]{1,0:T(8,128)(2,1)S(1)}, u32[]{:S(2)}, u32[]{:S(2)}) collective-permute-start(bf16[192,2560]{1,0:T(8,128)(2,1)} %bitcast.14), channel_id=1, source_target_pairs={{0,2},{1,3},{2,0},{3,1},{4,6},{5,7},{6,4},{7,5},{8,10},{9,11},{10,... | collective-permute-start | bytes 2949128 | tf_op jit(solution)/shard_map/ppermute | solution.py:377
  3.7 2.6 %collective-permute-start.5 = (bf16[128,2560]{1,0:T(8,128)(2,1)}, bf16[128,2560]{1,0:T(8,128)(2,1)S(1)}, u32[]{:S(2)}, u32[]{:S(2)}) collective-permute-start(bf16[128,2560]{1,0:T(8,128)(2,1)} %refs_2_.1), channel_id=1, source_target_pairs={{0,16},{4,20},{8,24},{12,28},{16,0},{20,4},{24,8},{28,12},{1,17},{... | collective-permute-start | bytes 1966088 | tf_op jit(solution)/shard_map/ppermute | solution.py:377
  6.3 2.4 %shard_map.111 = (f32[24,128]{1,0:T(8,128)}, bf16[64,2560]{1,0:T(8,128)(2,1)}, bf16[64,2560]{1,0:T(8,128)(2,1)}) custom-call(s32[6,128]{1,0:T(8,128)} %bitcast.19, s32[6,128]{1,0:T(8,128)} %bitcast.21, bf16[6,128]{1,0:T(8,128)(2,1)} %bitcast.27, s32[1,8]{1,0:T(1,128)} %refs_3_.1, bf16[128,2560]{1,0:T(8,128)(2,1)} %refs_2_.1), custom_call_target="tpu_custom_call" | custom-call | flops 167772160 | bytes 1310720 | tf_op jit(solution)/shard_map/pallas_call | solution.py:382
  8.6 1.6 %collective-permute-start.4 = (bf16[64,2560]{1,0:T(8,128)(2,1)}, bf16[64,2560]{1,0:T(8,128)(2,1)S(1)}, u32[]{:S(2)}, u32[]{:S(2)}) collective-permute-start(bf16[64,2560]{1,0:T(8,128)(2,1)} %get-tuple-element.57), channel_id=1, source_target_pairs={{0,8},{4,12},{8,0},{12,4},{16,24},{20,28},{24,16},{28,20},{1,9},{5... | collective-permute-start | bytes 983048 | tf_op jit(solution)/shard_map/ppermute | solution.py:377
  10.2 1.4 %collective-permute-start = (bf16[64,2560]{1,0:T(8,128)(2,1)}, bf16[64,2560]{1,0:T(8,128)(2,1)S(1)}, u32[]{:S(2)}, u32[]{:S(2)}) collective-permute-start(bf16[64,2560]{1,0:T(8,128)(2,1)} %get-tuple-element.53), channel_id=1, source_target_pairs={{0,12},{4,8},{8,4},{12,0},{16,28},{20,24},{24,20},{28,16},{1,13},{... | collective-permute-start | bytes 983048 | tf_op jit(solution)/shard_map/ppermute | solution.py:377
  11.6 1.2 %copy-done.1 = bf16[1,192,2560]{2,1,0:T(8,128)(2,1)S(1)} copy-done((bf16[1,192,2560]{2,1,0:T(8,128)(2,1)S(1)}, bf16[1,192,2560]{2,1,0:T(8,128)(2,1)}, u32[]{:S(2)}) %copy-start.1) | copy-done | bytes 983064
  12.8 1.1 %copy-done.2 = bf16[1,1,512,768]{3,2,1,0:T(8,128)(2,1)S(1)} copy-done((bf16[1,1,512,768]{3,2,1,0:T(8,128)(2,1)S(1)}, bf16[1,1,512,768]{3,2,1,0:T(8,128)(2,1)}, u32[]{:S(2)}) %copy-start.2) | copy-done | bytes 786456
  13.9 1.1 %copy-done.3 = bf16[1,1,512,768]{3,2,1,0:T(8,128)(2,1)S(1)} copy-done((bf16[1,1,512,768]{3,2,1,0:T(8,128)(2,1)S(1)}, bf16[1,1,512,768]{3,2,1,0:T(8,128)(2,1)}, u32[]{:S(2)}) %copy-start.3) | copy-done | bytes 786456
  15.1 0.7 copy-done.6
  15.8 0.8 shard_map.112
  16.6 0.0 copy-done
  16.6 0.3 shard_map.113
  16.9 0.6 collective-permute-start.3
  17.5 11.3 %collective-permute-done.4.refs_1_.refs_6_.refs_5_.refs_4_ = bf16[64,2560]{1,0:T(8,128)(2,1)S(1)} collective-permute-done((bf16[64,2560]{1,0:T(8,128)(2,1)}, bf16[64,2560]{1,0:T(8,128)(2,1)S(1)}, u32[]{:S(2)}, u32[]{:S(2)}) %collective-permute-start.4) | collective-permute-done | bytes 327712 | tf_op jit(solution)/shard_map/ppermute | solution.py:377
  28.8 2.2 %collective-permute-start.6 = (f32[24,128]{1,0:T(8,128)S(1)}, f32[24,128]{1,0:T(8,128)S(1)}, u32[]{:S(2)}, u32[]{:S(2)}) collective-permute-start(f32[24,128]{1,0:T(8,128)S(1)} %get-tuple-element.58.refs_1_.refs_7_.refs_2_), channel_id=1, source_target_pairs={{0,16},{4,20},{8,24},{12,28},{16,0},{20,4},{24,8},{28,12},{1,17},{... | collective-permute-start | bytes 36872 | tf_op jit(solution)/shard_map/ppermute | solution.py:377
  31.0 7.9 %collective-permute-done.refs_2_.refs_7_.refs_6_.refs_5_ = bf16[64,2560]{1,0:T(8,128)(2,1)S(1)} collective-permute-done((bf16[64,2560]{1,0:T(8,128)(2,1)}, bf16[64,2560]{1,0:T(8,128)(2,1)S(1)}, u32[]{:S(2)}, u32[]{:S(2)}) %collective-permute-start) | collective-permute-done | bytes 327712 | tf_op jit(solution)/shard_map/ppermute | solution.py:377
  38.9 0.0 collective-permute-start.1
  38.9 0.0 collective-permute-done.3.refs_0_.refs_5_.refs_4_.refs_3_
  38.9 0.0 collective-permute-done.6.refs_6_.refs_2_
  38.9 0.0 collective-permute-done.5.refs_5_.refs_1_
  38.9 0.0 collective-permute-done.2.refs_4_.refs_2_
  39.0 0.4 shard_map.114
  39.4 0.6 collective-permute-start.7
  40.0 0.0 collective-permute-start.10
  40.0 0.5 collective-permute-start.8
  40.5 3.0 %collective-permute-start.9 = (bf16[64,2048]{1,0:T(8,128)(2,1)S(1)}, bf16[64,2048]{1,0:T(8,128)(2,1)S(1)}, u32[]{:S(2)}, u32[]{:S(2)}) collective-permute-start(bf16[64,2048]{1,0:T(8,128)(2,1)S(1)} %get-tuple-element.65), channel_id=1, source_target_pairs={{0,8},{4,12},{8,0},{12,4},{16,24},{20,28},{24,16},{28,20},{1,9},{5... | collective-permute-start | bytes 786440 | tf_op jit(solution)/shard_map/ppermute | solution.py:377
  43.4 0.3 shard_map.116
  43.7 0.0 collective-permute-done.1.refs_1_
  43.7 0.0 collective-permute-done.7.refs_3_
  43.7 1.5 %shard_map.115 = (bf16[768,2560]{1,0:T(8,128)(2,1)S(1)}, f32[256,768]{1,0:T(8,128)S(1)}) custom-call(bf16[192,2560]{1,0:T(8,128)(2,1)S(1)} %get-tuple-element.54.refs_0_, bf16[192,2560]{1,0:T(8,128)(2,1)S(1)} %collective-permute-done.1.refs_1_, bf16[192,2560]{1,0:T(8,128)(2,1)S(1)} %collective-permute-done.2.refs_4_.refs_2_, ...), custom_call_target="tpu_custom_call" | custom-call | tf_op jit(solution)/shard_map/pallas_call | solution.py:454
  45.2 4.9 %collective-permute-done.10.refs_10_.refs_6_.refs_13_.refs_8_ = bf16[64,2048]{1,0:T(8,128)(2,1)S(1)} collective-permute-done((bf16[64,2048]{1,0:T(8,128)(2,1)S(1)}, bf16[64,2048]{1,0:T(8,128)(2,1)S(1)}, u32[]{:S(2)}, u32[]{:S(2)}) %collective-permute-start.10) | collective-permute-done | bytes 262176 | tf_op jit(solution)/shard_map/ppermute | solution.py:377
  50.1 3.9 %collective-permute-done.8.refs_8_.refs_4_.refs_11_.refs_6_ = bf16[64,2048]{1,0:T(8,128)(2,1)S(1)} collective-permute-done((bf16[64,2048]{1,0:T(8,128)(2,1)S(1)}, bf16[64,2048]{1,0:T(8,128)(2,1)S(1)}, u32[]{:S(2)}, u32[]{:S(2)}) %collective-permute-start.8) | collective-permute-done | bytes 262176 | tf_op jit(solution)/shard_map/ppermute | solution.py:377
  53.9 0.0 collective-permute-done.9.refs_9_.refs_5_.refs_12_.refs_7_
  53.9 0.7 shard_map.117
  54.6 0.1 collective-permute-start.11
  54.7 1.0 %shard_map.118 = (bf16[192,1920]{1,0:T(8,128)(2,1)S(1)}, f32[192,1920]{1,0:T(8,128)S(1)}) custom-call(bf16[4,192,512]{2,1,0:T(8,128)(2,1)S(1)} %get-tuple-element.51.refs_2_.refs_0_.refs_1_, bf16[512,1920]{1,0:T(8,128)(2,1)S(1)} %get-tuple-element.67.refs_1_.refs_2_), custom_call_target="tpu_custom_call" | custom-call | tf_op jit(solution)/shard_map/pallas_call | solution.py:478
  55.7 0.6 collective-permute-start.12
  56.3 0.7 collective-permute-done.11.refs_1_
  56.9 0.1 shard_map.119.refs_0_
  57.1 0.6 collective-permute-start.16
  57.6 1.1 %collective-permute-start.15 = (bf16[64,640]{1,0:T(8,128)(2,1)S(1)}, bf16[64,640]{1,0:T(8,128)(2,1)S(1)}, u32[]{:S(2)}, u32[]{:S(2)}) collective-permute-start(bf16[64,640]{1,0:T(8,128)(2,1)S(1)} %get-tuple-element.80), channel_id=1, source_target_pairs={{0,12},{4,8},{8,4},{12,0},{16,28},{20,24},{24,20},{28,16},{1,13},{... | collective-permute-start | bytes 245768 | tf_op jit(solution)/shard_map/ppermute | solution.py:377
  58.7 1.8 %collective-permute-start.14 = (bf16[64,640]{1,0:T(8,128)(2,1)S(1)}, bf16[64,640]{1,0:T(8,128)(2,1)S(1)}, u32[]{:S(2)}, u32[]{:S(2)}) collective-permute-start(bf16[64,640]{1,0:T(8,128)(2,1)S(1)} %get-tuple-element.78), channel_id=1, source_target_pairs={{0,8},{4,12},{8,0},{12,4},{16,24},{20,28},{24,16},{28,20},{1,9},{5... | collective-permute-start | bytes 245768 | tf_op jit(solution)/shard_map/ppermute | solution.py:377
  60.5 0.6 collective-permute-start.13
  61.1 0.0 collective-permute-done.12.refs_2_.refs_6_
  61.1 1.8 %shard_map.120 = (f32[256,768]{1,0:T(8,128)S(1)}, bf16[512,768]{1,0:T(8,128)(2,1)}, bf16[512,768]{1,0:T(8,128)(2,1)}, f32[2,128]{1,0:T(2,128)S(1)}) custom-call(bf16[192,1920]{1,0:T(8,128)(2,1)S(1)} %shard_map.119.refs_0_, bf16[64,640]{1,0:T(8,128)(2,1)S(1)} %get-tuple-element.63.refs_1_.refs_6_, ...), custom_call_target="tpu_custom_call" | custom-call | tf_op jit(solution)/shard_map/pallas_call | solution.py:490
  62.9 0.6 shard_map.121.refs_0_.refs_5_
  63.5 0.2 collective-permute-done.15.refs_9_.refs_4_
  63.7 0.7 collective-permute-done.14.refs_8_.refs_3_
  64.4 0.5 collective-permute-done.13.refs_7_.refs_2_
  65.0 0.9 %shard_map.122 = (f32[192,640]{1,0:T(8,128)S(1)}, f32[192,640]{1,0:T(8,128)S(1)}, bf16[192,640]{1,0:T(8,128)(2,1)S(1)}, bf16[192,640]{1,0:T(8,128)(2,1)S(1)}) custom-call(f32[192,1920]{1,0:T(8,128)S(1)} %shard_map.121.refs_0_.refs_5_, bf16[4,192,512]{2,1,0:T(8,128)(2,1)S(1)} %get-tuple-element.51.refs_2_.refs_0_.refs_1_, ...), custom_call_target="tpu_custom_call" | custom-call | flops 503316480 | bytes 3276800 | tf_op jit(solution)/shard_map/pallas_call | solution.py:421
  65.8 0.1 collective-permute-start.17
  65.9 0.5 collective-permute-start.18
  66.4 0.7 shard_map.123
  67.1 0.3 collective-permute-done.17.refs_1_
  67.4 0.4 collective-permute-done.18.refs_3_
  67.7 0.1 shard_map.125
  67.8 1.6 %collective-permute-start.19 = (bf16[192,640]{1,0:T(8,128)(2,1)S(1)}, bf16[192,640]{1,0:T(8,128)(2,1)S(1)}, u32[]{:S(2)}, u32[]{:S(2)}) collective-permute-start(bf16[192,640]{1,0:T(8,128)(2,1)S(1)} %shard_map.125), channel_id=1, source_target_pairs={{0,2},{1,3},{2,0},{3,1},{4,6},{5,7},{6,4},{7,5},{8,10},{9,11},{10,... | collective-permute-start | bytes 737288 | tf_op jit(solution)/shard_map/ppermute | solution.py:377
  69.4 10.3 %all_to_all.11 = f32[8,1,64]{2,1,0:T(1,128)S(1)} all-to-all(f32[8,1,64]{2,1,0:T(1,128)S(1)} %bitcast.18), channel_id=1, replica_groups=mesh['exp'=8,'edp'=4] {'exp'}, dimensions={0} | all-to-all | bytes 4096 | tf_op jit(solution)/shard_map/all_to_all | solution.py:515
  79.7 0.0 collective-permute-done.16.refs_7_
  79.7 0.0 copy-done.4
  79.7 0.0 copy-done.5
  79.7 1.5 %shard_map.124 = (bf16[192,2560]{1,0:T(8,128)(2,1)}, f32[6,128]{1,0:T(8,128)}, bf16[512,768]{1,0:T(8,128)(2,1)}, bf16[512,768]{1,0:T(8,128)(2,1)}) custom-call(s32[6,128]{1,0:T(8,128)S(1)} %bitcast.20, s32[6,128]{1,0:T(8,128)S(1)} %bitcast.22, f32[24,128]{1,0:T(8,128)S(1)} %get-tuple-element.58.refs_1_.refs_7_.refs_2_, ...), custom_call_target="tpu_custom_call", output_to_operand_aliasing={{2}: (8, {}), {3}: (9, {})} | custom-call | tf_op jit(solution)/shard_map/pallas_call | solution.py:516
  81.2 0.0 collective-permute-done.19.refs_2_
  81.2 0.8 shard_map.126
  (7 shorter events, 0.0 us)
Async XLA Ops:
  0.6 38.3 %collective-permute-start.2 = (bf16[192,2560]{1,0:T(8,128)(2,1)}, bf16[192,2560]{1,0:T(8,128)(2,1)S(1)}, u32[]{:S(2)}, u32[]{:S(2)}) collective-permute-start(bf16[192,2560]{1,0:T(8,128)(2,1)} %bitcast.14), channel_id=1, source_target_pairs={{0,2},{1,3},{2,0},{3,1},{4,6},{5,7},{6,4},{7,5},{8,10},{9,11},{10,... | collective-permute-start | bytes 2949128 | tf_op jit(solution)/shard_map/ppermute | solution.py:377
  3.7 35.3 %collective-permute-start.5 = (bf16[128,2560]{1,0:T(8,128)(2,1)}, bf16[128,2560]{1,0:T(8,128)(2,1)S(1)}, u32[]{:S(2)}, u32[]{:S(2)}) collective-permute-start(bf16[128,2560]{1,0:T(8,128)(2,1)} %refs_2_.1), channel_id=1, source_target_pairs={{0,16},{4,20},{8,24},{12,28},{16,0},{20,4},{24,8},{28,12},{1,17},{... | collective-permute-start | bytes 1966088 | tf_op jit(solution)/shard_map/ppermute | solution.py:377
  6.3 10.3 %copy-start = (bf16[128,2560]{1,0:T(8,128)(2,1)S(1)}, bf16[128,2560]{1,0:T(8,128)(2,1)}, u32[]{:S(2)}) copy-start(bf16[128,2560]{1,0:T(8,128)(2,1)} %refs_2_.1) | copy-start | bytes 1966084
  8.6 20.2 %collective-permute-start.4 = (bf16[64,2560]{1,0:T(8,128)(2,1)}, bf16[64,2560]{1,0:T(8,128)(2,1)S(1)}, u32[]{:S(2)}, u32[]{:S(2)}) collective-permute-start(bf16[64,2560]{1,0:T(8,128)(2,1)} %get-tuple-element.57), channel_id=1, source_target_pairs={{0,8},{4,12},{8,0},{12,4},{16,24},{20,28},{24,16},{28,20},{1,9},{5... | collective-permute-start | bytes 983048 | tf_op jit(solution)/shard_map/ppermute | solution.py:377
  10.2 28.7 %collective-permute-start = (bf16[64,2560]{1,0:T(8,128)(2,1)}, bf16[64,2560]{1,0:T(8,128)(2,1)S(1)}, u32[]{:S(2)}, u32[]{:S(2)}) collective-permute-start(bf16[64,2560]{1,0:T(8,128)(2,1)} %get-tuple-element.53), channel_id=1, source_target_pairs={{0,12},{4,8},{8,4},{12,0},{16,28},{20,24},{24,20},{28,16},{1,13},{... | collective-permute-start | bytes 983048 | tf_op jit(solution)/shard_map/ppermute | solution.py:377
  11.6 1.2 %copy-start.1 = (bf16[1,192,2560]{2,1,0:T(8,128)(2,1)S(1)}, bf16[1,192,2560]{2,1,0:T(8,128)(2,1)}, u32[]{:S(2)}) copy-start(bf16[1,192,2560]{2,1,0:T(8,128)(2,1)} %param.13) | copy-start | bytes 2949124
  12.8 1.1 %copy-start.2 = (bf16[1,1,512,768]{3,2,1,0:T(8,128)(2,1)S(1)}, bf16[1,1,512,768]{3,2,1,0:T(8,128)(2,1)}, u32[]{:S(2)}) copy-start(bf16[1,1,512,768]{3,2,1,0:T(8,128)(2,1)} %param.14) | copy-start | bytes 2359300
  13.9 1.1 %copy-start.3 = (bf16[1,1,512,768]{3,2,1,0:T(8,128)(2,1)S(1)}, bf16[1,1,512,768]{3,2,1,0:T(8,128)(2,1)}, u32[]{:S(2)}) copy-start(bf16[1,1,512,768]{3,2,1,0:T(8,128)(2,1)} %param.15) | copy-start | bytes 2359300
  15.1 0.7 copy-start.6
  16.9 22.0 %collective-permute-start.3 = (bf16[64,2560]{1,0:T(8,128)(2,1)S(1)}, bf16[64,2560]{1,0:T(8,128)(2,1)S(1)}, u32[]{:S(2)}, u32[]{:S(2)}) collective-permute-start(bf16[64,2560]{1,0:T(8,128)(2,1)S(1)} %get-tuple-element.56), channel_id=1, source_target_pairs={{0,4},{4,0},{8,12},{12,8},{16,20},{20,16},{24,28},{28,24},{1,5},{5... | collective-permute-start | bytes 983048 | tf_op jit(solution)/shard_map/ppermute | solution.py:377
  28.8 10.1 %collective-permute-start.6 = (f32[24,128]{1,0:T(8,128)S(1)}, f32[24,128]{1,0:T(8,128)S(1)}, u32[]{:S(2)}, u32[]{:S(2)}) collective-permute-start(f32[24,128]{1,0:T(8,128)S(1)} %get-tuple-element.58.refs_1_.refs_7_.refs_2_), channel_id=1, source_target_pairs={{0,16},{4,20},{8,24},{12,28},{16,0},{20,4},{24,8},{28,12},{1,17},{... | collective-permute-start | bytes 36872 | tf_op jit(solution)/shard_map/ppermute | solution.py:377
  38.9 4.8 %collective-permute-start.1 = (bf16[192,2560]{1,0:T(8,128)(2,1)S(1)}, bf16[192,2560]{1,0:T(8,128)(2,1)S(1)}, u32[]{:S(2)}, u32[]{:S(2)}) collective-permute-start(bf16[192,2560]{1,0:T(8,128)(2,1)S(1)} %get-tuple-element.54.refs_0_), channel_id=1, source_target_pairs={{0,1},{1,0},{2,3},{3,2},{4,5},{5,4},{6,7},{7,6},{8,9},{9,8},{10,11... | collective-permute-start | bytes 2949128 | tf_op jit(solution)/shard_map/ppermute | solution.py:377
  39.4 4.3 %collective-permute-start.7 = (bf16[192,2560]{1,0:T(8,128)(2,1)S(1)}, bf16[192,2560]{1,0:T(8,128)(2,1)S(1)}, u32[]{:S(2)}, u32[]{:S(2)}) collective-permute-start(bf16[192,2560]{1,0:T(8,128)(2,1)S(1)} %collective-permute-done.2.refs_4_.refs_2_), channel_id=1, source_target_pairs={{0,1},{1,0},{2,3},{3,2},{4,5},{5,4},{6,7},{7,6},{8,9},{9,8},{10,11... | collective-permute-start | bytes 2949128 | tf_op jit(solution)/shard_map/ppermute | solution.py:377
  40.0 10.1 %collective-permute-start.10 = (bf16[64,2048]{1,0:T(8,128)(2,1)S(1)}, bf16[64,2048]{1,0:T(8,128)(2,1)S(1)}, u32[]{:S(2)}, u32[]{:S(2)}) collective-permute-start(bf16[64,2048]{1,0:T(8,128)(2,1)S(1)} %get-tuple-element.66), channel_id=1, source_target_pairs={{0,12},{4,8},{8,4},{12,0},{16,28},{20,24},{24,20},{28,16},{1,13},{... | collective-permute-start | bytes 786440 | tf_op jit(solution)/shard_map/ppermute | solution.py:377
  40.0 14.0 %collective-permute-start.8 = (bf16[64,2048]{1,0:T(8,128)(2,1)S(1)}, bf16[64,2048]{1,0:T(8,128)(2,1)S(1)}, u32[]{:S(2)}, u32[]{:S(2)}) collective-permute-start(bf16[64,2048]{1,0:T(8,128)(2,1)S(1)} %get-tuple-element.64), channel_id=1, source_target_pairs={{0,4},{4,0},{8,12},{12,8},{16,20},{20,16},{24,28},{28,24},{1,5},{5... | collective-permute-start | bytes 786440 | tf_op jit(solution)/shard_map/ppermute | solution.py:377
  40.5 13.5 %collective-permute-start.9 = (bf16[64,2048]{1,0:T(8,128)(2,1)S(1)}, bf16[64,2048]{1,0:T(8,128)(2,1)S(1)}, u32[]{:S(2)}, u32[]{:S(2)}) collective-permute-start(bf16[64,2048]{1,0:T(8,128)(2,1)S(1)} %get-tuple-element.65), channel_id=1, source_target_pairs={{0,8},{4,12},{8,0},{12,4},{16,24},{20,28},{24,16},{28,20},{1,9},{5... | collective-permute-start | bytes 786440 | tf_op jit(solution)/shard_map/ppermute | solution.py:377
  54.6 2.3 %collective-permute-start.11 = (bf16[192,1920]{1,0:T(8,128)(2,1)S(1)}, bf16[192,1920]{1,0:T(8,128)(2,1)S(1)}, u32[]{:S(2)}, u32[]{:S(2)}) collective-permute-start(bf16[192,1920]{1,0:T(8,128)(2,1)S(1)} %get-tuple-element.69), channel_id=1, source_target_pairs={{0,1},{1,0},{2,3},{3,2},{4,5},{5,4},{6,7},{7,6},{8,9},{9,8},{10,11... | collective-permute-start | bytes 2211848 | tf_op jit(solution)/shard_map/ppermute | solution.py:377
  55.7 5.4 %collective-permute-start.12 = (bf16[192,1920]{1,0:T(8,128)(2,1)S(1)}, bf16[192,1920]{1,0:T(8,128)(2,1)S(1)}, u32[]{:S(2)}, u32[]{:S(2)}) collective-permute-start(bf16[192,1920]{1,0:T(8,128)(2,1)S(1)} %get-tuple-element.70), channel_id=1, source_target_pairs={{0,1},{1,0},{2,3},{3,2},{4,5},{5,4},{6,7},{7,6},{8,9},{9,8},{10,11... | collective-permute-start | bytes 2211848 | tf_op jit(solution)/shard_map/ppermute | solution.py:377
  57.1 22.6 %collective-permute-start.16 = (bf16[192,1920]{1,0:T(8,128)(2,1)S(1)}, bf16[192,1920]{1,0:T(8,128)(2,1)S(1)}, u32[]{:S(2)}, u32[]{:S(2)}) collective-permute-start(bf16[192,1920]{1,0:T(8,128)(2,1)S(1)} %shard_map.119.refs_0_), channel_id=1, source_target_pairs={{0,2},{1,3},{2,0},{3,1},{4,6},{5,7},{6,4},{7,5},{8,10},{9,11},{10,... | collective-permute-start | bytes 2211848 | tf_op jit(solution)/shard_map/ppermute | solution.py:377
  57.6 6.1 %collective-permute-start.15 = (bf16[64,640]{1,0:T(8,128)(2,1)S(1)}, bf16[64,640]{1,0:T(8,128)(2,1)S(1)}, u32[]{:S(2)}, u32[]{:S(2)}) collective-permute-start(bf16[64,640]{1,0:T(8,128)(2,1)S(1)} %get-tuple-element.80), channel_id=1, source_target_pairs={{0,12},{4,8},{8,4},{12,0},{16,28},{20,24},{24,20},{28,16},{1,13},{... | collective-permute-start | bytes 245768 | tf_op jit(solution)/shard_map/ppermute | solution.py:377
  58.7 5.7 %collective-permute-start.14 = (bf16[64,640]{1,0:T(8,128)(2,1)S(1)}, bf16[64,640]{1,0:T(8,128)(2,1)S(1)}, u32[]{:S(2)}, u32[]{:S(2)}) collective-permute-start(bf16[64,640]{1,0:T(8,128)(2,1)S(1)} %get-tuple-element.78), channel_id=1, source_target_pairs={{0,8},{4,12},{8,0},{12,4},{16,24},{20,28},{24,16},{28,20},{1,9},{5... | collective-permute-start | bytes 245768 | tf_op jit(solution)/shard_map/ppermute | solution.py:377
  60.5 4.4 %collective-permute-start.13 = (bf16[64,640]{1,0:T(8,128)(2,1)S(1)}, bf16[64,640]{1,0:T(8,128)(2,1)S(1)}, u32[]{:S(2)}, u32[]{:S(2)}) collective-permute-start(bf16[64,640]{1,0:T(8,128)(2,1)S(1)} %get-tuple-element.76), channel_id=1, source_target_pairs={{0,4},{4,0},{8,12},{12,8},{16,20},{20,16},{24,28},{28,24},{1,5},{5... | collective-permute-start | bytes 245768 | tf_op jit(solution)/shard_map/ppermute | solution.py:377
  65.8 1.6 %collective-permute-start.17 = (bf16[192,640]{1,0:T(8,128)(2,1)S(1)}, bf16[192,640]{1,0:T(8,128)(2,1)S(1)}, u32[]{:S(2)}, u32[]{:S(2)}) collective-permute-start(bf16[192,640]{1,0:T(8,128)(2,1)S(1)} %get-tuple-element.89), channel_id=1, source_target_pairs={{0,1},{1,0},{2,3},{3,2},{4,5},{5,4},{6,7},{7,6},{8,9},{9,8},{10,11... | collective-permute-start | bytes 737288 | tf_op jit(solution)/shard_map/ppermute | solution.py:377
  65.9 1.9 %collective-permute-start.18 = (bf16[192,640]{1,0:T(8,128)(2,1)S(1)}, bf16[192,640]{1,0:T(8,128)(2,1)S(1)}, u32[]{:S(2)}, u32[]{:S(2)}) collective-permute-start(bf16[192,640]{1,0:T(8,128)(2,1)S(1)} %get-tuple-element.91), channel_id=1, source_target_pairs={{0,1},{1,0},{2,3},{3,2},{4,5},{5,4},{6,7},{7,6},{8,9},{9,8},{10,11... | collective-permute-start | bytes 737288 | tf_op jit(solution)/shard_map/ppermute | solution.py:377
  66.4 13.3 %copy-start.4 = (s32[128,6]{0,1:T(8,128)S(1)}, s32[128,6]{0,1:T(8,128)}, u32[]{:S(2)}) copy-start(s32[128,6]{0,1:T(8,128)} %param.10) | copy-start | bytes 9220
  66.4 13.3 %copy-start.5 = (s32[128,6]{0,1:T(8,128)S(1)}, s32[128,6]{0,1:T(8,128)}, u32[]{:S(2)}) copy-start(s32[128,6]{0,1:T(8,128)} %param.11) | copy-start | bytes 9220
  67.8 13.4 %collective-permute-start.19 = (bf16[192,640]{1,0:T(8,128)(2,1)S(1)}, bf16[192,640]{1,0:T(8,128)(2,1)S(1)}, u32[]{:S(2)}, u32[]{:S(2)}) collective-permute-start(bf16[192,640]{1,0:T(8,128)(2,1)S(1)} %shard_map.125), channel_id=1, source_target_pairs={{0,2},{1,3},{2,0},{3,1},{4,6},{5,7},{6,4},{7,5},{8,10},{9,11},{10,... | collective-permute-start | bytes 737288 | tf_op jit(solution)/shard_map/ppermute | solution.py:377

commit v7 on v6

--- a/solution.py
+++ b/solution.py
@@ -50,7 +50,7 @@
     slot = slot_ref[...]
     limit = jnp.zeros_like(slot)
     for expert in range(n_exp):
-        limit = jnp.where(choice == expert, counts_ref[0, expert], limit)
+        limit = jnp.where(choice == expert, counts_ref[:, expert : expert + 1], limit)
     kept = slot < capacity
     live = kept & (slot < limit)
     meta_ref[...] = jnp.zeros_like(meta_ref)
@@ -382,7 +382,7 @@
     meta, *found = call(
         functools.partial(routing_body, capacity, n_exp, far),
         [shape(META_ROWS, LANES, dtype=f32)] + [shape(capacity, width)] * (far // 2),
-        [BLOCK, BLOCK, BLOCK, SMEM, BLOCK],
+        [BLOCK] * 5,
         56,
         flops=2 * far * capacity * tok_rows * width,
         moved=out_grad.size * 4,

time: 82.4 us -> 82.4 us (level)
  no operation moved by 1% of the time
where the time goes in v7:
time: 82.4 us; the launch traced here: 82.1 us
  waiting for transfers between devices  30.6 us (37%)
  starting transfers between devices  22.3 us (27%)
  Pallas kernels  13.9 us (17%)
  blocking collectives  10.3 us (12%)
  local copies, waits for them, and re-layouts  4.18 us (5%)
    ppermute x20, waiting for transfers between devices, hop(): return lax.ppermute(x, axis, flip(lax.axis_size(axis), mask))  30.6 us
    ppermute x20, starting transfers between devices, hop(): return lax.ppermute(x, axis, flip(lax.axis_size(axis), mask))  22.3 us
    all_to_all x1, blocking collectives, relayed(): returned = lax.all_to_all(score, 'exp', split_axis=0, concat_axis=0)  10.3 us
    unnamed x14, local copies, waits for them, and re-layouts  4.18 us
    pallas_call x1, Pallas kernels, relayed(): call(functools.partial(routing_body, capacity, n_exp, far), [shape(META_R...  2.38 us
    pallas_call x1, Pallas kernels, relayed(): call(functools.partial(project_far_body, far, cuts[0]), [shape(far * capa...  1.82 us
  transfers between devices with their start and end apart: 20, of which 10 were waited for; matrix products, arithmetic and copies ran while one was open for 0% of the time, Pallas kernels for 15%

profile of v7, /device:TPU:0, one launch (start us, length us, event | category | flops | bytes accessed | tf_op | source)
XLA Modules:
  0.0 82.1 jit_solution(17771288773887367428)
XLA Ops:
  0.6 3.0 %collective-permute-start.2 = (bf16[192,2560]{1,0:T(8,128)(2,1)}, bf16[192,2560]{1,0:T(8,128)(2,1)S(1)}, u32[]{:S(2)}, u32[]{:S(2)}) collective-permute-start(bf16[192,2560]{1,0:T(8,128)(2,1)} %bitcast.14), channel_id=1, source_target_pairs={{0,2},{1,3},{2,0},{3,1},{4,6},{5,7},{6,4},{7,5},{8,10},{9,11},{10,... | collective-permute-start | bytes 2949128 | tf_op jit(solution)/shard_map/ppermute | solution.py:377
  3.7 2.6 %collective-permute-start.5 = (bf16[128,2560]{1,0:T(8,128)(2,1)}, bf16[128,2560]{1,0:T(8,128)(2,1)S(1)}, u32[]{:S(2)}, u32[]{:S(2)}) collective-permute-start(bf16[128,2560]{1,0:T(8,128)(2,1)} %refs_2_.1), channel_id=1, source_target_pairs={{0,16},{4,20},{8,24},{12,28},{16,0},{20,4},{24,8},{28,12},{1,17},{... | collective-permute-start | bytes 1966088 | tf_op jit(solution)/shard_map/ppermute | solution.py:377
  6.3 2.4 %shard_map.111 = (f32[24,128]{1,0:T(8,128)}, bf16[64,2560]{1,0:T(8,128)(2,1)}, bf16[64,2560]{1,0:T(8,128)(2,1)}) custom-call(s32[6,128]{1,0:T(8,128)} %bitcast.19, s32[6,128]{1,0:T(8,128)} %bitcast.21, bf16[6,128]{1,0:T(8,128)(2,1)} %bitcast.27, s32[1,8]{1,0:T(1,128)} %refs_3_.1, bf16[128,2560]{1,0:T(8,128)(2,1)} %refs_2_.1), custom_call_target="tpu_custom_call" | custom-call | flops 167772160 | bytes 1310720 | tf_op jit(solution)/shard_map/pallas_call | solution.py:382
  8.6 1.6 %collective-permute-start.4 = (bf16[64,2560]{1,0:T(8,128)(2,1)}, bf16[64,2560]{1,0:T(8,128)(2,1)S(1)}, u32[]{:S(2)}, u32[]{:S(2)}) collective-permute-start(bf16[64,2560]{1,0:T(8,128)(2,1)} %get-tuple-element.57), channel_id=1, source_target_pairs={{0,8},{4,12},{8,0},{12,4},{16,24},{20,28},{24,16},{28,20},{1,9},{5... | collective-permute-start | bytes 983048 | tf_op jit(solution)/shard_map/ppermute | solution.py:377
  10.2 1.4 %collective-permute-start = (bf16[64,2560]{1,0:T(8,128)(2,1)}, bf16[64,2560]{1,0:T(8,128)(2,1)S(1)}, u32[]{:S(2)}, u32[]{:S(2)}) collective-permute-start(bf16[64,2560]{1,0:T(8,128)(2,1)} %get-tuple-element.53), channel_id=1, source_target_pairs={{0,12},{4,8},{8,4},{12,0},{16,28},{20,24},{24,20},{28,16},{1,13},{... | collective-permute-start | bytes 983048 | tf_op jit(solution)/shard_map/ppermute | solution.py:377
  11.6 1.2 %copy-done.1 = bf16[1,192,2560]{2,1,0:T(8,128)(2,1)S(1)} copy-done((bf16[1,192,2560]{2,1,0:T(8,128)(2,1)S(1)}, bf16[1,192,2560]{2,1,0:T(8,128)(2,1)}, u32[]{:S(2)}) %copy-start.1) | copy-done | bytes 983064
  12.8 1.1 %copy-done.2 = bf16[1,1,512,768]{3,2,1,0:T(8,128)(2,1)S(1)} copy-done((bf16[1,1,512,768]{3,2,1,0:T(8,128)(2,1)S(1)}, bf16[1,1,512,768]{3,2,1,0:T(8,128)(2,1)}, u32[]{:S(2)}) %copy-start.2) | copy-done | bytes 786456
  13.9 1.1 %copy-done.3 = bf16[1,1,512,768]{3,2,1,0:T(8,128)(2,1)S(1)} copy-done((bf16[1,1,512,768]{3,2,1,0:T(8,128)(2,1)S(1)}, bf16[1,1,512,768]{3,2,1,0:T(8,128)(2,1)}, u32[]{:S(2)}) %copy-start.3) | copy-done | bytes 786456
  15.1 0.7 copy-done.6
  15.8 0.8 shard_map.112
  16.6 0.0 copy-done
  16.6 0.3 shard_map.113
  16.9 0.6 collective-permute-start.3
  17.5 11.3 %collective-permute-done.4.refs_1_.refs_6_.refs_5_.refs_4_ = bf16[64,2560]{1,0:T(8,128)(2,1)S(1)} collective-permute-done((bf16[64,2560]{1,0:T(8,128)(2,1)}, bf16[64,2560]{1,0:T(8,128)(2,1)S(1)}, u32[]{:S(2)}, u32[]{:S(2)}) %collective-permute-start.4) | collective-permute-done | bytes 327712 | tf_op jit(solution)/shard_map/ppermute | solution.py:377
  28.8 2.2 %collective-permute-start.6 = (f32[24,128]{1,0:T(8,128)S(1)}, f32[24,128]{1,0:T(8,128)S(1)}, u32[]{:S(2)}, u32[]{:S(2)}) collective-permute-start(f32[24,128]{1,0:T(8,128)S(1)} %get-tuple-element.58.refs_1_.refs_7_.refs_2_), channel_id=1, source_target_pairs={{0,16},{4,20},{8,24},{12,28},{16,0},{20,4},{24,8},{28,12},{1,17},{... | collective-permute-start | bytes 36872 | tf_op jit(solution)/shard_map/ppermute | solution.py:377
  31.0 7.9 %collective-permute-done.refs_2_.refs_7_.refs_6_.refs_5_ = bf16[64,2560]{1,0:T(8,128)(2,1)S(1)} collective-permute-done((bf16[64,2560]{1,0:T(8,128)(2,1)}, bf16[64,2560]{1,0:T(8,128)(2,1)S(1)}, u32[]{:S(2)}, u32[]{:S(2)}) %collective-permute-start) | collective-permute-done | bytes 327712 | tf_op jit(solution)/shard_map/ppermute | solution.py:377
  38.9 0.0 collective-permute-start.1
  38.9 0.0 collective-permute-done.3.refs_0_.refs_5_.refs_4_.refs_3_
  38.9 0.0 collective-permute-done.6.refs_6_.refs_2_
  38.9 0.0 collective-permute-done.5.refs_5_.refs_1_
  38.9 0.0 collective-permute-done.2.refs_4_.refs_2_
  39.0 0.4 shard_map.114
  39.4 0.6 collective-permute-start.7
  40.0 0.0 collective-permute-start.10
  40.0 0.5 collective-permute-start.8
  40.5 3.0 %collective-permute-start.9 = (bf16[64,2048]{1,0:T(8,128)(2,1)S(1)}, bf16[64,2048]{1,0:T(8,128)(2,1)S(1)}, u32[]{:S(2)}, u32[]{:S(2)}) collective-permute-start(bf16[64,2048]{1,0:T(8,128)(2,1)S(1)} %get-tuple-element.65), channel_id=1, source_target_pairs={{0,8},{4,12},{8,0},{12,4},{16,24},{20,28},{24,16},{28,20},{1,9},{5... | collective-permute-start | bytes 786440 | tf_op jit(solution)/shard_map/ppermute | solution.py:377
  43.4 0.3 shard_map.116
  43.7 0.0 collective-permute-done.1.refs_1_
  43.7 0.0 collective-permute-done.7.refs_3_
  43.7 1.5 %shard_map.115 = (bf16[768,2560]{1,0:T(8,128)(2,1)S(1)}, f32[256,768]{1,0:T(8,128)S(1)}) custom-call(bf16[192,2560]{1,0:T(8,128)(2,1)S(1)} %get-tuple-element.54.refs_0_, bf16[192,2560]{1,0:T(8,128)(2,1)S(1)} %collective-permute-done.1.refs_1_, bf16[192,2560]{1,0:T(8,128)(2,1)S(1)} %collective-permute-done.2.refs_4_.refs_2_, ...), custom_call_target="tpu_custom_call" | custom-call | tf_op jit(solution)/shard_map/pallas_call | solution.py:454
  45.2 4.9 %collective-permute-done.10.refs_10_.refs_6_.refs_13_.refs_8_ = bf16[64,2048]{1,0:T(8,128)(2,1)S(1)} collective-permute-done((bf16[64,2048]{1,0:T(8,128)(2,1)S(1)}, bf16[64,2048]{1,0:T(8,128)(2,1)S(1)}, u32[]{:S(2)}, u32[]{:S(2)}) %collective-permute-start.10) | collective-permute-done | bytes 262176 | tf_op jit(solution)/shard_map/ppermute | solution.py:377
  50.1 3.9 %collective-permute-done.8.refs_8_.refs_4_.refs_11_.refs_6_ = bf16[64,2048]{1,0:T(8,128)(2,1)S(1)} collective-permute-done((bf16[64,2048]{1,0:T(8,128)(2,1)S(1)}, bf16[64,2048]{1,0:T(8,128)(2,1)S(1)}, u32[]{:S(2)}, u32[]{:S(2)}) %collective-permute-start.8) | collective-permute-done | bytes 262176 | tf_op jit(solution)/shard_map/ppermute | solution.py:377
  53.9 0.0 collective-permute-done.9.refs_9_.refs_5_.refs_12_.refs_7_
  53.9 0.7 shard_map.117
  54.7 0.1 collective-permute-start.11
  54.7 1.0 %shard_map.118 = (bf16[192,1920]{1,0:T(8,128)(2,1)S(1)}, f32[192,1920]{1,0:T(8,128)S(1)}) custom-call(bf16[4,192,512]{2,1,0:T(8,128)(2,1)S(1)} %get-tuple-element.51.refs_2_.refs_0_.refs_1_, bf16[512,1920]{1,0:T(8,128)(2,1)S(1)} %get-tuple-element.67.refs_1_.refs_2_), custom_call_target="tpu_custom_call" | custom-call | tf_op jit(solution)/shard_map/pallas_call | solution.py:478
  55.7 0.6 collective-permute-start.12
  56.3 0.7 collective-permute-done.11.refs_1_
  56.9 0.1 shard_map.119.refs_0_
  57.1 0.6 collective-permute-start.16
  57.6 1.1 %collective-permute-start.15 = (bf16[64,640]{1,0:T(8,128)(2,1)S(1)}, bf16[64,640]{1,0:T(8,128)(2,1)S(1)}, u32[]{:S(2)}, u32[]{:S(2)}) collective-permute-start(bf16[64,640]{1,0:T(8,128)(2,1)S(1)} %get-tuple-element.80), channel_id=1, source_target_pairs={{0,12},{4,8},{8,4},{12,0},{16,28},{20,24},{24,20},{28,16},{1,13},{... | collective-permute-start | bytes 245768 | tf_op jit(solution)/shard_map/ppermute | solution.py:377
  58.7 1.8 %collective-permute-start.14 = (bf16[64,640]{1,0:T(8,128)(2,1)S(1)}, bf16[64,640]{1,0:T(8,128)(2,1)S(1)}, u32[]{:S(2)}, u32[]{:S(2)}) collective-permute-start(bf16[64,640]{1,0:T(8,128)(2,1)S(1)} %get-tuple-element.78), channel_id=1, source_target_pairs={{0,8},{4,12},{8,0},{12,4},{16,24},{20,28},{24,16},{28,20},{1,9},{5... | collective-permute-start | bytes 245768 | tf_op jit(solution)/shard_map/ppermute | solution.py:377
  60.5 0.6 collective-permute-start.13
  61.1 0.0 collective-permute-done.12.refs_2_.refs_6_
  61.1 1.8 %shard_map.120 = (f32[256,768]{1,0:T(8,128)S(1)}, bf16[512,768]{1,0:T(8,128)(2,1)}, bf16[512,768]{1,0:T(8,128)(2,1)}, f32[2,128]{1,0:T(2,128)S(1)}) custom-call(bf16[192,1920]{1,0:T(8,128)(2,1)S(1)} %shard_map.119.refs_0_, bf16[64,640]{1,0:T(8,128)(2,1)S(1)} %get-tuple-element.63.refs_1_.refs_6_, ...), custom_call_target="tpu_custom_call" | custom-call | tf_op jit(solution)/shard_map/pallas_call | solution.py:490
  63.0 0.6 shard_map.121.refs_0_.refs_5_
  63.6 0.2 collective-permute-done.15.refs_9_.refs_4_
  63.7 0.7 collective-permute-done.14.refs_8_.refs_3_
  64.5 0.5 collective-permute-done.13.refs_7_.refs_2_
  65.0 0.9 %shard_map.122 = (f32[192,640]{1,0:T(8,128)S(1)}, f32[192,640]{1,0:T(8,128)S(1)}, bf16[192,640]{1,0:T(8,128)(2,1)S(1)}, bf16[192,640]{1,0:T(8,128)(2,1)S(1)}) custom-call(f32[192,1920]{1,0:T(8,128)S(1)} %shard_map.121.refs_0_.refs_5_, bf16[4,192,512]{2,1,0:T(8,128)(2,1)S(1)} %get-tuple-element.51.refs_2_.refs_0_.refs_1_, ...), custom_call_target="tpu_custom_call" | custom-call | flops 503316480 | bytes 3276800 | tf_op jit(solution)/shard_map/pallas_call | solution.py:421
  65.8 0.1 collective-permute-start.17
  65.9 0.5 collective-permute-start.18
  66.4 0.7 shard_map.123
  67.1 0.3 collective-permute-done.17.refs_1_
  67.4 0.4 collective-permute-done.18.refs_3_
  67.8 0.1 shard_map.125
  67.8 1.6 %collective-permute-start.19 = (bf16[192,640]{1,0:T(8,128)(2,1)S(1)}, bf16[192,640]{1,0:T(8,128)(2,1)S(1)}, u32[]{:S(2)}, u32[]{:S(2)}) collective-permute-start(bf16[192,640]{1,0:T(8,128)(2,1)S(1)} %shard_map.125), channel_id=1, source_target_pairs={{0,2},{1,3},{2,0},{3,1},{4,6},{5,7},{6,4},{7,5},{8,10},{9,11},{10,... | collective-permute-start | bytes 737288 | tf_op jit(solution)/shard_map/ppermute | solution.py:377
  69.4 10.3 %all_to_all.11 = f32[8,1,64]{2,1,0:T(1,128)S(1)} all-to-all(f32[8,1,64]{2,1,0:T(1,128)S(1)} %bitcast.18), channel_id=1, replica_groups=mesh['exp'=8,'edp'=4] {'exp'}, dimensions={0} | all-to-all | bytes 4096 | tf_op jit(solution)/shard_map/all_to_all | solution.py:515
  79.7 0.0 collective-permute-done.16.refs_7_
  79.7 0.0 copy-done.4
  79.7 0.0 copy-done.5
  79.7 1.5 %shard_map.124 = (bf16[192,2560]{1,0:T(8,128)(2,1)}, f32[6,128]{1,0:T(8,128)}, bf16[512,768]{1,0:T(8,128)(2,1)}, bf16[512,768]{1,0:T(8,128)(2,1)}) custom-call(s32[6,128]{1,0:T(8,128)S(1)} %bitcast.20, s32[6,128]{1,0:T(8,128)S(1)} %bitcast.22, f32[24,128]{1,0:T(8,128)S(1)} %get-tuple-element.58.refs_1_.refs_7_.refs_2_, ...), custom_call_target="tpu_custom_call", output_to_operand_aliasing={{2}: (8, {}), {3}: (9, {})} | custom-call | tf_op jit(solution)/shard_map/pallas_call | solution.py:516
  81.2 0.0 collective-permute-done.19.refs_2_
  81.3 0.8 shard_map.126
  (7 shorter events, 0.0 us)
Async XLA Ops:
  0.6 38.3 %collective-permute-start.2 = (bf16[192,2560]{1,0:T(8,128)(2,1)}, bf16[192,2560]{1,0:T(8,128)(2,1)S(1)}, u32[]{:S(2)}, u32[]{:S(2)}) collective-permute-start(bf16[192,2560]{1,0:T(8,128)(2,1)} %bitcast.14), channel_id=1, source_target_pairs={{0,2},{1,3},{2,0},{3,1},{4,6},{5,7},{6,4},{7,5},{8,10},{9,11},{10,... | collective-permute-start | bytes 2949128 | tf_op jit(solution)/shard_map/ppermute | solution.py:377
  3.7 35.3 %collective-permute-start.5 = (bf16[128,2560]{1,0:T(8,128)(2,1)}, bf16[128,2560]{1,0:T(8,128)(2,1)S(1)}, u32[]{:S(2)}, u32[]{:S(2)}) collective-permute-start(bf16[128,2560]{1,0:T(8,128)(2,1)} %refs_2_.1), channel_id=1, source_target_pairs={{0,16},{4,20},{8,24},{12,28},{16,0},{20,4},{24,8},{28,12},{1,17},{... | collective-permute-start | bytes 1966088 | tf_op jit(solution)/shard_map/ppermute | solution.py:377
  6.3 10.3 %copy-start = (bf16[128,2560]{1,0:T(8,128)(2,1)S(1)}, bf16[128,2560]{1,0:T(8,128)(2,1)}, u32[]{:S(2)}) copy-start(bf16[128,2560]{1,0:T(8,128)(2,1)} %refs_2_.1) | copy-start | bytes 1966084
  8.6 20.2 %collective-permute-start.4 = (bf16[64,2560]{1,0:T(8,128)(2,1)}, bf16[64,2560]{1,0:T(8,128)(2,1)S(1)}, u32[]{:S(2)}, u32[]{:S(2)}) collective-permute-start(bf16[64,2560]{1,0:T(8,128)(2,1)} %get-tuple-element.57), channel_id=1, source_target_pairs={{0,8},{4,12},{8,0},{12,4},{16,24},{20,28},{24,16},{28,20},{1,9},{5... | collective-permute-start | bytes 983048 | tf_op jit(solution)/shard_map/ppermute | solution.py:377
  10.2 28.7 %collective-permute-start = (bf16[64,2560]{1,0:T(8,128)(2,1)}, bf16[64,2560]{1,0:T(8,128)(2,1)S(1)}, u32[]{:S(2)}, u32[]{:S(2)}) collective-permute-start(bf16[64,2560]{1,0:T(8,128)(2,1)} %get-tuple-element.53), channel_id=1, source_target_pairs={{0,12},{4,8},{8,4},{12,0},{16,28},{20,24},{24,20},{28,16},{1,13},{... | collective-permute-start | bytes 983048 | tf_op jit(solution)/shard_map/ppermute | solution.py:377
  11.6 1.2 %copy-start.1 = (bf16[1,192,2560]{2,1,0:T(8,128)(2,1)S(1)}, bf16[1,192,2560]{2,1,0:T(8,128)(2,1)}, u32[]{:S(2)}) copy-start(bf16[1,192,2560]{2,1,0:T(8,128)(2,1)} %param.13) | copy-start | bytes 2949124
  12.8 1.1 %copy-start.2 = (bf16[1,1,512,768]{3,2,1,0:T(8,128)(2,1)S(1)}, bf16[1,1,512,768]{3,2,1,0:T(8,128)(2,1)}, u32[]{:S(2)}) copy-start(bf16[1,1,512,768]{3,2,1,0:T(8,128)(2,1)} %param.14) | copy-start | bytes 2359300
  13.9 1.1 %copy-start.3 = (bf16[1,1,512,768]{3,2,1,0:T(8,128)(2,1)S(1)}, bf16[1,1,512,768]{3,2,1,0:T(8,128)(2,1)}, u32[]{:S(2)}) copy-start(bf16[1,1,512,768]{3,2,1,0:T(8,128)(2,1)} %param.15) | copy-start | bytes 2359300
  15.1 0.7 copy-start.6
  16.9 22.0 %collective-permute-start.3 = (bf16[64,2560]{1,0:T(8,128)(2,1)S(1)}, bf16[64,2560]{1,0:T(8,128)(2,1)S(1)}, u32[]{:S(2)}, u32[]{:S(2)}) collective-permute-start(bf16[64,2560]{1,0:T(8,128)(2,1)S(1)} %get-tuple-element.56), channel_id=1, source_target_pairs={{0,4},{4,0},{8,12},{12,8},{16,20},{20,16},{24,28},{28,24},{1,5},{5... | collective-permute-start | bytes 983048 | tf_op jit(solution)/shard_map/ppermute | solution.py:377
  28.8 10.1 %collective-permute-start.6 = (f32[24,128]{1,0:T(8,128)S(1)}, f32[24,128]{1,0:T(8,128)S(1)}, u32[]{:S(2)}, u32[]{:S(2)}) collective-permute-start(f32[24,128]{1,0:T(8,128)S(1)} %get-tuple-element.58.refs_1_.refs_7_.refs_2_), channel_id=1, source_target_pairs={{0,16},{4,20},{8,24},{12,28},{16,0},{20,4},{24,8},{28,12},{1,17},{... | collective-permute-start | bytes 36872 | tf_op jit(solution)/shard_map/ppermute | solution.py:377
  38.9 4.8 %collective-permute-start.1 = (bf16[192,2560]{1,0:T(8,128)(2,1)S(1)}, bf16[192,2560]{1,0:T(8,128)(2,1)S(1)}, u32[]{:S(2)}, u32[]{:S(2)}) collective-permute-start(bf16[192,2560]{1,0:T(8,128)(2,1)S(1)} %get-tuple-element.54.refs_0_), channel_id=1, source_target_pairs={{0,1},{1,0},{2,3},{3,2},{4,5},{5,4},{6,7},{7,6},{8,9},{9,8},{10,11... | collective-permute-start | bytes 2949128 | tf_op jit(solution)/shard_map/ppermute | solution.py:377
  39.4 4.3 %collective-permute-start.7 = (bf16[192,2560]{1,0:T(8,128)(2,1)S(1)}, bf16[192,2560]{1,0:T(8,128)(2,1)S(1)}, u32[]{:S(2)}, u32[]{:S(2)}) collective-permute-start(bf16[192,2560]{1,0:T(8,128)(2,1)S(1)} %collective-permute-done.2.refs_4_.refs_2_), channel_id=1, source_target_pairs={{0,1},{1,0},{2,3},{3,2},{4,5},{5,4},{6,7},{7,6},{8,9},{9,8},{10,11... | collective-permute-start | bytes 2949128 | tf_op jit(solution)/shard_map/ppermute | solution.py:377
  40.0 10.1 %collective-permute-start.10 = (bf16[64,2048]{1,0:T(8,128)(2,1)S(1)}, bf16[64,2048]{1,0:T(8,128)(2,1)S(1)}, u32[]{:S(2)}, u32[]{:S(2)}) collective-permute-start(bf16[64,2048]{1,0:T(8,128)(2,1)S(1)} %get-tuple-element.66), channel_id=1, source_target_pairs={{0,12},{4,8},{8,4},{12,0},{16,28},{20,24},{24,20},{28,16},{1,13},{... | collective-permute-start | bytes 786440 | tf_op jit(solution)/shard_map/ppermute | solution.py:377
  40.0 14.0 %collective-permute-start.8 = (bf16[64,2048]{1,0:T(8,128)(2,1)S(1)}, bf16[64,2048]{1,0:T(8,128)(2,1)S(1)}, u32[]{:S(2)}, u32[]{:S(2)}) collective-permute-start(bf16[64,2048]{1,0:T(8,128)(2,1)S(1)} %get-tuple-element.64), channel_id=1, source_target_pairs={{0,4},{4,0},{8,12},{12,8},{16,20},{20,16},{24,28},{28,24},{1,5},{5... | collective-permute-start | bytes 786440 | tf_op jit(solution)/shard_map/ppermute | solution.py:377
  40.5 13.5 %collective-permute-start.9 = (bf16[64,2048]{1,0:T(8,128)(2,1)S(1)}, bf16[64,2048]{1,0:T(8,128)(2,1)S(1)}, u32[]{:S(2)}, u32[]{:S(2)}) collective-permute-start(bf16[64,2048]{1,0:T(8,128)(2,1)S(1)} %get-tuple-element.65), channel_id=1, source_target_pairs={{0,8},{4,12},{8,0},{12,4},{16,24},{20,28},{24,16},{28,20},{1,9},{5... | collective-permute-start | bytes 786440 | tf_op jit(solution)/shard_map/ppermute | solution.py:377
  54.7 2.3 %collective-permute-start.11 = (bf16[192,1920]{1,0:T(8,128)(2,1)S(1)}, bf16[192,1920]{1,0:T(8,128)(2,1)S(1)}, u32[]{:S(2)}, u32[]{:S(2)}) collective-permute-start(bf16[192,1920]{1,0:T(8,128)(2,1)S(1)} %get-tuple-element.69), channel_id=1, source_target_pairs={{0,1},{1,0},{2,3},{3,2},{4,5},{5,4},{6,7},{7,6},{8,9},{9,8},{10,11... | collective-permute-start | bytes 2211848 | tf_op jit(solution)/shard_map/ppermute | solution.py:377
  55.7 5.4 %collective-permute-start.12 = (bf16[192,1920]{1,0:T(8,128)(2,1)S(1)}, bf16[192,1920]{1,0:T(8,128)(2,1)S(1)}, u32[]{:S(2)}, u32[]{:S(2)}) collective-permute-start(bf16[192,1920]{1,0:T(8,128)(2,1)S(1)} %get-tuple-element.70), channel_id=1, source_target_pairs={{0,1},{1,0},{2,3},{3,2},{4,5},{5,4},{6,7},{7,6},{8,9},{9,8},{10,11... | collective-permute-start | bytes 2211848 | tf_op jit(solution)/shard_map/ppermute | solution.py:377
  57.1 22.6 %collective-permute-start.16 = (bf16[192,1920]{1,0:T(8,128)(2,1)S(1)}, bf16[192,1920]{1,0:T(8,128)(2,1)S(1)}, u32[]{:S(2)}, u32[]{:S(2)}) collective-permute-start(bf16[192,1920]{1,0:T(8,128)(2,1)S(1)} %shard_map.119.refs_0_), channel_id=1, source_target_pairs={{0,2},{1,3},{2,0},{3,1},{4,6},{5,7},{6,4},{7,5},{8,10},{9,11},{10,... | collective-permute-start | bytes 2211848 | tf_op jit(solution)/shard_map/ppermute | solution.py:377
  57.6 6.1 %collective-permute-start.15 = (bf16[64,640]{1,0:T(8,128)(2,1)S(1)}, bf16[64,640]{1,0:T(8,128)(2,1)S(1)}, u32[]{:S(2)}, u32[]{:S(2)}) collective-permute-start(bf16[64,640]{1,0:T(8,128)(2,1)S(1)} %get-tuple-element.80), channel_id=1, source_target_pairs={{0,12},{4,8},{8,4},{12,0},{16,28},{20,24},{24,20},{28,16},{1,13},{... | collective-permute-start | bytes 245768 | tf_op jit(solution)/shard_map/ppermute | solution.py:377
  58.7 5.7 %collective-permute-start.14 = (bf16[64,640]{1,0:T(8,128)(2,1)S(1)}, bf16[64,640]{1,0:T(8,128)(2,1)S(1)}, u32[]{:S(2)}, u32[]{:S(2)}) collective-permute-start(bf16[64,640]{1,0:T(8,128)(2,1)S(1)} %get-tuple-element.78), channel_id=1, source_target_pairs={{0,8},{4,12},{8,0},{12,4},{16,24},{20,28},{24,16},{28,20},{1,9},{5... | collective-permute-start | bytes 245768 | tf_op jit(solution)/shard_map/ppermute | solution.py:377
  60.5 4.4 %collective-permute-start.13 = (bf16[64,640]{1,0:T(8,128)(2,1)S(1)}, bf16[64,640]{1,0:T(8,128)(2,1)S(1)}, u32[]{:S(2)}, u32[]{:S(2)}) collective-permute-start(bf16[64,640]{1,0:T(8,128)(2,1)S(1)} %get-tuple-element.76), channel_id=1, source_target_pairs={{0,4},{4,0},{8,12},{12,8},{16,20},{20,16},{24,28},{28,24},{1,5},{5... | collective-permute-start | bytes 245768 | tf_op jit(solution)/shard_map/ppermute | solution.py:377
  65.8 1.6 %collective-permute-start.17 = (bf16[192,640]{1,0:T(8,128)(2,1)S(1)}, bf16[192,640]{1,0:T(8,128)(2,1)S(1)}, u32[]{:S(2)}, u32[]{:S(2)}) collective-permute-start(bf16[192,640]{1,0:T(8,128)(2,1)S(1)} %get-tuple-element.89), channel_id=1, source_target_pairs={{0,1},{1,0},{2,3},{3,2},{4,5},{5,4},{6,7},{7,6},{8,9},{9,8},{10,11... | collective-permute-start | bytes 737288 | tf_op jit(solution)/shard_map/ppermute | solution.py:377
  65.9 1.9 %collective-permute-start.18 = (bf16[192,640]{1,0:T(8,128)(2,1)S(1)}, bf16[192,640]{1,0:T(8,128)(2,1)S(1)}, u32[]{:S(2)}, u32[]{:S(2)}) collective-permute-start(bf16[192,640]{1,0:T(8,128)(2,1)S(1)} %get-tuple-element.91), channel_id=1, source_target_pairs={{0,1},{1,0},{2,3},{3,2},{4,5},{5,4},{6,7},{7,6},{8,9},{9,8},{10,11... | collective-permute-start | bytes 737288 | tf_op jit(solution)/shard_map/ppermute | solution.py:377
  66.4 13.3 %copy-start.4 = (s32[128,6]{0,1:T(8,128)S(1)}, s32[128,6]{0,1:T(8,128)}, u32[]{:S(2)}) copy-start(s32[128,6]{0,1:T(8,128)} %param.10) | copy-start | bytes 9220
  66.4 13.3 %copy-start.5 = (s32[128,6]{0,1:T(8,128)S(1)}, s32[128,6]{0,1:T(8,128)}, u32[]{:S(2)}) copy-start(s32[128,6]{0,1:T(8,128)} %param.11) | copy-start | bytes 9220
  67.8 13.4 %collective-permute-start.19 = (bf16[192,640]{1,0:T(8,128)(2,1)S(1)}, bf16[192,640]{1,0:T(8,128)(2,1)S(1)}, u32[]{:S(2)}, u32[]{:S(2)}) collective-permute-start(bf16[192,640]{1,0:T(8,128)(2,1)S(1)} %shard_map.125), channel_id=1, source_target_pairs={{0,2},{1,3},{2,0},{3,1},{4,6},{5,7},{6,4},{7,5},{8,10},{9,11},{10,... | collective-permute-start | bytes 737288 | tf_op jit(solution)/shard_map/ppermute | solution.py:377
